TPU v7x, 256 devices: a whole 4x4x8 slice. The times are simulated.
256 devices in a mesh: row: 16 (over y, z_hi, core), col: 16 (over x, z_lo).
Axes of the slice: x: 4, y: 4, z: 8 (z_hi: 2, z_lo: 4; z = z_hi * 4 + z_lo), core: 2. Of those that a mesh axis runs over, the one named last changes fastest.
Arguments:
- p_blocks: bfloat16 [16, 16, 32, 128, 128], P('row', 'col')
- coords: int32 [16, 16, 2, 32], P('row', 'col'), may hold values from 0 to 2047, as said below
- tasks: int32 [16, 16, 4, 3, 256], P('row', 'col'), may hold values from -1 to 31, as said below
- window_panels: int32 [4], replicated, may hold values from 0 to 31, as said below
- branch: int32 [16, 16, 32], P('row', 'col'), may hold values from 0 to 1
Outputs:
- p_next: bfloat16 [16, 16, 32, 128, 128], P('row', 'col')
- traces: float32 [2], replicated
Inputs may be any that keep to these rules, and one draw needn't show every extreme that they name: `coords`: global block row and column lie in the block's row and column panel; in each pair of equal row and column panels exactly 4 of the 8 slots are diagonal blocks, no other block is. `tasks`: index 0 is below 32 or -1, index 1 below 16, index 2 below 16; in each device's step the live products come first, 128 or more of them, and all 256 are live in some device's step. `window_panels`: distinct panel numbers; the last panel is among them.
All inputs are finite; a program needn't handle non-finite values.
Results may differ from a plain program's by a relative error of at most 0.001.
Values may be sent and summed in bfloat16 or wider, within the bound.
No kernel may reach another device: no remote copies, remote signals or barrier semaphores. Data moves between devices by JAX's collectives and lax.ppermute only.
A program may use at most 64 MiB of HBM per device.

v0:
```python
import jax
import jax.numpy as jnp
from jax import lax
from jax.sharding import PartitionSpec as P

BS = 128
NBLK = 2048
PB = 64
Q = 8


def block_trace(blocks):
    return jnp.sum(jnp.diagonal(blocks, axis1=1, axis2=2).astype(jnp.float32), axis=-1)


def accumulate(product, col_panel, row_panel, step_tasks):
    count = step_tasks.shape[1]
    width = 64
    slots = product.shape[0]

    def one_block(index, running):
        piece = lax.dynamic_slice_in_dim(step_tasks, index * width, width, 1)
        left_blocks = jnp.take(col_panel, piece[1], axis=0)
        right_blocks = jnp.take(row_panel, piece[2], axis=0)
        prods = jnp.einsum(
            "tij,tjk->tik", left_blocks, right_blocks, preferred_element_type=jnp.float32
        )
        flat_prods = prods.reshape(width, prods.shape[1] * prods.shape[2])
        target = jnp.where(piece[0] < 0, slots, piece[0])
        return running.at[target].add(flat_prods, mode="drop")

    return lax.fori_loop(0, count // width, one_block, product)


def body(p_blocks, coords, tasks, window_panels, branch):
    rows_count = lax.axis_size("row")
    cols_count = lax.axis_size("col")
    panels_down = NBLK // (PB * rows_count)
    panels_across = NBLK // (PB * cols_count)
    own_blocks = p_blocks[0, 0]
    slots = own_blocks.shape[0]
    size_block = own_blocks.shape[1]
    stored = slots // (panels_down * panels_across)
    tiles = own_blocks.reshape(panels_down, panels_across, stored, size_block, size_block)
    grid_row = lax.axis_index("row")
    grid_col = lax.axis_index("col")
    diag_mask = (coords[0, 0, 0] == coords[0, 0, 1]).astype(jnp.float32)
    old_local = jnp.sum(diag_mask * block_trace(own_blocks))
    old_total = lax.psum(old_local, ("row", "col"))
    product = jnp.zeros((slots, size_block * size_block), jnp.float32)
    for step in range(tasks.shape[2]):
        panel = window_panels[step]
        owner_col = panel // panels_across
        owner_row = panel // panels_down
        col_local = lax.dynamic_index_in_dim(tiles, panel % panels_across, 1, keepdims=False)
        col_local = col_local.reshape(panels_down * stored, size_block, size_block)
        row_local = lax.dynamic_index_in_dim(tiles, panel % panels_down, 0, keepdims=False)
        row_local = row_local.reshape(panels_across * stored, size_block, size_block)
        col_term = jnp.where(grid_col == owner_col, col_local.astype(jnp.float32), 0.0)
        col_panel = lax.psum(col_term.astype(jnp.bfloat16), "col")
        row_term = jnp.where(grid_row == owner_row, row_local.astype(jnp.float32), 0.0)
        row_panel = lax.psum(row_term.astype(jnp.bfloat16), "row")
        product = accumulate(product, col_panel, row_panel, tasks[0, 0, step])
    own_flat = own_blocks.reshape(slots, size_block * size_block).astype(jnp.float32)
    own_branch = branch[0, 0].reshape(slots, 1)
    purified = jnp.where(own_branch == 0, product, 2.0 * own_flat - product)
    purified_blocks = purified.reshape(slots, size_block, size_block)
    new_local = jnp.sum(diag_mask * block_trace(purified_blocks))
    new_total = lax.psum(new_local, ("row", "col"))
    scale_factor = 1.0 / (NBLK // PB * (Q // 2) * BS) ** 0.5
    traces = jnp.stack([old_total, new_total]) * scale_factor
    p_next = purified_blocks.astype(jnp.bfloat16).reshape(1, 1, slots, size_block, size_block)
    return (p_next, traces.astype(jnp.float32))


def solution(mesh):
    in_specs = (
        P("row", "col", None, None, None),
        P("row", "col", None, None),
        P("row", "col", None, None, None),
        P(),
        P("row", "col", None),
    )
    out_specs = (P("row", "col", None, None, None), P())
    return jax.shard_map(body, mesh=mesh, in_specs=in_specs, out_specs=out_specs, check_vma=False)
```

profile of v0, /device:TPU:2, one launch (start us, length us, event | category | flops | bytes accessed | tf_op | source)
XLA Modules:
  0.0 831.5 jit_solution(16914036030027021273)
XLA Ops:
  19.0 3.5 select_convert_fusion
  25.4 3.3 copy.11
  32.4 192.8 %all-reduce.8.cloned.1.call-done = (bf16[16,128,128]{2,1,0:T(8,128)(2,1)}, bf16[16,128,128]{2,1,0:T(8,128)(2,1)}, bf16[16,128,128]{2,1,0:T(8,128)(2,1)}, bf16[16,128,128]{2,1,0:T(8,128)(2,1)}) async-done(((bf16[16,128,128]{2,1,0:T(8,128)(2,1)}, bf16[16,128,128]{2,1,0:T(8,128)(2,1)}, bf16[16,128,128]{2,1,0:T(8,128)(2,1)}, bf16[16,128,128]{2,1,0:T(8,128)(2,1)}), (bf16[16,128,128]{2,1,0:T(8,128)(2,1)}, ...) | async-done | bytes 2097168 | tf_op jit(solution)/shard_map/psum | solution.py:62
  225.2 170.4 %all-reduce.6.cloned.1.call-done = (bf16[16,128,128]{2,1,0:T(8,128)(2,1)}, bf16[16,128,128]{2,1,0:T(8,128)(2,1)}, bf16[16,128,128]{2,1,0:T(8,128)(2,1)}, bf16[16,128,128]{2,1,0:T(8,128)(2,1)}) async-done(((bf16[16,128,128]{2,1,0:T(8,128)(2,1)}, bf16[16,128,128]{2,1,0:T(8,128)(2,1)}, bf16[16,128,128]{2,1,0:T(8,128)(2,1)}, bf16[16,128,128]{2,1,0:T(8,128)(2,1)}), (bf16[16,128,128]{2,1,0:T(8,128)(2,1)}, ...) | async-done | bytes 2097168 | tf_op jit(solution)/shard_map/psum | solution.py:60
  397.1 87.1 %while.52 = (s32[]{:T(128)}, f32[32,16384]{1,0:T(8,128)}, s32[3,256]{1,0:T(4,128)S(1)}, bf16[16,128,128]{2,1,0:T(8,128)(2,1)}, bf16[16,128,128]{2,1,0:T(8,128)(2...) while((s32[]{:T(128)}, f32[32,16384]{1,0:T(8,128)}, s32[3,256]{1,0:T(4,128)S(1)}, ...), condition=%wide.region_4.6_spmd, body=%wide.region_2.5_spmd.sunk | while | flops 271584320 | bytes 23081360 | solution.py:32
  399.3 3.2 gather_fusion.1
  402.5 4.3 fusion.72
  406.9 12.1 %scatter_custom_fusion.17 = f32[32,16384]{1,0:T(8,128)} fusion(f32[32,16384]{1,0:T(8,128)} %get-tuple-element.671, s32[64]{0:T(128)S(1)} %fusion.71, f32[8,8,128,128]{3,2,1,0:T(8,128)} %bitcast.133), kind=kCustom, calls=%fused_computation.14.clone.1 | custom fusion | flops 1048576 | bytes 6291456 | tf_op jit(solution)/shard_map/while/body/eval_jaxpr/scatter-add | solution.py:30
  421.0 3.2 gather_fusion.1
  424.3 4.3 fusion.72
  428.6 12.1 %scatter_custom_fusion.17 = f32[32,16384]{1,0:T(8,128)} fusion(f32[32,16384]{1,0:T(8,128)} %get-tuple-element.671, s32[64]{0:T(128)S(1)} %fusion.71, f32[8,8,128,128]{3,2,1,0:T(8,128)} %bitcast.133), kind=kCustom, calls=%fused_computation.14.clone.1 | custom fusion | flops 1048576 | bytes 6291456 | tf_op jit(solution)/shard_map/while/body/eval_jaxpr/scatter-add | solution.py:30
  442.8 3.2 gather_fusion.1
  446.0 4.3 fusion.72
  450.3 12.1 %scatter_custom_fusion.17 = f32[32,16384]{1,0:T(8,128)} fusion(f32[32,16384]{1,0:T(8,128)} %get-tuple-element.671, s32[64]{0:T(128)S(1)} %fusion.71, f32[8,8,128,128]{3,2,1,0:T(8,128)} %bitcast.133), kind=kCustom, calls=%fused_computation.14.clone.1 | custom fusion | flops 1048576 | bytes 6291456 | tf_op jit(solution)/shard_map/while/body/eval_jaxpr/scatter-add | solution.py:30
  464.5 3.2 gather_fusion.1
  467.8 4.3 fusion.72
  472.1 12.1 %scatter_custom_fusion.17 = f32[32,16384]{1,0:T(8,128)} fusion(f32[32,16384]{1,0:T(8,128)} %get-tuple-element.671, s32[64]{0:T(128)S(1)} %fusion.71, f32[8,8,128,128]{3,2,1,0:T(8,128)} %bitcast.133), kind=kCustom, calls=%fused_computation.14.clone.1 | custom fusion | flops 1048576 | bytes 6291456 | tf_op jit(solution)/shard_map/while/body/eval_jaxpr/scatter-add | solution.py:30
  484.2 79.1 %while.53 = (s32[]{:T(128)}, f32[32,16384]{1,0:T(8,128)}, s32[3,256]{1,0:T(4,128)S(1)}, bf16[16,128,128]{2,1,0:T(8,128)(2,1)S(1)}, bf16[16,128,128]{2,1,0:T(8,12...) while((s32[]{:T(128)}, f32[32,16384]{1,0:T(8,128)}, s32[3,256]{1,0:T(4,128)S(1)}, ...), condition=%wide.region_9.11_spmd, body=%wide.region_7.10_spmd.sunk | while | flops 271584320 | bytes 23081360 | solution.py:32
  487.9 4.3 fusion.77
  492.2 12.1 %scatter_custom_fusion.19 = f32[32,16384]{1,0:T(8,128)} fusion(f32[32,16384]{1,0:T(8,128)} %get-tuple-element.698, s32[64]{0:T(128)S(1)} %fusion.76, f32[8,8,128,128]{3,2,1,0:T(8,128)} %bitcast.134), kind=kCustom, calls=%fused_computation.34.clone.1 | custom fusion | flops 1048576 | bytes 6291456 | tf_op jit(solution)/shard_map/while/body/eval_jaxpr/scatter-add | solution.py:30
  507.6 4.3 fusion.77
  511.9 12.1 %scatter_custom_fusion.19 = f32[32,16384]{1,0:T(8,128)} fusion(f32[32,16384]{1,0:T(8,128)} %get-tuple-element.698, s32[64]{0:T(128)S(1)} %fusion.76, f32[8,8,128,128]{3,2,1,0:T(8,128)} %bitcast.134), kind=kCustom, calls=%fused_computation.34.clone.1 | custom fusion | flops 1048576 | bytes 6291456 | tf_op jit(solution)/shard_map/while/body/eval_jaxpr/scatter-add | solution.py:30
  527.2 4.3 fusion.77
  531.6 12.1 %scatter_custom_fusion.19 = f32[32,16384]{1,0:T(8,128)} fusion(f32[32,16384]{1,0:T(8,128)} %get-tuple-element.698, s32[64]{0:T(128)S(1)} %fusion.76, f32[8,8,128,128]{3,2,1,0:T(8,128)} %bitcast.134), kind=kCustom, calls=%fused_computation.34.clone.1 | custom fusion | flops 1048576 | bytes 6291456 | tf_op jit(solution)/shard_map/while/body/eval_jaxpr/scatter-add | solution.py:30
  546.9 4.3 fusion.77
  551.2 12.1 %scatter_custom_fusion.19 = f32[32,16384]{1,0:T(8,128)} fusion(f32[32,16384]{1,0:T(8,128)} %get-tuple-element.698, s32[64]{0:T(128)S(1)} %fusion.76, f32[8,8,128,128]{3,2,1,0:T(8,128)} %bitcast.134), kind=kCustom, calls=%fused_computation.34.clone.1 | custom fusion | flops 1048576 | bytes 6291456 | tf_op jit(solution)/shard_map/while/body/eval_jaxpr/scatter-add | solution.py:30
  563.3 87.2 %while.54 = (s32[]{:T(128)}, f32[32,16384]{1,0:T(8,128)}, s32[3,256]{1,0:T(4,128)S(1)}, bf16[16,128,128]{2,1,0:T(8,128)(2,1)}, bf16[16,128,128]{2,1,0:T(8,128)(2...) while((s32[]{:T(128)}, f32[32,16384]{1,0:T(8,128)}, s32[3,256]{1,0:T(4,128)S(1)}, ...), condition=%wide.region_14.16_spmd, body=%wide.region_12.15_spmd.sunk | while | flops 271584320 | bytes 23081360 | solution.py:32
  565.6 3.2 gather_fusion.5
  568.9 4.3 fusion.82
  573.2 12.1 %scatter_custom_fusion.21 = f32[32,16384]{1,0:T(8,128)} fusion(f32[32,16384]{1,0:T(8,128)} %get-tuple-element.725, s32[64]{0:T(128)S(1)} %fusion.81, f32[8,8,128,128]{3,2,1,0:T(8,128)} %bitcast.135), kind=kCustom, calls=%fused_computation.54.clone.1 | custom fusion | flops 1048576 | bytes 6291456 | tf_op jit(solution)/shard_map/while/body/eval_jaxpr/scatter-add | solution.py:30
  590.6 4.3 fusion.82
  595.0 12.1 %scatter_custom_fusion.21 = f32[32,16384]{1,0:T(8,128)} fusion(f32[32,16384]{1,0:T(8,128)} %get-tuple-element.725, s32[64]{0:T(128)S(1)} %fusion.81, f32[8,8,128,128]{3,2,1,0:T(8,128)} %bitcast.135), kind=kCustom, calls=%fused_computation.54.clone.1 | custom fusion | flops 1048576 | bytes 6291456 | tf_op jit(solution)/shard_map/while/body/eval_jaxpr/scatter-add | solution.py:30
  612.4 4.3 fusion.82
  616.7 12.1 %scatter_custom_fusion.21 = f32[32,16384]{1,0:T(8,128)} fusion(f32[32,16384]{1,0:T(8,128)} %get-tuple-element.725, s32[64]{0:T(128)S(1)} %fusion.81, f32[8,8,128,128]{3,2,1,0:T(8,128)} %bitcast.135), kind=kCustom, calls=%fused_computation.54.clone.1 | custom fusion | flops 1048576 | bytes 6291456 | tf_op jit(solution)/shard_map/while/body/eval_jaxpr/scatter-add | solution.py:30
  634.1 4.3 fusion.82
  638.5 12.1 %scatter_custom_fusion.21 = f32[32,16384]{1,0:T(8,128)} fusion(f32[32,16384]{1,0:T(8,128)} %get-tuple-element.725, s32[64]{0:T(128)S(1)} %fusion.81, f32[8,8,128,128]{3,2,1,0:T(8,128)} %bitcast.135), kind=kCustom, calls=%fused_computation.54.clone.1 | custom fusion | flops 1048576 | bytes 6291456 | tf_op jit(solution)/shard_map/while/body/eval_jaxpr/scatter-add | solution.py:30
  650.6 78.9 %while.55 = (s32[]{:T(128)}, f32[32,16384]{1,0:T(8,128)}, s32[3,256]{1,0:T(4,128)S(1)}, bf16[16,128,128]{2,1,0:T(8,128)(2,1)S(1)}, bf16[16,128,128]{2,1,0:T(8,12...) while((s32[]{:T(128)}, f32[32,16384]{1,0:T(8,128)}, s32[3,256]{1,0:T(4,128)S(1)}, ...), condition=%wide.region_19.21_spmd, body=%wide.region_17.20_spmd.sunk | while | flops 271584320 | bytes 23081360 | solution.py:32
  654.0 4.3 fusion.87
  658.3 12.1 %scatter_custom_fusion.23 = f32[32,16384]{1,0:T(8,128)} fusion(f32[32,16384]{1,0:T(8,128)} %get-tuple-element.752, s32[64]{0:T(128)S(1)} %fusion.86, f32[8,8,128,128]{3,2,1,0:T(8,128)} %bitcast.136), kind=kCustom, calls=%fused_computation.74.clone.1 | custom fusion | flops 1048576 | bytes 6291456 | tf_op jit(solution)/shard_map/while/body/eval_jaxpr/scatter-add | solution.py:30
  673.7 4.3 fusion.87
  678.0 12.1 %scatter_custom_fusion.23 = f32[32,16384]{1,0:T(8,128)} fusion(f32[32,16384]{1,0:T(8,128)} %get-tuple-element.752, s32[64]{0:T(128)S(1)} %fusion.86, f32[8,8,128,128]{3,2,1,0:T(8,128)} %bitcast.136), kind=kCustom, calls=%fused_computation.74.clone.1 | custom fusion | flops 1048576 | bytes 6291456 | tf_op jit(solution)/shard_map/while/body/eval_jaxpr/scatter-add | solution.py:30
  693.3 4.3 fusion.87
  697.7 12.1 %scatter_custom_fusion.23 = f32[32,16384]{1,0:T(8,128)} fusion(f32[32,16384]{1,0:T(8,128)} %get-tuple-element.752, s32[64]{0:T(128)S(1)} %fusion.86, f32[8,8,128,128]{3,2,1,0:T(8,128)} %bitcast.136), kind=kCustom, calls=%fused_computation.74.clone.1 | custom fusion | flops 1048576 | bytes 6291456 | tf_op jit(solution)/shard_map/while/body/eval_jaxpr/scatter-add | solution.py:30
  713.0 4.3 fusion.87
  717.3 12.1 %scatter_custom_fusion.23 = f32[32,16384]{1,0:T(8,128)} fusion(f32[32,16384]{1,0:T(8,128)} %get-tuple-element.752, s32[64]{0:T(128)S(1)} %fusion.86, f32[8,8,128,128]{3,2,1,0:T(8,128)} %bitcast.136), kind=kCustom, calls=%fused_computation.74.clone.1 | custom fusion | flops 1048576 | bytes 6291456 | tf_op jit(solution)/shard_map/while/body/eval_jaxpr/scatter-add | solution.py:30
  729.4 3.6 convert_bitcast_fusion
  733.1 4.7 copy.12
  741.4 81.2 %all-reduce = (f32[1]{0:T(128)}, f32[1]{0:T(128)}) all-reduce(f32[1]{0:T(128)} %bitcast.39, f32[1]{0:T(128)} %bitcast.37), channel_id=1, replica_groups=mesh['row'=16,'col'=16] {'row','col'}, use_global_device_ids=true, to_apply=%region_25.27 | all-reduce | flops 2 | bytes 16 | tf_op jit(solution)/shard_map/psum | solution.py:69
  (127 shorter events, 67.2 us)
Async XLA Ops:
  7.2 218.1 %all-reduce.8.cloned.1.call-start = ((), (), s32[]{:S(2)}) async-start(), calls=%async_computation.1 | async-start | bytes 4194304 | tf_op jit(solution)/shard_map/psum | solution.py:62
  22.5 1.2 copy-start.4
  22.5 373.2 %all-reduce.6.cloned.1.call-start = ((), (), s32[]{:S(2)}) async-start(), calls=%async_computation | async-start | bytes 4194304 | tf_op jit(solution)/shard_map/psum | solution.py:60
  25.4 5.4 copy-start.7
  25.4 5.4 copy-start.5
  397.1 87.1 %copy-start.2 = (bf16[16,128,128]{2,1,0:T(8,128)(2,1)S(1)}, bf16[16,128,128]{2,1,0:T(8,128)(2,1)}, u32[]{:S(2)}) copy-start(bf16[16,128,128]{2,1,0:T(8,128)(2,1)} %get-tuple-element.692) | copy-start | bytes 1572868
  397.1 87.1 %copy-start.3 = (bf16[16,128,128]{2,1,0:T(8,128)(2,1)S(1)}, bf16[16,128,128]{2,1,0:T(8,128)(2,1)}, u32[]{:S(2)}) copy-start(bf16[16,128,128]{2,1,0:T(8,128)(2,1)} %get-tuple-element.691) | copy-start | bytes 1572868
  563.3 87.2 %copy-start = (bf16[16,128,128]{2,1,0:T(8,128)(2,1)S(1)}, bf16[16,128,128]{2,1,0:T(8,128)(2,1)}, u32[]{:S(2)}) copy-start(bf16[16,128,128]{2,1,0:T(8,128)(2,1)} %get-tuple-element.746) | copy-start | bytes 1572868
  563.3 87.2 %copy-start.1 = (bf16[16,128,128]{2,1,0:T(8,128)(2,1)S(1)}, bf16[16,128,128]{2,1,0:T(8,128)(2,1)}, u32[]{:S(2)}) copy-start(bf16[16,128,128]{2,1,0:T(8,128)(2,1)} %get-tuple-element.745) | copy-start | bytes 1572868
  737.7 3.0 copy-start.6
Sparse Core Ops, SparseCore 0:
  22.6 202.5 all-reduce.7
  228.7 166.9 all-reduce.5
where the time goes:
time: 844 us; the launch traced here: 832 us
  waiting for transfers between devices  363 us (43%)
  other arithmetic  207 us (25%)
  local copies, waits for them, and re-layouts  85 us (10%)
  blocking collectives  81.2 us (10%)
  matrix products  69.3 us (8%)
  between operations  24.6 us (3%)
    scatter-add x16, other arithmetic, one_block(): return running.at[target].add(flat_prods, mode='drop')  194 us
    psum x1, waiting for transfers between devices, body(): row_panel = lax.psum(row_term.astype(jnp.bfloat16), 'row')  193 us
    psum x1, waiting for transfers between devices, body(): col_panel = lax.psum(col_term.astype(jnp.bfloat16), 'col')  170 us
    psum x1, blocking collectives, body(): new_total = lax.psum(new_local, ('row', 'col'))  81.2 us
    dot_general x16, matrix products, one_block(): jnp.einsum('tij,tjk->tik', left_blocks, right_blocks, preferred_element_t...  69.3 us
    gather x16, local copies, waits for them, and re-layouts, one_block(): left_blocks = jnp.take(col_panel, piece[1], axis=0)  43.1 us
    gather x16, local copies, waits for them, and re-layouts, one_block(): right_blocks = jnp.take(row_panel, piece[2], axis=0)  23.7 us
  transfers between devices with their start and end apart: 2, of which 2 were waited for; matrix products, arithmetic and copies ran while one was open for 1% of the time, Pallas kernels for 0%

commit v1 on v0

v1 whole, which is shorter than its diff:
```python
import functools

import jax
import jax.numpy as jnp
from jax import lax
from jax.experimental import pallas as pl
from jax.experimental.pallas import tpu as pltpu
from jax.sharding import PartitionSpec as P

BS = 128
Q = 8
WIN = 4
NO = 32
TASKS = 1024
GROUP = 4
UNROLL = 4
NGROUP = 288
ZERO = 64
SCALE = 1.0 / (32 * 4 * 128) ** 0.5


def swap(value, axis, bit):
    return lax.ppermute(value, axis, [(i, i ^ bit) for i in range(16)])


def pick(stack, index):
    return lax.dynamic_index_in_dim(stack, index, 0, keepdims=False)


def column_panels(tiles, panels):
    me = lax.axis_index("col")
    x, z = me // 4, me % 4
    by_x = jnp.moveaxis(tiles, 2, 0)
    parts = [pick(by_x, x)] + [swap(pick(by_x, x ^ d), "col", 4 * d) for d in (1, 2, 3)]
    parts = jnp.moveaxis(jnp.stack(parts), 2, 1).reshape(8, 4, BS, BS)
    owner = panels // 2
    mine = [pick(parts, (x ^ (owner[s] // 4)) * 2 + panels[s] % 2) for s in range(WIN)]
    by_z = jnp.stack(mine, 1)
    parts = [pick(by_z, z)] + [swap(pick(by_z, z ^ d), "col", d) for d in (1, 2, 3)]
    parts = jnp.stack(parts)
    held = jnp.stack([pick(parts[:, s], z ^ (owner[s] % 4)) for s in range(WIN)])
    line = jnp.concatenate([held] + [swap(held, "col", d) for d in (1, 2, 3)])
    return [line] + [swap(line, "col", 4 * d) for d in (1, 2, 3)]


def row_panels(tiles, panels):
    me = lax.axis_index("row")
    y, zh, core = me // 4, (me // 2) % 2, me % 2
    by_y = jnp.moveaxis(tiles, 2, 0)
    parts = [pick(by_y, y)] + [swap(pick(by_y, y ^ d), "row", 4 * d) for d in (1, 2, 3)]
    parts = jnp.stack(parts).reshape(8, 2, 2, BS, BS)
    owner = panels // 2
    mine = [pick(parts, (y ^ (owner[s] // 4)) * 2 + panels[s] % 2) for s in range(WIN)]
    by_j = jnp.stack(mine, 1)
    own = pick(by_j, core)
    got = swap(pick(by_j, 1 - core), "row", 1)
    here = (owner % 2 == core).reshape(WIN, 1, 1, 1)
    half = jnp.where(here, own, got)
    got = swap(half, "row", 2)
    here = ((owner // 2) % 2 == zh).reshape(WIN, 1, 1, 1)
    half = jnp.where(here, half, got).reshape(WIN * 2, BS, BS)
    line = jnp.concatenate([half] + [swap(half, "row", 4 * d) for d in (1, 2, 3)])
    return [line, swap(line, "row", 1)]


def plan(tasks, coords):
    me_r, me_c = lax.axis_index("row"), lax.axis_index("col")
    x, z = me_c // 4, me_c % 4
    y, core = me_r // 4, me_r % 2
    outs = tasks[:, 0].reshape(TASKS)
    left = tasks[:, 1].reshape(TASKS)
    right = tasks[:, 2].reshape(TASKS)
    step = jnp.arange(TASKS, dtype=jnp.int32) // (TASKS // WIN)
    left = (x ^ (left % 8 // 2)) * 16 + (z ^ (left // 8 * 2 + left % 2)) * 4 + step
    right = (core ^ (right // 8)) * 32 + (y ^ (right % 8 // 2)) * 8 + step * 2 + right % 2
    slots = jnp.arange(NO, dtype=jnp.int32)
    hot = outs[:, None] == slots[None, :]
    hot_bf = hot.astype(jnp.bfloat16)
    ids = jnp.arange(TASKS, dtype=jnp.int32)
    earlier = (ids[None, :] < ids[:, None]).astype(jnp.bfloat16)
    seen = jnp.dot(earlier, hot_bf, preferred_element_type=jnp.float32).astype(jnp.int32)
    counts = jnp.sum(hot.astype(jnp.int32), axis=0)
    groups = (counts + GROUP - 1) // GROUP
    diag = coords[0] == coords[1]
    order = jnp.where(diag, 0, NO) + slots
    starts = jnp.sum(jnp.where(order[None, :] < order[:, None], groups[None, :], 0), axis=1)
    place = jnp.sum(jnp.where(hot, seen + GROUP * starts[None, :], 0), axis=1)
    place = jnp.where(outs >= 0, place, -1)
    spots = jnp.arange(NGROUP * GROUP, dtype=jnp.int32)
    move = (spots[:, None] == place[None, :]).astype(jnp.bfloat16)
    pair = jnp.stack([left - ZERO, right], axis=1).astype(jnp.bfloat16)
    lists = jnp.dot(move, pair, preferred_element_type=jnp.float32).astype(jnp.int32)
    gid = jnp.arange(NGROUP, dtype=jnp.int32)[:, None]
    inside = (gid >= starts[None, :]) & (gid < (starts + groups)[None, :])
    target = jnp.sum(jnp.where(inside, slots[None, :], 0), axis=1)
    total = jnp.sum(groups)
    diag_total = jnp.sum(jnp.where(diag, groups, 0))
    return lists[:, 0] + ZERO, lists[:, 1], target, jnp.stack([total, diag_total]), diag.astype(jnp.int32)


def group_product(left_ref, right_ref, lhs, rhs, group):
    spots = [group * GROUP + k for k in range(GROUP)]
    a = jnp.concatenate([lhs[left_ref[t]] for t in spots], axis=1)
    b = jnp.concatenate([rhs[right_ref[t]] for t in spots], axis=0)
    return jnp.dot(a, b, preferred_element_type=jnp.float32)


def trace_kernel(left_ref, right_ref, target_ref, total_ref, branch_ref, diag_ref, lhs, rhs, own, out, old, new):
    out[...] = jnp.zeros_like(out)
    any_diag = functools.reduce(jnp.maximum, [diag_ref[o] for o in range(NO)])

    @pl.when(any_diag > 0)
    def _():
        old[...] = jnp.zeros_like(old)
        new[...] = jnp.zeros_like(new)

        def add_own(o, carry):
            @pl.when(diag_ref[o] > 0)
            def _():
                block = own[o].astype(jnp.float32)
                old[...] += block
                new[...] += block * jnp.where(branch_ref[o] == 0, 0.0, 2.0)

            return carry

        lax.fori_loop(0, NO, add_own, 0)

        def one(g, carry):
            part = group_product(left_ref, right_ref, lhs, rhs, g)
            new[...] += part * jnp.where(branch_ref[target_ref[g]] == 0, 1.0, -1.0)
            return carry

        lax.fori_loop(0, total_ref[1], one, 0)
        shape = (BS, BS)
        eye = lax.broadcasted_iota(jnp.int32, shape, 0) == lax.broadcasted_iota(jnp.int32, shape, 1)
        out[0:1, :] = jnp.sum(jnp.where(eye, old[...], 0.0), axis=0, keepdims=True)
        out[1:2, :] = jnp.sum(jnp.where(eye, new[...], 0.0), axis=0, keepdims=True)


def main_kernel(left_ref, right_ref, target_ref, total_ref, branch_ref, lhs, rhs, own, out, acc):
    acc[...] = jnp.zeros_like(acc)

    def some(it, carry):
        for u in range(UNROLL):
            g = it * UNROLL + u
            part = group_product(left_ref, right_ref, lhs, rhs, g)
            o = target_ref[g]
            acc[o] += part
        return carry

    lax.fori_loop(0, (total_ref[0] + UNROLL - 1) // UNROLL, some, 0)

    def finish(o, carry):
        product = acc[o]
        flip = 2.0 * own[o].astype(jnp.float32) - product
        out[o] = jnp.where(branch_ref[o] == 0, product, flip).astype(jnp.bfloat16)
        return carry

    lax.fori_loop(0, NO, finish, 0)


def reduce_all(value):
    for axis, bits in (("row", (1, 2)), ("row", (4, 8)), ("col", (1, 2)), ("col", (4, 8))):
        low, high = bits
        one, two, three = (swap(value, axis, b) for b in (low, high, low + high))
        value = (value + one) + (two + three)
    return value


def body(p_blocks, coords, tasks, window_panels, branch):
    own = p_blocks[0, 0]
    tiles = own.reshape(2, 2, 4, 2, BS, BS)
    left, right, target, totals, diag = plan(tasks[0, 0], coords[0, 0])
    columns = column_panels(tiles, window_panels)
    rows = row_panels(tiles, window_panels)
    lhs = jnp.concatenate(columns + [jnp.zeros((1, BS, BS), jnp.bfloat16)])
    rhs = jnp.concatenate(rows)
    smem = pl.BlockSpec(memory_space=pltpu.SMEM)
    vmem = pl.BlockSpec(memory_space=pltpu.VMEM)
    params = pltpu.CompilerParams(vmem_limit_bytes=24 << 20)
    part = pl.pallas_call(
        trace_kernel,
        out_shape=jax.ShapeDtypeStruct((8, BS), jnp.float32),
        in_specs=[smem] * 6 + [vmem] * 3,
        out_specs=vmem,
        scratch_shapes=[pltpu.VMEM((BS, BS), jnp.float32)] * 2,
        compiler_params=params,
        name="trace_part",
    )(left, right, target, totals, branch[0, 0], diag, lhs, rhs, own)
    traces = jnp.sum(reduce_all(part), axis=1)[:2] * SCALE
    p_next = pl.pallas_call(
        main_kernel,
        out_shape=jax.ShapeDtypeStruct((NO, BS, BS), jnp.bfloat16),
        in_specs=[smem] * 5 + [vmem] * 3,
        out_specs=vmem,
        scratch_shapes=[pltpu.VMEM((NO, BS, BS), jnp.float32)],
        compiler_params=params,
        cost_estimate=pl.CostEstimate(flops=4 << 30, bytes_accessed=8 << 20, transcendentals=0),
        name="block_products",
    )(left, right, target, totals, branch[0, 0], lhs, rhs, own)
    return p_next[None, None], traces


def solution(mesh):
    in_specs = (
        P("row", "col", None, None, None),
        P("row", "col", None, None),
        P("row", "col", None, None, None),
        P(),
        P("row", "col", None),
    )
    out_specs = (P("row", "col", None, None, None), P())
    return jax.shard_map(body, mesh=mesh, in_specs=in_specs, out_specs=out_specs, check_vma=False)
```

time: 844 us -> 160 us (0.19); the launches traced: 832 us -> 160 us
  waiting for transfers between devices: 363 us -> 49.9 us
  other arithmetic: 207 us -> 4.12 us
  blocking collectives: 81.2 us -> 0 us
  local copies, waits for them, and re-layouts: 85 us -> 4.17 us
  matrix products: 69.3 us -> 1.42 us
  starting transfers between devices: 0.08 us -> 62.4 us
  Pallas kernels: 0 us -> 18.9 us
    psum x2 -> x0, waiting for transfers between devices: 363 us -> none  [the longest x1 193 us: body(): row_panel = lax.psum(row_term.astype(jnp.bfloat16), 'row')]
    scatter-add x16 -> x0, other arithmetic: 194 us -> none  [one_block(): return running.at[target].add(flat_prods, mode='drop')]
    psum x1 -> x0, blocking collectives: 81.2 us -> none  [body(): new_total = lax.psum(new_local, ('row', 'col'))]
    gather x34 -> x0, local copies, waits for them, and re-layouts: 70.5 us -> none  [the longest x16 43.1 us: one_block(): left_blocks = jnp.take(col_panel, piece[1], axis=0)]
    dot_general x16 -> x2, matrix products: 69.3 us -> 1.42 us  [the longest x1 0.87 us: plan(): jnp.dot(move, pair, preferred_element_type=jnp.float32).astype(jnp.int32)]
    ppermute x0 -> x33, starting transfers between devices: none -> 62.4 us  [swap(): return lax.ppermute(value, axis, [(i, i ^ bit) for i in range(16)])]
    ppermute x0 -> x33, waiting for transfers between devices: none -> 49.9 us  [swap(): return lax.ppermute(value, axis, [(i, i ^ bit) for i in range(16)])]
    pallas_call x0 -> x2, Pallas kernels: none -> 18.9 us  [the longest x1 18.1 us: body(): pl.pallas_call(main_kernel, out_shape=jax.ShapeDtypeStruct((NO, BS, BS),...]
  transfers between devices with their start and end apart: 2 -> 33, of which waited for: 2 -> 15; matrix products, arithmetic and copies ran while one was open for 1% -> 4% of each run, Pallas kernels for 0% -> 11%
where the time goes in v1:
time: 160 us
  starting transfers between devices  62.4 us (39%)
  waiting for transfers between devices  49.9 us (31%)
  Pallas kernels  18.9 us (12%)
  between operations  18.9 us (12%)
  local copies, waits for them, and re-layouts  4.17 us (3%)
  other arithmetic  4.12 us (3%)
    ppermute x33, starting transfers between devices, swap(): return lax.ppermute(value, axis, [(i, i ^ bit) for i in range(16)])  62.4 us
    ppermute x33, waiting for transfers between devices, swap(): return lax.ppermute(value, axis, [(i, i ^ bit) for i in range(16)])  49.9 us
    pallas_call x1, Pallas kernels, body(): pl.pallas_call(main_kernel, out_shape=jax.ShapeDtypeStruct((NO, BS, BS),...  18.1 us
  transfers between devices with their start and end apart: 33, of which 15 were waited for; matrix products, arithmetic and copies ran while one was open for 4% of the time, Pallas kernels for 11%

profile of v1, /device:TPU:2, one launch (start us, length us, event | category | flops | bytes accessed | tf_op | source)
XLA Modules:
  0.0 159.8 jit_solution(4422318196671208732)
XLA Ops:
  0.7 1.7 %dynamic-slice_bitcast_fusion.4 = (bf16[1,2,2,2,128,128]{5,4,3,2,1,0:T(8,128)(2,1)S(1)}, bf16[2,2,2,128,128]{4,3,2,1,0:T(8,128)(2,1)S(1)}, bf16[2,2,2,128,128]{4...) fusion(bf16[2,2,4,2,128,128]{5,4,3,2,1,0:T(8,128)(2,1)} %bitcas, ...), kind=kLoop, calls=%fused_computation.21 | loop fusion | bytes 4194336 | tf_op jit(solution)/shard_map/jit(dynamic_index_in_dim)/dynamic_slice | solution.py:27
  2.4 1.6 collective-permute-start.2
  4.0 2.8 %collective-permute-start.1 = (bf16[2,2,2,128,128]{4,3,2,1,0:T(8,128)(2,1)S(1)}, bf16[2,2,2,128,128]{4,3,2,1,0:T(8,128)(2,1)S(1)}, u32[]{:S(2)}, u32[]{:S(2)}) collective-permute-start(bf16[2,2,2,128,128]{4,3,2,1,0:T(8,128)(2,1)S(1)} %get-tuple-element.28), channel_id=1, source_target_pairs={{0,8},{1,9},{2,10},{3,11},{4,12},{5,13},{6,14},{7,15},{8,0},{9,1},... | collective-permute-start | bytes 786440 | tf_op jit(solution)/shard_map/ppermute | solution.py:23
  6.9 2.8 %collective-permute-start.14 = (bf16[2,2,2,128,128]{4,3,2,1,0:T(8,128)(2,1)S(1)}, bf16[2,2,2,128,128]{4,3,2,1,0:T(8,128)(2,1)S(1)}, u32[]{:S(2)}, u32[]{:S(2)}) collective-permute-start(bf16[2,2,2,128,128]{4,3,2,1,0:T(8,128)(2,1)S(1)} %get-tuple-element.24), channel_id=1, source_target_pairs={{0,192},{16,208},{32,224},{48,240},{64,128},{80,144},{96,160},{112... | collective-permute-start | bytes 786440 | tf_op jit(solution)/shard_map/ppermute | solution.py:23
  9.6 0.6 collective-permute-start.13
  10.4 0.6 fusion.23
  11.3 0.5 fusion.7
  11.9 0.7 fusion.26
  12.8 0.7 fusion.25
  31.1 0.9 fusion.3
  32.0 0.7 collective-permute-start.12
  33.1 4.5 %collective-permute-start.5 = (bf16[4,128,128]{2,1,0:T(8,128)(2,1)S(1)}, bf16[4,128,128]{2,1,0:T(8,128)(2,1)S(1)}, u32[]{:S(2)}, u32[]{:S(2)}) collective-permute-start(bf16[4,128,128]{2,1,0:T(8,128)(2,1)S(1)} %get-tuple-element.40), channel_id=1, source_target_pairs={{0,3},{1,2},{2,1},{3,0},{4,7},{5,6},{6,5},{7,4},{8,11},{9,10},{10,... | collective-permute-start | bytes 393224 | tf_op jit(solution)/shard_map/ppermute | solution.py:23
  37.6 0.7 collective-permute-start.3
  39.0 2.6 %collective-permute-done.5 = bf16[4,128,128]{2,1,0:T(8,128)(2,1)S(1)} collective-permute-done((bf16[4,128,128]{2,1,0:T(8,128)(2,1)S(1)}, bf16[4,128,128]{2,1,0:T(8,128)(2,1)S(1)}, u32[]{:S(2)}, u32[]{:S(2)}) %collective-permute-start.5) | collective-permute-done | bytes 131104 | tf_op jit(solution)/shard_map/ppermute | solution.py:23
  41.6 4.9 %collective-permute-done.4 = bf16[4,128,128]{2,1,0:T(8,128)(2,1)S(1)} collective-permute-done((bf16[4,128,128]{2,1,0:T(8,128)(2,1)S(1)}, bf16[4,128,128]{2,1,0:T(8,128)(2,1)S(1)}, u32[]{:S(2)}, u32[]{:S(2)}) %collective-permute-start.4) | collective-permute-done | bytes 131104 | tf_op jit(solution)/shard_map/ppermute | solution.py:23
  46.8 0.4 collective-permute-start.6
  47.2 3.0 %collective-permute-start.7 = (bf16[4,128,128]{2,1,0:T(8,128)(2,1)S(1)}, bf16[4,128,128]{2,1,0:T(8,128)(2,1)S(1)}, u32[]{:S(2)}, u32[]{:S(2)}) collective-permute-start(bf16[4,128,128]{2,1,0:T(8,128)(2,1)S(1)} %pad_maximum_fusion.5), channel_id=1, source_target_pairs={{0,2},{1,3},{2,0},{3,1},{4,6},{5,7},{6,4},{7,5},{8,10},{9,11},{10,... | collective-permute-start | bytes 393224 | tf_op jit(solution)/shard_map/ppermute | solution.py:23
  50.3 1.0 collective-permute-start.8
  51.4 6.2 %collective-permute-start.16 = (bf16[4,2,128,128]{3,2,1,0:T(8,128)(2,1)S(1)}, bf16[4,2,128,128]{3,2,1,0:T(8,128)(2,1)S(1)}, u32[]{:S(2)}, u32[]{:S(2)}) collective-permute-start(bf16[4,2,128,128]{3,2,1,0:T(8,128)(2,1)S(1)} %bitcast_select_fusion), channel_id=1, source_target_pairs={{0,32},{16,48},{32,0},{48,16},{64,96},{80,112},{96,64},{112,80},{1... | collective-permute-start | bytes 786440 | tf_op jit(solution)/shard_map/ppermute | solution.py:23
  57.7 12.7 %collective-permute-done.7 = bf16[4,128,128]{2,1,0:T(8,128)(2,1)S(1)} collective-permute-done((bf16[4,128,128]{2,1,0:T(8,128)(2,1)S(1)}, bf16[4,128,128]{2,1,0:T(8,128)(2,1)S(1)}, u32[]{:S(2)}, u32[]{:S(2)}) %collective-permute-start.7) | collective-permute-done | bytes 131104 | tf_op jit(solution)/shard_map/ppermute | solution.py:23
  70.4 2.0 %collective-permute-done.16 = bf16[4,2,128,128]{3,2,1,0:T(8,128)(2,1)S(1)} collective-permute-done((bf16[4,2,128,128]{3,2,1,0:T(8,128)(2,1)S(1)}, bf16[4,2,128,128]{3,2,1,0:T(8,128)(2,1)S(1)}, u32[]{:S(2)}, u32[]{:S(2)}) %collective-permute-start.16) | collective-permute-done | bytes 262176 | tf_op jit(solution)/shard_map/ppermute | solution.py:23
  72.5 1.6 %collective-permute-start.17 = (bf16[8,128,128]{2,1,0:T(8,128)(2,1)S(1)}, bf16[8,128,128]{2,1,0:T(8,128)(2,1)S(1)}, u32[]{:S(2)}, u32[]{:S(2)}) collective-permute-start(bf16[8,128,128]{2,1,0:T(8,128)(2,1)S(1)} %bitcast.112), channel_id=1, source_target_pairs={{0,64},{16,80},{32,96},{48,112},{64,0},{80,16},{96,32},{112,48},{1... | collective-permute-start | bytes 786440 | tf_op jit(solution)/shard_map/ppermute | solution.py:23
  74.1 2.9 %collective-permute-start.18 = (bf16[8,128,128]{2,1,0:T(8,128)(2,1)S(1)}, bf16[8,128,128]{2,1,0:T(8,128)(2,1)S(1)}, u32[]{:S(2)}, u32[]{:S(2)}) collective-permute-start(bf16[8,128,128]{2,1,0:T(8,128)(2,1)S(1)} %bitcast.113), channel_id=1, source_target_pairs={{0,128},{16,144},{32,160},{48,176},{64,192},{80,208},{96,224},{112... | collective-permute-start | bytes 786440 | tf_op jit(solution)/shard_map/ppermute | solution.py:23
  77.4 0.6 collective-permute-start.9
  78.1 2.5 %collective-permute-start.10 = (bf16[16,128,128]{2,1,0:T(8,128)(2,1)S(1)}, bf16[16,128,128]{2,1,0:T(8,128)(2,1)S(1)}, u32[]{:S(2)}, u32[]{:S(2)}) collective-permute-start(bf16[16,128,128]{2,1,0:T(8,128)(2,1)S(1)} %get-tuple-element.43), channel_id=1, source_target_pairs={{0,8},{1,9},{2,10},{3,11},{4,12},{5,13},{6,14},{7,15},{8,0},{9,1},... | collective-permute-start | bytes 1572872 | tf_op jit(solution)/shard_map/ppermute | solution.py:23
  80.6 1.1 collective-permute-start.11
  81.7 3.8 %collective-permute-done.18 = bf16[8,128,128]{2,1,0:T(8,128)(2,1)S(1)} collective-permute-done((bf16[8,128,128]{2,1,0:T(8,128)(2,1)S(1)}, bf16[8,128,128]{2,1,0:T(8,128)(2,1)S(1)}, u32[]{:S(2)}, u32[]{:S(2)}) %collective-permute-start.18) | collective-permute-done | bytes 262176 | tf_op jit(solution)/shard_map/ppermute | solution.py:23
  85.5 2.5 %collective-permute-done.19 = bf16[8,128,128]{2,1,0:T(8,128)(2,1)S(1)} collective-permute-done((bf16[8,128,128]{2,1,0:T(8,128)(2,1)S(1)}, bf16[8,128,128]{2,1,0:T(8,128)(2,1)S(1)}, u32[]{:S(2)}, u32[]{:S(2)}) %collective-permute-start.19) | collective-permute-done | bytes 262176 | tf_op jit(solution)/shard_map/ppermute | solution.py:23
  88.3 1.4 pad_add_fusion.total_ref
  89.7 2.6 %collective-permute-done.9 = bf16[16,128,128]{2,1,0:T(8,128)(2,1)S(1)} collective-permute-done((bf16[16,128,128]{2,1,0:T(8,128)(2,1)S(1)}, bf16[16,128,128]{2,1,0:T(8,128)(2,1)S(1)}, u32[]{:S(2)}, u32[]{:S(2)}) %collective-permute-start.9) | collective-permute-done | bytes 524320 | tf_op jit(solution)/shard_map/ppermute | solution.py:23
  92.4 7.0 %collective-permute-done.10 = bf16[16,128,128]{2,1,0:T(8,128)(2,1)S(1)} collective-permute-done((bf16[16,128,128]{2,1,0:T(8,128)(2,1)S(1)}, bf16[16,128,128]{2,1,0:T(8,128)(2,1)S(1)}, u32[]{:S(2)}, u32[]{:S(2)}) %collective-permute-start.10) | collective-permute-done | bytes 524320 | tf_op jit(solution)/shard_map/ppermute | solution.py:23
  99.4 1.6 collective-permute-done.11
  101.4 0.8 trace_part.1
  102.4 5.9 %collective-permute-start.21 = (f32[8,128]{1,0:T(8,128)S(1)}, f32[8,128]{1,0:T(8,128)S(1)}, u32[]{:S(2)}, u32[]{:S(2)}) collective-permute-start(f32[8,128]{1,0:T(8,128)S(1)} %trace_part.1), channel_id=1, source_target_pairs={{0,16},{16,0},{32,48},{48,32},{64,80},{80,64},{96,112},{112,96},{1... | collective-permute-start | bytes 12296 | tf_op jit(solution)/shard_map/ppermute | solution.py:23
  108.3 1.5 collective-permute-done.22
  109.8 1.9 %collective-permute-start.25 = (f32[8,128]{1,0:T(8,128)S(1)}, f32[8,128]{1,0:T(8,128)S(1)}, u32[]{:S(2)}, u32[]{:S(2)}) collective-permute-start(f32[8,128]{1,0:T(8,128)S(1)} %add_add_fusion.2), channel_id=1, source_target_pairs={{0,128},{16,144},{32,160},{48,176},{64,192},{80,208},{96,224},{112... | collective-permute-start | bytes 12296 | tf_op jit(solution)/shard_map/ppermute | solution.py:23
  111.7 11.5 %collective-permute-start.26 = (f32[8,128]{1,0:T(8,128)S(1)}, f32[8,128]{1,0:T(8,128)S(1)}, u32[]{:S(2)}, u32[]{:S(2)}) collective-permute-start(f32[8,128]{1,0:T(8,128)S(1)} %add_add_fusion.2), channel_id=1, source_target_pairs={{0,192},{16,208},{32,224},{48,240},{64,128},{80,144},{96,160},{112... | collective-permute-start | bytes 12296 | tf_op jit(solution)/shard_map/ppermute | solution.py:23
  123.3 1.6 collective-permute-done.26
  124.8 2.0 %collective-permute-done.24 = f32[8,128]{1,0:T(8,128)S(1)} collective-permute-done((f32[8,128]{1,0:T(8,128)S(1)}, f32[8,128]{1,0:T(8,128)S(1)}, u32[]{:S(2)}, u32[]{:S(2)}) %collective-permute-start.24) | collective-permute-done | bytes 4128 | tf_op jit(solution)/shard_map/ppermute | solution.py:23
  126.9 3.9 %collective-permute-start.28 = (f32[8,128]{1,0:T(8,128)S(1)}, f32[8,128]{1,0:T(8,128)S(1)}, u32[]{:S(2)}, u32[]{:S(2)}) collective-permute-start(f32[8,128]{1,0:T(8,128)S(1)} %add_add_fusion.1), channel_id=1, source_target_pairs={{0,2},{1,3},{2,0},{3,1},{4,6},{5,7},{6,4},{7,5},{8,10},{9,11},{10,... | collective-permute-start | bytes 12296 | tf_op jit(solution)/shard_map/ppermute | solution.py:23
  130.8 0.7 collective-permute-start.27
  131.5 0.9 collective-permute-done.28
  132.4 3.8 %collective-permute-done.29 = f32[8,128]{1,0:T(8,128)S(1)} collective-permute-done((f32[8,128]{1,0:T(8,128)S(1)}, f32[8,128]{1,0:T(8,128)S(1)}, u32[]{:S(2)}, u32[]{:S(2)}) %collective-permute-start.29) | collective-permute-done | bytes 4128 | tf_op jit(solution)/shard_map/ppermute | solution.py:23
  136.2 1.2 collective-permute-start.31
  137.4 0.8 collective-permute-start.32
  138.2 2.8 %collective-permute-start.30 = (f32[8,128]{1,0:T(8,128)S(1)}, f32[8,128]{1,0:T(8,128)S(1)}, u32[]{:S(2)}, u32[]{:S(2)}) collective-permute-start(f32[8,128]{1,0:T(8,128)S(1)} %add_add_fusion), channel_id=1, source_target_pairs={{0,4},{1,5},{2,6},{3,7},{4,0},{5,1},{6,2},{7,3},{8,12},{9,13},{10,... | collective-permute-start | bytes 12296 | tf_op jit(solution)/shard_map/ppermute | solution.py:23
  141.0 18.1 %block_products.1 = bf16[32,128,128]{2,1,0:T(8,128)(2,1)} custom-call(s32[1152]{0:T(1024)S(1)} %get-tuple-element.3.left_ref, s32[1152]{0:T(1024)S(1)} %get-tuple-element.2.right_ref, s32[288]{0:T(512)S(1)} %select_reduce_fusion.target_ref, s32[2]{0:T(128)S(1)} %pad_add_fusion.total_ref, s32[32]{0:T(128)S(1)} %bitcast.109, ...), custom_call_target="tpu_custom_call" | custom-call | flops 4294967296 | bytes 8388608 | tf_op jit(solution)/shard_map/block_products/pallas_call | solution.py:191
  159.3 0.5 slice_multiply_fusion
  (92 shorter events, 3.8 us)
Async XLA Ops:
  0.7 9.6 %copy-start.4 = (s32[1,1,2,32]{3,2,1,0:T(2,128)S(1)}, s32[1,1,2,32]{3,2,1,0:T(2,128)}, u32[]{:S(2)}) copy-start(s32[1,1,2,32]{3,2,1,0:T(2,128)} %param.6) | copy-start | bytes 772
  0.7 9.6 %copy-start.3 = (s32[1,1,4,3,256]{4,2,3,1,0:T(4,128)S(1)}, s32[1,1,4,3,256]{4,2,3,1,0:T(4,128)}, u32[]{:S(2)}) copy-start(s32[1,1,4,3,256]{4,2,3,1,0:T(4,128)} %param.7) | copy-start | bytes 36868
  0.7 11.1 %copy-start.2 = (s32[4]{0:T(128)S(1)}, s32[4]{0:T(128)}, u32[]{:S(2)}) copy-start(s32[4]{0:T(128)} %param.8) | copy-start | bytes 52
  2.4 29.5 %collective-permute-start.2 = (bf16[2,2,2,128,128]{4,3,2,1,0:T(8,128)(2,1)S(1)}, bf16[2,2,2,128,128]{4,3,2,1,0:T(8,128)(2,1)S(1)}, u32[]{:S(2)}, u32[]{:S(2)}) collective-permute-start(bf16[2,2,2,128,128]{4,3,2,1,0:T(8,128)(2,1)S(1)} %get-tuple-element.27), channel_id=1, source_target_pairs={{0,12},{1,13},{2,14},{3,15},{4,8},{5,9},{6,10},{7,11},{8,4},{9,5},... | collective-permute-start | bytes 786440 | tf_op jit(solution)/shard_map/ppermute | solution.py:23
  4.0 28.7 %collective-permute-start.1 = (bf16[2,2,2,128,128]{4,3,2,1,0:T(8,128)(2,1)S(1)}, bf16[2,2,2,128,128]{4,3,2,1,0:T(8,128)(2,1)S(1)}, u32[]{:S(2)}, u32[]{:S(2)}) collective-permute-start(bf16[2,2,2,128,128]{4,3,2,1,0:T(8,128)(2,1)S(1)} %get-tuple-element.28), channel_id=1, source_target_pairs={{0,8},{1,9},{2,10},{3,11},{4,12},{5,13},{6,14},{7,15},{8,0},{9,1},... | collective-permute-start | bytes 786440 | tf_op jit(solution)/shard_map/ppermute | solution.py:23
  6.9 25.8 %collective-permute-start = (bf16[2,2,2,128,128]{4,3,2,1,0:T(8,128)(2,1)S(1)}, bf16[2,2,2,128,128]{4,3,2,1,0:T(8,128)(2,1)S(1)}, u32[]{:S(2)}, u32[]{:S(2)}) collective-permute-start(bf16[2,2,2,128,128]{4,3,2,1,0:T(8,128)(2,1)S(1)} %get-tuple-element.29), channel_id=1, source_target_pairs={{0,4},{1,5},{2,6},{3,7},{4,0},{5,1},{6,2},{7,3},{8,12},{9,13},{10,... | collective-permute-start | bytes 786440 | tf_op jit(solution)/shard_map/ppermute | solution.py:23
  6.9 30.7 %collective-permute-start.14 = (bf16[2,2,2,128,128]{4,3,2,1,0:T(8,128)(2,1)S(1)}, bf16[2,2,2,128,128]{4,3,2,1,0:T(8,128)(2,1)S(1)}, u32[]{:S(2)}, u32[]{:S(2)}) collective-permute-start(bf16[2,2,2,128,128]{4,3,2,1,0:T(8,128)(2,1)S(1)} %get-tuple-element.24), channel_id=1, source_target_pairs={{0,192},{16,208},{32,224},{48,240},{64,128},{80,144},{96,160},{112... | collective-permute-start | bytes 786440 | tf_op jit(solution)/shard_map/ppermute | solution.py:23
  9.6 28.6 %collective-permute-start.13 = (bf16[2,2,2,128,128]{4,3,2,1,0:T(8,128)(2,1)S(1)}, bf16[2,2,2,128,128]{4,3,2,1,0:T(8,128)(2,1)S(1)}, u32[]{:S(2)}, u32[]{:S(2)}) collective-permute-start(bf16[2,2,2,128,128]{4,3,2,1,0:T(8,128)(2,1)S(1)} %get-tuple-element.25), channel_id=1, source_target_pairs={{0,128},{16,144},{32,160},{48,176},{64,192},{80,208},{96,224},{112... | collective-permute-start | bytes 786440 | tf_op jit(solution)/shard_map/ppermute | solution.py:23
  32.0 6.6 %collective-permute-start.12 = (bf16[2,2,2,128,128]{4,3,2,1,0:T(8,128)(2,1)S(1)}, bf16[2,2,2,128,128]{4,3,2,1,0:T(8,128)(2,1)S(1)}, u32[]{:S(2)}, u32[]{:S(2)}) collective-permute-start(bf16[2,2,2,128,128]{4,3,2,1,0:T(8,128)(2,1)S(1)} %get-tuple-element.26), channel_id=1, source_target_pairs={{0,64},{16,80},{32,96},{48,112},{64,0},{80,16},{96,32},{112,48},{1... | collective-permute-start | bytes 786440 | tf_op jit(solution)/shard_map/ppermute | solution.py:23
  33.1 8.5 %collective-permute-start.5 = (bf16[4,128,128]{2,1,0:T(8,128)(2,1)S(1)}, bf16[4,128,128]{2,1,0:T(8,128)(2,1)S(1)}, u32[]{:S(2)}, u32[]{:S(2)}) collective-permute-start(bf16[4,128,128]{2,1,0:T(8,128)(2,1)S(1)} %get-tuple-element.40), channel_id=1, source_target_pairs={{0,3},{1,2},{2,1},{3,0},{4,7},{5,6},{6,5},{7,4},{8,11},{9,10},{10,... | collective-permute-start | bytes 393224 | tf_op jit(solution)/shard_map/ppermute | solution.py:23
  37.6 8.9 %collective-permute-start.4 = (bf16[4,128,128]{2,1,0:T(8,128)(2,1)S(1)}, bf16[4,128,128]{2,1,0:T(8,128)(2,1)S(1)}, u32[]{:S(2)}, u32[]{:S(2)}) collective-permute-start(bf16[4,128,128]{2,1,0:T(8,128)(2,1)S(1)} %get-tuple-element.41), channel_id=1, source_target_pairs={{0,2},{1,3},{2,0},{3,1},{4,6},{5,7},{6,4},{7,5},{8,10},{9,11},{10,... | collective-permute-start | bytes 393224 | tf_op jit(solution)/shard_map/ppermute | solution.py:23
  37.6 8.9 %collective-permute-start.3 = (bf16[4,128,128]{2,1,0:T(8,128)(2,1)S(1)}, bf16[4,128,128]{2,1,0:T(8,128)(2,1)S(1)}, u32[]{:S(2)}, u32[]{:S(2)}) collective-permute-start(bf16[4,128,128]{2,1,0:T(8,128)(2,1)S(1)} %get-tuple-element.42), channel_id=1, source_target_pairs={{0,1},{1,0},{2,3},{3,2},{4,5},{5,4},{6,7},{7,6},{8,9},{9,8},{10,11... | collective-permute-start | bytes 393224 | tf_op jit(solution)/shard_map/ppermute | solution.py:23
  38.9 12.4 %collective-permute-start.15 = (bf16[4,2,128,128]{3,2,1,0:T(8,128)(2,1)S(1)}, bf16[4,2,128,128]{3,2,1,0:T(8,128)(2,1)S(1)}, u32[]{:S(2)}, u32[]{:S(2)}) collective-permute-start(bf16[4,2,128,128]{3,2,1,0:T(8,128)(2,1)S(1)} %dynamic-slice_bitcast_fusion), channel_id=1, source_target_pairs={{0,16},{16,0},{32,48},{48,32},{64,80},{80,64},{96,112},{112,96},{1... | collective-permute-start | bytes 786440 | tf_op jit(solution)/shard_map/ppermute | solution.py:23
  46.8 10.8 %collective-permute-start.6 = (bf16[4,128,128]{2,1,0:T(8,128)(2,1)S(1)}, bf16[4,128,128]{2,1,0:T(8,128)(2,1)S(1)}, u32[]{:S(2)}, u32[]{:S(2)}) collective-permute-start(bf16[4,128,128]{2,1,0:T(8,128)(2,1)S(1)} %pad_maximum_fusion.5), channel_id=1, source_target_pairs={{0,1},{1,0},{2,3},{3,2},{4,5},{5,4},{6,7},{7,6},{8,9},{9,8},{10,11... | collective-permute-start | bytes 393224 | tf_op jit(solution)/shard_map/ppermute | solution.py:23
  47.2 23.1 %collective-permute-start.7 = (bf16[4,128,128]{2,1,0:T(8,128)(2,1)S(1)}, bf16[4,128,128]{2,1,0:T(8,128)(2,1)S(1)}, u32[]{:S(2)}, u32[]{:S(2)}) collective-permute-start(bf16[4,128,128]{2,1,0:T(8,128)(2,1)S(1)} %pad_maximum_fusion.5), channel_id=1, source_target_pairs={{0,2},{1,3},{2,0},{3,1},{4,6},{5,7},{6,4},{7,5},{8,10},{9,11},{10,... | collective-permute-start | bytes 393224 | tf_op jit(solution)/shard_map/ppermute | solution.py:23
  50.3 27.0 %collective-permute-start.8 = (bf16[4,128,128]{2,1,0:T(8,128)(2,1)S(1)}, bf16[4,128,128]{2,1,0:T(8,128)(2,1)S(1)}, u32[]{:S(2)}, u32[]{:S(2)}) collective-permute-start(bf16[4,128,128]{2,1,0:T(8,128)(2,1)S(1)} %pad_maximum_fusion.5), channel_id=1, source_target_pairs={{0,3},{1,2},{2,1},{3,0},{4,7},{5,6},{6,5},{7,4},{8,11},{9,10},{10,... | collective-permute-start | bytes 393224 | tf_op jit(solution)/shard_map/ppermute | solution.py:23
  51.4 21.0 %collective-permute-start.16 = (bf16[4,2,128,128]{3,2,1,0:T(8,128)(2,1)S(1)}, bf16[4,2,128,128]{3,2,1,0:T(8,128)(2,1)S(1)}, u32[]{:S(2)}, u32[]{:S(2)}) collective-permute-start(bf16[4,2,128,128]{3,2,1,0:T(8,128)(2,1)S(1)} %bitcast_select_fusion), channel_id=1, source_target_pairs={{0,32},{16,48},{32,0},{48,16},{64,96},{80,112},{96,64},{112,80},{1... | collective-permute-start | bytes 786440 | tf_op jit(solution)/shard_map/ppermute | solution.py:23
  72.5 8.1 %collective-permute-start.17 = (bf16[8,128,128]{2,1,0:T(8,128)(2,1)S(1)}, bf16[8,128,128]{2,1,0:T(8,128)(2,1)S(1)}, u32[]{:S(2)}, u32[]{:S(2)}) collective-permute-start(bf16[8,128,128]{2,1,0:T(8,128)(2,1)S(1)} %bitcast.112), channel_id=1, source_target_pairs={{0,64},{16,80},{32,96},{48,112},{64,0},{80,16},{96,32},{112,48},{1... | collective-permute-start | bytes 786440 | tf_op jit(solution)/shard_map/ppermute | solution.py:23
  74.1 11.4 %collective-permute-start.18 = (bf16[8,128,128]{2,1,0:T(8,128)(2,1)S(1)}, bf16[8,128,128]{2,1,0:T(8,128)(2,1)S(1)}, u32[]{:S(2)}, u32[]{:S(2)}) collective-permute-start(bf16[8,128,128]{2,1,0:T(8,128)(2,1)S(1)} %bitcast.113), channel_id=1, source_target_pairs={{0,128},{16,144},{32,160},{48,176},{64,192},{80,208},{96,224},{112... | collective-permute-start | bytes 786440 | tf_op jit(solution)/shard_map/ppermute | solution.py:23
  77.0 11.0 %collective-permute-start.19 = (bf16[8,128,128]{2,1,0:T(8,128)(2,1)S(1)}, bf16[8,128,128]{2,1,0:T(8,128)(2,1)S(1)}, u32[]{:S(2)}, u32[]{:S(2)}) collective-permute-start(bf16[8,128,128]{2,1,0:T(8,128)(2,1)S(1)} %bitcast.114), channel_id=1, source_target_pairs={{0,192},{16,208},{32,224},{48,240},{64,128},{80,144},{96,160},{112... | collective-permute-start | bytes 786440 | tf_op jit(solution)/shard_map/ppermute | solution.py:23
  77.4 14.9 %collective-permute-start.9 = (bf16[16,128,128]{2,1,0:T(8,128)(2,1)S(1)}, bf16[16,128,128]{2,1,0:T(8,128)(2,1)S(1)}, u32[]{:S(2)}, u32[]{:S(2)}) collective-permute-start(bf16[16,128,128]{2,1,0:T(8,128)(2,1)S(1)} %get-tuple-element.43), channel_id=1, source_target_pairs={{0,4},{1,5},{2,6},{3,7},{4,0},{5,1},{6,2},{7,3},{8,12},{9,13},{10,... | collective-permute-start | bytes 1572872 | tf_op jit(solution)/shard_map/ppermute | solution.py:23
  78.1 21.2 %collective-permute-start.10 = (bf16[16,128,128]{2,1,0:T(8,128)(2,1)S(1)}, bf16[16,128,128]{2,1,0:T(8,128)(2,1)S(1)}, u32[]{:S(2)}, u32[]{:S(2)}) collective-permute-start(bf16[16,128,128]{2,1,0:T(8,128)(2,1)S(1)} %get-tuple-element.43), channel_id=1, source_target_pairs={{0,8},{1,9},{2,10},{3,11},{4,12},{5,13},{6,14},{7,15},{8,0},{9,1},... | collective-permute-start | bytes 1572872 | tf_op jit(solution)/shard_map/ppermute | solution.py:23
  80.6 20.4 %collective-permute-start.11 = (bf16[16,128,128]{2,1,0:T(8,128)(2,1)S(1)}, bf16[16,128,128]{2,1,0:T(8,128)(2,1)S(1)}, u32[]{:S(2)}, u32[]{:S(2)}) collective-permute-start(bf16[16,128,128]{2,1,0:T(8,128)(2,1)S(1)} %get-tuple-element.43), channel_id=1, source_target_pairs={{0,12},{1,13},{2,14},{3,15},{4,8},{5,9},{6,10},{7,11},{8,4},{9,5},... | collective-permute-start | bytes 1572872 | tf_op jit(solution)/shard_map/ppermute | solution.py:23
  88.2 13.0 %collective-permute-start.20 = (bf16[32,128,128]{2,1,0:T(8,128)(2,1)S(1)}, bf16[32,128,128]{2,1,0:T(8,128)(2,1)S(1)}, u32[]{:S(2)}, u32[]{:S(2)}) collective-permute-start(bf16[32,128,128]{2,1,0:T(8,128)(2,1)S(1)} %pad_maximum_fusion.1), channel_id=1, source_target_pairs={{0,16},{16,0},{32,48},{48,32},{64,80},{80,64},{96,112},{112,96},{1... | collective-permute-start | bytes 3145736 | tf_op jit(solution)/shard_map/ppermute | solution.py:23
  99.4 2.0 %copy-start = (bf16[1,1,32,128,128]{4,3,2,1,0:T(8,128)(2,1)S(1)}, bf16[1,1,32,128,128]{4,3,2,1,0:T(8,128)(2,1)}, u32[]{:S(2)}) copy-start(bf16[1,1,32,128,128]{4,3,2,1,0:T(8,128)(2,1)} %param.5) | copy-start | bytes 3145732
  99.4 2.0 %copy-start.1 = (s32[1,1,32]{2,1,0:T(1,128)S(1)}, s32[1,1,32]{2,1,0:T(1,128)}, u32[]{:S(2)}) copy-start(s32[1,1,32]{2,1,0:T(1,128)} %param.9) | copy-start | bytes 388
  102.2 7.6 %collective-permute-start.22 = (f32[8,128]{1,0:T(8,128)S(1)}, f32[8,128]{1,0:T(8,128)S(1)}, u32[]{:S(2)}, u32[]{:S(2)}) collective-permute-start(f32[8,128]{1,0:T(8,128)S(1)} %trace_part.1), channel_id=1, source_target_pairs={{0,32},{16,48},{32,0},{48,16},{64,96},{80,112},{96,64},{112,80},{1... | collective-permute-start | bytes 12296 | tf_op jit(solution)/shard_map/ppermute | solution.py:23
  102.3 7.5 %collective-permute-start.23 = (f32[8,128]{1,0:T(8,128)S(1)}, f32[8,128]{1,0:T(8,128)S(1)}, u32[]{:S(2)}, u32[]{:S(2)}) collective-permute-start(f32[8,128]{1,0:T(8,128)S(1)} %trace_part.1), channel_id=1, source_target_pairs={{0,48},{16,32},{32,16},{48,0},{64,112},{80,96},{96,80},{112,64},{1... | collective-permute-start | bytes 12296 | tf_op jit(solution)/shard_map/ppermute | solution.py:23
  102.4 7.4 %collective-permute-start.21 = (f32[8,128]{1,0:T(8,128)S(1)}, f32[8,128]{1,0:T(8,128)S(1)}, u32[]{:S(2)}, u32[]{:S(2)}) collective-permute-start(f32[8,128]{1,0:T(8,128)S(1)} %trace_part.1), channel_id=1, source_target_pairs={{0,16},{16,0},{32,48},{48,32},{64,80},{80,64},{96,112},{112,96},{1... | collective-permute-start | bytes 12296 | tf_op jit(solution)/shard_map/ppermute | solution.py:23
  109.8 13.5 %collective-permute-start.25 = (f32[8,128]{1,0:T(8,128)S(1)}, f32[8,128]{1,0:T(8,128)S(1)}, u32[]{:S(2)}, u32[]{:S(2)}) collective-permute-start(f32[8,128]{1,0:T(8,128)S(1)} %add_add_fusion.2), channel_id=1, source_target_pairs={{0,128},{16,144},{32,160},{48,176},{64,192},{80,208},{96,224},{112... | collective-permute-start | bytes 12296 | tf_op jit(solution)/shard_map/ppermute | solution.py:23
  111.7 13.1 %collective-permute-start.26 = (f32[8,128]{1,0:T(8,128)S(1)}, f32[8,128]{1,0:T(8,128)S(1)}, u32[]{:S(2)}, u32[]{:S(2)}) collective-permute-start(f32[8,128]{1,0:T(8,128)S(1)} %add_add_fusion.2), channel_id=1, source_target_pairs={{0,192},{16,208},{32,224},{48,240},{64,128},{80,144},{96,160},{112... | collective-permute-start | bytes 12296 | tf_op jit(solution)/shard_map/ppermute | solution.py:23
  123.3 3.6 %collective-permute-start.24 = (f32[8,128]{1,0:T(8,128)S(1)}, f32[8,128]{1,0:T(8,128)S(1)}, u32[]{:S(2)}, u32[]{:S(2)}) collective-permute-start(f32[8,128]{1,0:T(8,128)S(1)} %add_add_fusion.2), channel_id=1, source_target_pairs={{0,64},{16,80},{32,96},{48,112},{64,0},{80,16},{96,32},{112,48},{1... | collective-permute-start | bytes 12296 | tf_op jit(solution)/shard_map/ppermute | solution.py:23
  126.9 5.5 %collective-permute-start.28 = (f32[8,128]{1,0:T(8,128)S(1)}, f32[8,128]{1,0:T(8,128)S(1)}, u32[]{:S(2)}, u32[]{:S(2)}) collective-permute-start(f32[8,128]{1,0:T(8,128)S(1)} %add_add_fusion.1), channel_id=1, source_target_pairs={{0,2},{1,3},{2,0},{3,1},{4,6},{5,7},{6,4},{7,5},{8,10},{9,11},{10,... | collective-permute-start | bytes 12296 | tf_op jit(solution)/shard_map/ppermute | solution.py:23
  130.8 5.4 %collective-permute-start.29 = (f32[8,128]{1,0:T(8,128)S(1)}, f32[8,128]{1,0:T(8,128)S(1)}, u32[]{:S(2)}, u32[]{:S(2)}) collective-permute-start(f32[8,128]{1,0:T(8,128)S(1)} %add_add_fusion.1), channel_id=1, source_target_pairs={{0,3},{1,2},{2,1},{3,0},{4,7},{5,6},{6,5},{7,4},{8,11},{9,10},{10,... | collective-permute-start | bytes 12296 | tf_op jit(solution)/shard_map/ppermute | solution.py:23
  130.8 5.4 %collective-permute-start.27 = (f32[8,128]{1,0:T(8,128)S(1)}, f32[8,128]{1,0:T(8,128)S(1)}, u32[]{:S(2)}, u32[]{:S(2)}) collective-permute-start(f32[8,128]{1,0:T(8,128)S(1)} %add_add_fusion.1), channel_id=1, source_target_pairs={{0,1},{1,0},{2,3},{3,2},{4,5},{5,4},{6,7},{7,6},{8,9},{9,8},{10,11... | collective-permute-start | bytes 12296 | tf_op jit(solution)/shard_map/ppermute | solution.py:23
  136.2 22.9 %collective-permute-start.31 = (f32[8,128]{1,0:T(8,128)S(1)}, f32[8,128]{1,0:T(8,128)S(1)}, u32[]{:S(2)}, u32[]{:S(2)}) collective-permute-start(f32[8,128]{1,0:T(8,128)S(1)} %add_add_fusion), channel_id=1, source_target_pairs={{0,8},{1,9},{2,10},{3,11},{4,12},{5,13},{6,14},{7,15},{8,0},{9,1},... | collective-permute-start | bytes 12296 | tf_op jit(solution)/shard_map/ppermute | solution.py:23
  137.4 21.8 %collective-permute-start.32 = (f32[8,128]{1,0:T(8,128)S(1)}, f32[8,128]{1,0:T(8,128)S(1)}, u32[]{:S(2)}, u32[]{:S(2)}) collective-permute-start(f32[8,128]{1,0:T(8,128)S(1)} %add_add_fusion), channel_id=1, source_target_pairs={{0,12},{1,13},{2,14},{3,15},{4,8},{5,9},{6,10},{7,11},{8,4},{9,5},... | collective-permute-start | bytes 12296 | tf_op jit(solution)/shard_map/ppermute | solution.py:23
  138.2 21.0 %collective-permute-start.30 = (f32[8,128]{1,0:T(8,128)S(1)}, f32[8,128]{1,0:T(8,128)S(1)}, u32[]{:S(2)}, u32[]{:S(2)}) collective-permute-start(f32[8,128]{1,0:T(8,128)S(1)} %add_add_fusion), channel_id=1, source_target_pairs={{0,4},{1,5},{2,6},{3,7},{4,0},{5,1},{6,2},{7,3},{8,12},{9,13},{10,... | collective-permute-start | bytes 12296 | tf_op jit(solution)/shard_map/ppermute | solution.py:23

commit v2 on v0

v2 whole, which is shorter than its diff:
```python
import functools

import jax
import jax.numpy as jnp
from jax import lax
from jax.experimental import pallas as pl
from jax.experimental.pallas import tpu as pltpu
from jax.sharding import PartitionSpec as P

BS = 128
WIN = 4
NO = 32
TASKS = 1024
GROUP = 4
UNROLL = 8
NGROUP = 288
ZERO = 64
FIRST = 8
SCALE = 1.0 / (32 * 4 * 128) ** 0.5


def swap(value, axis, bit):
    return lax.ppermute(value, axis, [(i, i ^ bit) for i in range(16)])


def pick(stack, index):
    return lax.dynamic_index_in_dim(stack, index, 0, keepdims=False)


def choose(parts, index):
    mask_shape = (WIN,) + (1,) * (parts[0].ndim - 1)
    out = jnp.broadcast_to(parts[0], (WIN,) + parts[0].shape[1:])
    for d in range(1, len(parts)):
        out = jnp.where((index == d).reshape(mask_shape), parts[d], out)
    return out


def scatter_columns(by_x, panels, x):
    parts = [pick(by_x, x)] + [swap(pick(by_x, x ^ d), "col", 4 * d) for d in (1, 2, 3)]
    index = ((x ^ (panels >> 3)) << 1) | (panels & 1)
    return choose([part[None, :, j] for part in parts for j in range(2)], index)


def scatter_rows(by_y, panels, y):
    parts = [pick(by_y, y)] + [swap(pick(by_y, y ^ d), "row", 4 * d) for d in (1, 2, 3)]
    index = ((y ^ (panels >> 3)) << 1) | (panels & 1)
    return choose([part[None, i] for part in parts for i in range(2)], index)


def panels_to_all(own, panels):
    me_r, me_c = lax.axis_index("row"), lax.axis_index("col")
    x, z = me_c >> 2, me_c & 3
    y, zh, core = me_r >> 2, (me_r >> 1) & 1, me_r & 1
    by_q = jnp.moveaxis(own.reshape(2, 2, 4, 2, BS, BS), 2, 0)
    mine = scatter_columns(by_q, panels, x).reshape(WIN, 4, BS, BS)
    by_j = scatter_rows(by_q, panels, y)

    by_z = jnp.moveaxis(mine, 1, 0)
    parts = [pick(by_z, z)] + [swap(pick(by_z, z ^ d), "col", d) for d in (1, 2, 3)]
    held = choose(parts, z ^ ((panels >> 1) & 3))

    by_j = jnp.moveaxis(by_j, 1, 0)
    got = swap(pick(by_j, 1 - core), "row", 1)
    half = choose([pick(by_j, core), got], ((panels >> 1) & 1) ^ core)

    line = jnp.concatenate([held] + [swap(held, "col", d) for d in (1, 2, 3)])
    line, half = lax.optimization_barrier((line, half))
    columns = [line] + [swap(line, "col", 4 * d) for d in (1, 2, 3)]

    half = choose([half, swap(half, "row", 2)], ((panels >> 2) & 1) ^ zh).reshape(WIN * 2, BS, BS)
    half, columns[1], columns[3] = lax.optimization_barrier((half, columns[1], columns[3]))
    line = jnp.concatenate([half] + [swap(half, "row", 4 * d) for d in (1, 2, 3)])
    return columns, [line, swap(line, "row", 1)]


def plan(tasks, coords):
    me_r, me_c = lax.axis_index("row"), lax.axis_index("col")
    x, z = me_c >> 2, me_c & 3
    y, core = me_r >> 2, me_r & 1
    outs = tasks[:, 0].reshape(TASKS)
    left = tasks[:, 1].reshape(TASKS)
    right = tasks[:, 2].reshape(TASKS)
    step = jnp.arange(TASKS, dtype=jnp.int32) >> 8
    left = ((x ^ ((left & 7) >> 1)) << 4) + ((z ^ (((left >> 3) << 1) + (left & 1))) << 2) + step
    right = ((core ^ (right >> 3)) << 5) + ((y ^ ((right & 7) >> 1)) << 3) + (step << 1) + (right & 1)
    slots = jnp.arange(NO, dtype=jnp.int32)
    hot = outs[:, None] == slots[None, :]
    hot_bf = hot.astype(jnp.bfloat16)
    ids = jnp.arange(TASKS, dtype=jnp.int32)
    earlier = (ids[None, :] < ids[:, None]).astype(jnp.bfloat16)
    seen = jnp.dot(earlier, hot_bf, preferred_element_type=jnp.float32).astype(jnp.int32)
    counts = jnp.sum(hot.astype(jnp.int32), axis=0)
    groups = (counts + GROUP - 1) >> 2
    diag = coords[0] == coords[1]
    order = jnp.where(diag, 0, NO) + slots
    before = order[None, :] < order[:, None]
    starts = jnp.sum(jnp.where(before, groups[None, :], 0), axis=1)
    rank = jnp.sum(before.astype(jnp.int32), axis=1)
    place = jnp.sum(jnp.where(hot, seen + GROUP * starts[None, :], 0), axis=1)
    place = jnp.where(outs >= 0, place, -1)
    spots = jnp.arange(NGROUP * GROUP, dtype=jnp.int32)
    move = (spots[:, None] == place[None, :]).astype(jnp.bfloat16)
    pair = jnp.stack([left - ZERO, right], axis=1).astype(jnp.bfloat16)
    lists = jnp.dot(move, pair, preferred_element_type=jnp.float32).astype(jnp.int32)
    gid = jnp.arange(NGROUP, dtype=jnp.int32)[:, None]
    target = jnp.sum((gid >= (starts + groups)[None, :]).astype(jnp.int32), axis=1)
    slot_of = jnp.sum(jnp.where(rank[:, None] == slots[None, :], slots[:, None], 0), axis=0)
    limits = jnp.array([0, FIRST, NO], jnp.int32)
    bounds = jnp.sum(jnp.where(rank[None, :] < limits[:, None], groups[None, :], 0), axis=1)
    return lists[:, 0] + ZERO, lists[:, 1], target, bounds, slot_of, diag.astype(jnp.int32)


def group_product(left_ref, right_ref, lhs, rhs, group):
    spots = [group * GROUP + k for k in range(GROUP)]
    a = jnp.concatenate([lhs[left_ref[t]] for t in spots], axis=1)
    b = jnp.concatenate([rhs[right_ref[t]] for t in spots], axis=0)
    return jnp.dot(a, b, preferred_element_type=jnp.float32)


def accumulate(part, base, count, left_ref, right_ref, target_ref, bounds_ref, lhs, rhs, acc):
    acc[...] = jnp.zeros_like(acc)
    first, last = bounds_ref[part], bounds_ref[part + 1]

    def some(it, carry):
        for u in range(UNROLL):
            g = first + it * UNROLL + u
            product = group_product(left_ref, right_ref, lhs, rhs, g)
            acc[jnp.minimum(target_ref[g] - base, count)] += product
        return carry

    lax.fori_loop(0, (last - first + UNROLL - 1) >> 3, some, 0)


def first_kernel(left_ref, right_ref, target_ref, bounds_ref, slot_ref, branch_ref, diag_ref, lhs, rhs, own, out, sums, acc, old, new):
    old[...] = jnp.zeros_like(old)
    new[...] = jnp.zeros_like(new)
    accumulate(0, 0, FIRST, left_ref, right_ref, target_ref, bounds_ref, lhs, rhs, acc)

    def finish(i, carry):
        o = slot_ref[i]
        product = acc[i]
        block = own[o].astype(jnp.float32)
        value = jnp.where(branch_ref[o] == 0, product, 2.0 * block - product)
        out[i] = value.astype(jnp.bfloat16)

        @pl.when(diag_ref[o] > 0)
        def _():
            old[...] += block
            new[...] += value

        return carry

    lax.fori_loop(0, FIRST, finish, 0)
    shape = (BS, BS)
    eye = lax.broadcasted_iota(jnp.int32, shape, 0) == lax.broadcasted_iota(jnp.int32, shape, 1)
    sums[...] = jnp.zeros_like(sums)
    sums[0:1, :] = jnp.sum(jnp.where(eye, old[...], 0.0), axis=0, keepdims=True)
    sums[1:2, :] = jnp.sum(jnp.where(eye, new[...], 0.0), axis=0, keepdims=True)


def rest_kernel(left_ref, right_ref, target_ref, bounds_ref, slot_ref, branch_ref, diag_ref, lhs, rhs, own, filled, out, acc):
    accumulate(1, FIRST, NO - FIRST, left_ref, right_ref, target_ref, bounds_ref, lhs, rhs, acc)

    def copy(i, carry):
        out[slot_ref[i]] = filled[i]
        return carry

    lax.fori_loop(0, FIRST, copy, 0)

    def finish(i, carry):
        o = slot_ref[FIRST + i]
        product = acc[i]
        value = jnp.where(branch_ref[o] == 0, product, 2.0 * own[o].astype(jnp.float32) - product)
        out[o] = value.astype(jnp.bfloat16)
        return carry

    lax.fori_loop(0, NO - FIRST, finish, 0)


def products(kernel, count, out_shape, scratch, scalars, arrays):
    smem = pl.BlockSpec(memory_space=pltpu.SMEM)
    vmem = pl.BlockSpec(memory_space=pltpu.VMEM)
    return pl.pallas_call(
        kernel,
        out_shape=out_shape,
        in_specs=[smem] * len(scalars) + [vmem] * len(arrays),
        out_specs=jax.tree.map(lambda _: vmem, out_shape),
        scratch_shapes=[pltpu.VMEM((n, BS, BS) if n else (BS, BS), jnp.float32) for n in scratch],
        compiler_params=pltpu.CompilerParams(vmem_limit_bytes=16 << 20),
        cost_estimate=pl.CostEstimate(flops=count << 27, bytes_accessed=8 << 20, transcendentals=0),
        name="block_products",
    )(*scalars, *arrays)


def body(p_blocks, coords, tasks, window_panels, branch):
    own = p_blocks[0, 0]
    left, right, target, bounds, slot_of, diag = plan(tasks[0, 0], coords[0, 0])
    columns, rows = panels_to_all(own, window_panels)
    lhs = jnp.concatenate(columns + [jnp.zeros((1, BS, BS), jnp.bfloat16)])
    arrays = (lhs, jnp.concatenate(rows), own)
    scalars = (left, right, target, bounds, slot_of, branch[0, 0], diag)
    shapes = (jax.ShapeDtypeStruct((FIRST, BS, BS), jnp.bfloat16), jax.ShapeDtypeStruct((8, BS), jnp.float32))
    filled, value = products(first_kernel, FIRST, shapes, (FIRST + 1, 0, 0), scalars, arrays)
    for axis, low, high in (("row", 1, 2), ("row", 4, 8), ("col", 1, 2)):
        one, two, three = (swap(value, axis, b) for b in (low, high, low + high))
        value = (value + one) + (two + three)
    value, filled = lax.optimization_barrier((value, filled))
    one, two, three = (swap(value, "col", b) for b in (4, 8, 12))
    shapes = jax.ShapeDtypeStruct((NO, BS, BS), jnp.bfloat16)
    out = products(rest_kernel, NO - FIRST, shapes, (NO - FIRST + 1,), scalars, arrays + (filled,))
    value = (value + one) + (two + three)
    traces = jnp.sum(value, axis=1)[:2] * SCALE
    return out[None, None], traces


def solution(mesh):
    in_specs = (
        P("row", "col", None, None, None),
        P("row", "col", None, None),
        P("row", "col", None, None, None),
        P(),
        P("row", "col", None),
    )
    out_specs = (P("row", "col", None, None, None), P())
    return jax.shard_map(body, mesh=mesh, in_specs=in_specs, out_specs=out_specs, check_vma=False)
```

time: 844 us -> 128 us (0.15); the launches traced: 832 us -> 127 us
  waiting for transfers between devices: 363 us -> 48.8 us
  other arithmetic: 207 us -> 2.52 us
  local copies, waits for them, and re-layouts: 85 us -> 3.46 us
  blocking collectives: 81.2 us -> 0 us
  matrix products: 69.3 us -> 1.41 us
  starting transfers between devices: 0.08 us -> 55.6 us
  between operations: 24.6 us -> 1.14 us
  Pallas kernels: 0 us -> 14.4 us
    psum x2 -> x0, waiting for transfers between devices: 363 us -> none  [the longest x1 193 us: body(): row_panel = lax.psum(row_term.astype(jnp.bfloat16), 'row')]
    scatter-add x16 -> x0, other arithmetic: 194 us -> none  [one_block(): return running.at[target].add(flat_prods, mode='drop')]
    psum x1 -> x0, blocking collectives: 81.2 us -> none  [body(): new_total = lax.psum(new_local, ('row', 'col'))]
    gather x34 -> x0, local copies, waits for them, and re-layouts: 70.5 us -> none  [the longest x16 43.1 us: one_block(): left_blocks = jnp.take(col_panel, piece[1], axis=0)]
    dot_general x16 -> x2, matrix products: 69.3 us -> 1.41 us  [the longest x1 0.87 us: plan(): jnp.dot(move, pair, preferred_element_type=jnp.float32).astype(jnp.int32)]
    ppermute x0 -> x33, starting transfers between devices: none -> 55.6 us  [swap(): return lax.ppermute(value, axis, [(i, i ^ bit) for i in range(16)])]
    ppermute x0 -> x33, waiting for transfers between devices: none -> 48.8 us  [swap(): return lax.ppermute(value, axis, [(i, i ^ bit) for i in range(16)])]
    pallas_call x0 -> x2, Pallas kernels: none -> 14.4 us  [products(): pl.pallas_call(kernel, out_shape=out_shape, in_specs=[smem] * len(scalars...]
  transfers between devices with their start and end apart: 2 -> 33, of which waited for: 2 -> 21; matrix products, arithmetic and copies ran while one was open for 1% -> 4% of each run, Pallas kernels for 0% -> 8%
where the time goes in v2:
time: 128 us; the launch traced here: 127 us
  starting transfers between devices  55.6 us (43%)
  waiting for transfers between devices  48.8 us (38%)
  Pallas kernels  14.4 us (11%)
  local copies, waits for them, and re-layouts  3.46 us (3%)
  other arithmetic  2.52 us (2%)
  matrix products  1.41 us (1%)
    ppermute x33, starting transfers between devices, swap(): return lax.ppermute(value, axis, [(i, i ^ bit) for i in range(16)])  55.6 us
    ppermute x33, waiting for transfers between devices, swap(): return lax.ppermute(value, axis, [(i, i ^ bit) for i in range(16)])  48.8 us
    pallas_call x2, Pallas kernels, products(): pl.pallas_call(kernel, out_shape=out_shape, in_specs=[smem] * len(scalars...  14.4 us
  transfers between devices with their start and end apart: 33, of which 21 were waited for; matrix products, arithmetic and copies ran while one was open for 4% of the time, Pallas kernels for 8%

profile of v2, /device:TPU:2, one launch (start us, length us, event | category | flops | bytes accessed | tf_op | source)
XLA Modules:
  0.0 127.3 jit_solution(18226547578581525002)
XLA Ops:
  0.7 1.7 %dynamic-slice_bitcast_fusion.4 = (bf16[2,2,2,128,128]{4,3,2,1,0:T(8,128)(2,1)S(1)}, bf16[1,2,2,2,128,128]{5,4,3,2,1,0:T(8,128)(2,1)S(1)}, bf16[2,2,2,128,128]{4...) fusion(bf16[2,2,4,2,128,128]{5,4,3,2,1,0:T(8,128)(2,1)} %bitcas, ...), kind=kLoop, calls=%fused_computation.19 | loop fusion | bytes 4194336 | tf_op jit(solution)/shard_map/jit(dynamic_index_in_dim)/squeeze | solution.py:27
  2.4 2.3 %collective-permute-start.2 = (bf16[2,2,2,128,128]{4,3,2,1,0:T(8,128)(2,1)S(1)}, bf16[2,2,2,128,128]{4,3,2,1,0:T(8,128)(2,1)}, u32[]{:S(2)}, u32[]{:S(2)}) collective-permute-start(bf16[2,2,2,128,128]{4,3,2,1,0:T(8,128)(2,1)S(1)} %get-tuple-element.35), channel_id=1, source_target_pairs={{0,4},{1,5},{2,6},{3,7},{4,0},{5,1},{6,2},{7,3},{8,12},{9,13},{10,... | collective-permute-start | bytes 786440 | tf_op jit(solution)/shard_map/ppermute | solution.py:23
  4.8 0.7 collective-permute-start.1
  5.5 0.9 collective-permute-start
  6.3 1.2 collective-permute-start.11
  7.6 2.9 %collective-permute-start.10 = (bf16[2,2,2,128,128]{4,3,2,1,0:T(8,128)(2,1)S(1)}, bf16[2,2,2,128,128]{4,3,2,1,0:T(8,128)(2,1)S(1)}, u32[]{:S(2)}, u32[]{:S(2)}) collective-permute-start(bf16[2,2,2,128,128]{4,3,2,1,0:T(8,128)(2,1)S(1)} %get-tuple-element.33), channel_id=1, source_target_pairs={{0,128},{16,144},{32,160},{48,176},{64,192},{80,208},{96,224},{112... | collective-permute-start | bytes 786440 | tf_op jit(solution)/shard_map/ppermute | solution.py:23
  10.8 0.5 fusion.7
  11.6 0.4 collective-permute-done.2
  12.1 2.8 %collective-permute-start.9 = (bf16[2,2,2,128,128]{4,3,2,1,0:T(8,128)(2,1)S(1)}, bf16[2,2,2,128,128]{4,3,2,1,0:T(8,128)(2,1)S(1)}, u32[]{:S(2)}, u32[]{:S(2)}) collective-permute-start(bf16[2,2,2,128,128]{4,3,2,1,0:T(8,128)(2,1)S(1)} %get-tuple-element.30), channel_id=1, source_target_pairs={{0,192},{16,208},{32,224},{48,240},{64,128},{80,144},{96,160},{112... | collective-permute-start | bytes 786440 | tf_op jit(solution)/shard_map/ppermute | solution.py:23
  14.8 1.0 fusion.21
  15.8 1.4 %collective-permute-done.1 = bf16[2,2,2,128,128]{4,3,2,1,0:T(8,128)(2,1)S(1)} collective-permute-done((bf16[2,2,2,128,128]{4,3,2,1,0:T(8,128)(2,1)S(1)}, bf16[2,2,2,128,128]{4,3,2,1,0:T(8,128)(2,1)S(1)}, u32[]{:S(2)}, u32[]{:S(2)}) %collective-permute-start.1) | collective-permute-done | bytes 262176 | tf_op jit(solution)/shard_map/ppermute | solution.py:23
  17.2 1.3 %collective-permute-done = bf16[2,2,2,128,128]{4,3,2,1,0:T(8,128)(2,1)S(1)} collective-permute-done((bf16[2,2,2,128,128]{4,3,2,1,0:T(8,128)(2,1)S(1)}, bf16[2,2,2,128,128]{4,3,2,1,0:T(8,128)(2,1)S(1)}, u32[]{:S(2)}, u32[]{:S(2)}) %collective-permute-start) | collective-permute-done | bytes 262176 | tf_op jit(solution)/shard_map/ppermute | solution.py:23
  18.9 4.7 %collective-permute-start.3 = (bf16[4,128,128]{2,1,0:T(8,128)(2,1)S(1)}, bf16[4,128,128]{2,1,0:T(8,128)(2,1)S(1)}, u32[]{:S(2)}, u32[]{:S(2)}) collective-permute-start(bf16[4,128,128]{2,1,0:T(8,128)(2,1)S(1)} %get-tuple-element.40), channel_id=1, source_target_pairs={{0,3},{1,2},{2,1},{3,0},{4,7},{5,6},{6,5},{7,4},{8,11},{9,10},{10,... | collective-permute-start | bytes 393224 | tf_op jit(solution)/shard_map/ppermute | solution.py:23
  23.6 0.7 collective-permute-start.5
  24.3 0.7 collective-permute-done.9
  25.5 2.1 %collective-permute-done.3 = bf16[4,128,128]{2,1,0:T(8,128)(2,1)S(1)} collective-permute-done((bf16[4,128,128]{2,1,0:T(8,128)(2,1)S(1)}, bf16[4,128,128]{2,1,0:T(8,128)(2,1)S(1)}, u32[]{:S(2)}, u32[]{:S(2)}) %collective-permute-start.3) | collective-permute-done | bytes 131104 | tf_op jit(solution)/shard_map/ppermute | solution.py:23
  27.6 4.9 %collective-permute-done.4 = bf16[4,128,128]{2,1,0:T(8,128)(2,1)S(1)} collective-permute-done((bf16[4,128,128]{2,1,0:T(8,128)(2,1)S(1)}, bf16[4,128,128]{2,1,0:T(8,128)(2,1)S(1)}, u32[]{:S(2)}, u32[]{:S(2)}) %collective-permute-start.4) | collective-permute-done | bytes 131104 | tf_op jit(solution)/shard_map/ppermute | solution.py:23
  32.6 2.8 %collective-permute-start.8 = (bf16[4,128,128]{2,1,0:T(8,128)(2,1)S(1)}, bf16[4,128,128]{2,1,0:T(8,128)(2,1)S(1)}, u32[]{:S(2)}, u32[]{:S(2)}) collective-permute-start(bf16[4,128,128]{2,1,0:T(8,128)(2,1)S(1)} %fusion.9), channel_id=1, source_target_pairs={{0,3},{1,2},{2,1},{3,0},{4,7},{5,6},{6,5},{7,4},{8,11},{9,10},{10,... | collective-permute-start | bytes 393224 | tf_op jit(solution)/shard_map/ppermute | solution.py:23
  35.4 1.6 %collective-permute-start.6 = (bf16[4,128,128]{2,1,0:T(8,128)(2,1)S(1)}, bf16[4,128,128]{2,1,0:T(8,128)(2,1)S(1)}, u32[]{:S(2)}, u32[]{:S(2)}) collective-permute-start(bf16[4,128,128]{2,1,0:T(8,128)(2,1)S(1)} %fusion.9), channel_id=1, source_target_pairs={{0,1},{1,0},{2,3},{3,2},{4,5},{5,4},{6,7},{7,6},{8,9},{9,8},{10,11... | collective-permute-start | bytes 393224 | tf_op jit(solution)/shard_map/ppermute | solution.py:23
  37.1 3.8 %collective-permute-done.8 = bf16[4,128,128]{2,1,0:T(8,128)(2,1)S(1)} collective-permute-done((bf16[4,128,128]{2,1,0:T(8,128)(2,1)S(1)}, bf16[4,128,128]{2,1,0:T(8,128)(2,1)S(1)}, u32[]{:S(2)}, u32[]{:S(2)}) %collective-permute-start.8) | collective-permute-done | bytes 131104 | tf_op jit(solution)/shard_map/ppermute | solution.py:23
  40.9 3.4 %collective-permute-done.7 = bf16[4,128,128]{2,1,0:T(8,128)(2,1)S(1)} collective-permute-done((bf16[4,128,128]{2,1,0:T(8,128)(2,1)S(1)}, bf16[4,128,128]{2,1,0:T(8,128)(2,1)S(1)}, u32[]{:S(2)}, u32[]{:S(2)}) %collective-permute-start.7) | collective-permute-done | bytes 131104 | tf_op jit(solution)/shard_map/ppermute | solution.py:23
  44.5 3.9 %collective-permute-start.14 = (bf16[16,128,128]{2,1,0:T(8,128)(2,1)S(1)}, bf16[16,128,128]{2,1,0:T(8,128)(2,1)S(1)}, u32[]{:S(2)}, u32[]{:S(2)}) collective-permute-start(bf16[16,128,128]{2,1,0:T(8,128)(2,1)S(1)} %pad_maximum_fusion.1), channel_id=1, source_target_pairs={{0,4},{1,5},{2,6},{3,7},{4,0},{5,1},{6,2},{7,3},{8,12},{9,13},{10,... | collective-permute-start | bytes 1572872 | tf_op jit(solution)/shard_map/ppermute | solution.py:23
  48.4 5.9 %collective-permute-start.13 = (bf16[4,2,128,128]{3,2,1,0:T(8,128)(2,1)S(1)}, bf16[4,2,128,128]{3,2,1,0:T(8,128)(2,1)S(1)}, u32[]{:S(2)}, u32[]{:S(2)}) collective-permute-start(bf16[4,2,128,128]{3,2,1,0:T(8,128)(2,1)S(1)} %bitcast_select_fusion), channel_id=1, source_target_pairs={{0,32},{16,48},{32,0},{48,16},{64,96},{80,112},{96,64},{112,80},{1... | collective-permute-start | bytes 786440 | tf_op jit(solution)/shard_map/ppermute | solution.py:23
  54.4 0.9 fusion.3
  55.3 10.3 %collective-permute-done.13 = bf16[4,2,128,128]{3,2,1,0:T(8,128)(2,1)S(1)} collective-permute-done((bf16[4,2,128,128]{3,2,1,0:T(8,128)(2,1)S(1)}, bf16[4,2,128,128]{3,2,1,0:T(8,128)(2,1)S(1)}, u32[]{:S(2)}, u32[]{:S(2)}) %collective-permute-start.13) | collective-permute-done | bytes 262176 | tf_op jit(solution)/shard_map/ppermute | solution.py:23
  65.7 1.6 %collective-permute-start.17 = (bf16[8,128,128]{2,1,0:T(8,128)(2,1)S(1)}, bf16[8,128,128]{2,1,0:T(8,128)(2,1)S(1)}, u32[]{:S(2)}, u32[]{:S(2)}) collective-permute-start(bf16[8,128,128]{2,1,0:T(8,128)(2,1)S(1)} %bitcast.90), channel_id=1, source_target_pairs={{0,64},{16,80},{32,96},{48,112},{64,0},{80,16},{96,32},{112,48},{1... | collective-permute-start | bytes 786440 | tf_op jit(solution)/shard_map/ppermute | solution.py:23
  67.4 2.9 %collective-permute-start.18 = (bf16[8,128,128]{2,1,0:T(8,128)(2,1)S(1)}, bf16[8,128,128]{2,1,0:T(8,128)(2,1)S(1)}, u32[]{:S(2)}, u32[]{:S(2)}) collective-permute-start(bf16[8,128,128]{2,1,0:T(8,128)(2,1)S(1)} %bitcast.91), channel_id=1, source_target_pairs={{0,128},{16,144},{32,160},{48,176},{64,192},{80,208},{96,224},{112... | collective-permute-start | bytes 786440 | tf_op jit(solution)/shard_map/ppermute | solution.py:23
  70.6 2.2 %collective-permute-start.16 = (bf16[16,128,128]{2,1,0:T(8,128)(2,1)S(1)}, bf16[16,128,128]{2,1,0:T(8,128)(2,1)S(1)}, u32[]{:S(2)}, u32[]{:S(2)}) collective-permute-start(bf16[16,128,128]{2,1,0:T(8,128)(2,1)S(1)} %pad_maximum_fusion.1), channel_id=1, source_target_pairs={{0,8},{1,9},{2,10},{3,11},{4,12},{5,13},{6,14},{7,15},{8,0},{9,1},... | collective-permute-start | bytes 1572872 | tf_op jit(solution)/shard_map/ppermute | solution.py:23
  73.1 5.0 %collective-permute-done.18 = bf16[8,128,128]{2,1,0:T(8,128)(2,1)S(1)} collective-permute-done((bf16[8,128,128]{2,1,0:T(8,128)(2,1)S(1)}, bf16[8,128,128]{2,1,0:T(8,128)(2,1)S(1)}, u32[]{:S(2)}, u32[]{:S(2)}) %collective-permute-start.18) | collective-permute-done | bytes 262176 | tf_op jit(solution)/shard_map/ppermute | solution.py:23
  78.0 2.7 %collective-permute-done.19 = bf16[8,128,128]{2,1,0:T(8,128)(2,1)S(1)} collective-permute-done((bf16[8,128,128]{2,1,0:T(8,128)(2,1)S(1)}, bf16[8,128,128]{2,1,0:T(8,128)(2,1)S(1)}, u32[]{:S(2)}, u32[]{:S(2)}) %collective-permute-start.19) | collective-permute-done | bytes 262176 | tf_op jit(solution)/shard_map/ppermute | solution.py:23
  81.7 1.9 %collective-permute-done.20 = bf16[32,128,128]{2,1,0:T(8,128)(2,1)S(1)} collective-permute-done((bf16[32,128,128]{2,1,0:T(8,128)(2,1)S(1)}, bf16[32,128,128]{2,1,0:T(8,128)(2,1)S(1)}, u32[]{:S(2)}, u32[]{:S(2)}) %collective-permute-start.20) | collective-permute-done | bytes 1048608 | tf_op jit(solution)/shard_map/ppermute | solution.py:23
  83.7 3.7 %block_products.2 = (bf16[8,128,128]{2,1,0:T(8,128)(2,1)S(1)}, f32[8,128]{1,0:T(8,128)S(1)}) custom-call(s32[1152]{0:T(1024)S(1)} %get-tuple-element.21.left_ref, s32[1152]{0:T(1024)S(1)} %get-tuple-element.20.right_ref, s32[288]{0:T(512)S(1)} %convert_reduce_fusion.1.target_ref, s32[3]{0:T(128)S(1)} %select_reduce_fusion.1.bounds_ref, ...), custom_call_target="tpu_custom_call" | custom-call | flops 1073741824 | bytes 8388608 | tf_op jit(solution)/shard_map/block_products/pallas_call | solution.py:183
  87.4 5.1 %collective-permute-start.22 = (f32[8,128]{1,0:T(8,128)S(1)}, f32[8,128]{1,0:T(8,128)S(1)}, u32[]{:S(2)}, u32[]{:S(2)}) collective-permute-start(f32[8,128]{1,0:T(8,128)S(1)} %get-tuple-element.16), channel_id=1, source_target_pairs={{0,32},{16,48},{32,0},{48,16},{64,96},{80,112},{96,64},{112,80},{1... | collective-permute-start | bytes 12296 | tf_op jit(solution)/shard_map/ppermute | solution.py:23
  92.5 0.8 collective-permute-start.23
  93.5 1.5 %collective-permute-done.22 = f32[8,128]{1,0:T(8,128)S(1)} collective-permute-done((f32[8,128]{1,0:T(8,128)S(1)}, f32[8,128]{1,0:T(8,128)S(1)}, u32[]{:S(2)}, u32[]{:S(2)}) %collective-permute-start.22) | collective-permute-done | bytes 4128 | tf_op jit(solution)/shard_map/ppermute | solution.py:23
  95.0 4.4 %collective-permute-done.23 = f32[8,128]{1,0:T(8,128)S(1)} collective-permute-done((f32[8,128]{1,0:T(8,128)S(1)}, f32[8,128]{1,0:T(8,128)S(1)}, u32[]{:S(2)}, u32[]{:S(2)}) %collective-permute-start.23) | collective-permute-done | bytes 4128 | tf_op jit(solution)/shard_map/ppermute | solution.py:23
  99.5 0.8 collective-permute-start.25
  100.3 1.6 %collective-permute-start.26 = (f32[8,128]{1,0:T(8,128)S(1)}, f32[8,128]{1,0:T(8,128)S(1)}, u32[]{:S(2)}, u32[]{:S(2)}) collective-permute-start(f32[8,128]{1,0:T(8,128)S(1)} %add_add_fusion.2), channel_id=1, source_target_pairs={{0,192},{16,208},{32,224},{48,240},{64,128},{80,144},{96,160},{112... | collective-permute-start | bytes 12296 | tf_op jit(solution)/shard_map/ppermute | solution.py:23
  101.9 1.2 collective-permute-start.24
  103.1 1.6 %collective-permute-done.25 = f32[8,128]{1,0:T(8,128)S(1)} collective-permute-done((f32[8,128]{1,0:T(8,128)S(1)}, f32[8,128]{1,0:T(8,128)S(1)}, u32[]{:S(2)}, u32[]{:S(2)}) %collective-permute-start.25) | collective-permute-done | bytes 4128 | tf_op jit(solution)/shard_map/ppermute | solution.py:23
  105.5 2.1 %collective-permute-start.29 = (f32[8,128]{1,0:T(8,128)S(1)}, f32[8,128]{1,0:T(8,128)S(1)}, u32[]{:S(2)}, u32[]{:S(2)}) collective-permute-start(f32[8,128]{1,0:T(8,128)S(1)} %add_add_fusion.1), channel_id=1, source_target_pairs={{0,3},{1,2},{2,1},{3,0},{4,7},{5,6},{6,5},{7,4},{8,11},{9,10},{10,... | collective-permute-start | bytes 12296 | tf_op jit(solution)/shard_map/ppermute | solution.py:23
  107.6 1.3 %collective-permute-start.27 = (f32[8,128]{1,0:T(8,128)S(1)}, f32[8,128]{1,0:T(8,128)S(1)}, u32[]{:S(2)}, u32[]{:S(2)}) collective-permute-start(f32[8,128]{1,0:T(8,128)S(1)} %add_add_fusion.1), channel_id=1, source_target_pairs={{0,1},{1,0},{2,3},{3,2},{4,5},{5,4},{6,7},{7,6},{8,9},{9,8},{10,11... | collective-permute-start | bytes 12296 | tf_op jit(solution)/shard_map/ppermute | solution.py:23
  109.0 1.0 collective-permute-done.28
  110.0 1.0 collective-permute-done.29
  111.2 2.2 %collective-permute-start.31 = (f32[8,128]{1,0:T(8,128)S(1)}, f32[8,128]{1,0:T(8,128)S(1)}, u32[]{:S(2)}, u32[]{:S(2)}) collective-permute-start(f32[8,128]{1,0:T(8,128)S(1)} %add_add_fusion), channel_id=1, source_target_pairs={{0,8},{1,9},{2,10},{3,11},{4,12},{5,13},{6,14},{7,15},{8,0},{9,1},... | collective-permute-start | bytes 12296 | tf_op jit(solution)/shard_map/ppermute | solution.py:23
  113.7 2.3 %collective-permute-start.30 = (f32[8,128]{1,0:T(8,128)S(1)}, f32[8,128]{1,0:T(8,128)S(1)}, u32[]{:S(2)}, u32[]{:S(2)}) collective-permute-start(f32[8,128]{1,0:T(8,128)S(1)} %add_add_fusion), channel_id=1, source_target_pairs={{0,4},{1,5},{2,6},{3,7},{4,0},{5,1},{6,2},{7,3},{8,12},{9,13},{10,... | collective-permute-start | bytes 12296 | tf_op jit(solution)/shard_map/ppermute | solution.py:23
  115.9 10.7 %block_products.3 = bf16[32,128,128]{2,1,0:T(8,128)(2,1)} custom-call(s32[1152]{0:T(1024)S(1)} %get-tuple-element.21.left_ref, s32[1152]{0:T(1024)S(1)} %get-tuple-element.20.right_ref, s32[288]{0:T(512)S(1)} %convert_reduce_fusion.1.target_ref, s32[3]{0:T(128)S(1)} %select_reduce_fusion.1.bounds_ref, s32[32]{0:T(128)S(1)} %select_reduce_fusion.slot_ref, ...), custom_call_target="tpu_custom_call" | custom-call | flops 3221225472 | bytes 8388608 | tf_op jit(solution)/shard_map/block_products/pallas_call | solution.py:183
  126.8 0.5 slice_multiply_fusion
  (88 shorter events, 5.0 us)
Async XLA Ops:
  0.6 9.8 %copy-start.5 = (s32[1,1,2,32]{3,2,1,0:T(2,128)S(1)}, s32[1,1,2,32]{3,2,1,0:T(2,128)}, u32[]{:S(2)}) copy-start(s32[1,1,2,32]{3,2,1,0:T(2,128)} %param.7) | copy-start | bytes 772
  0.7 9.8 %copy-start.2 = (s32[1,1,4,3,256]{4,2,3,1,0:T(4,128)S(1)}, s32[1,1,4,3,256]{4,2,3,1,0:T(4,128)}, u32[]{:S(2)}) copy-start(s32[1,1,4,3,256]{4,2,3,1,0:T(4,128)} %param.8) | copy-start | bytes 36868
  0.7 10.8 %copy-start.3 = (s32[4]{0:T(128)S(1)}, s32[4]{0:T(128)}, u32[]{:S(2)}) copy-start(s32[4]{0:T(128)} %param.9) | copy-start | bytes 52
  2.4 9.7 %collective-permute-start.2 = (bf16[2,2,2,128,128]{4,3,2,1,0:T(8,128)(2,1)S(1)}, bf16[2,2,2,128,128]{4,3,2,1,0:T(8,128)(2,1)}, u32[]{:S(2)}, u32[]{:S(2)}) collective-permute-start(bf16[2,2,2,128,128]{4,3,2,1,0:T(8,128)(2,1)S(1)} %get-tuple-element.35), channel_id=1, source_target_pairs={{0,4},{1,5},{2,6},{3,7},{4,0},{5,1},{6,2},{7,3},{8,12},{9,13},{10,... | collective-permute-start | bytes 786440 | tf_op jit(solution)/shard_map/ppermute | solution.py:23
  4.8 12.4 %collective-permute-start.1 = (bf16[2,2,2,128,128]{4,3,2,1,0:T(8,128)(2,1)S(1)}, bf16[2,2,2,128,128]{4,3,2,1,0:T(8,128)(2,1)S(1)}, u32[]{:S(2)}, u32[]{:S(2)}) collective-permute-start(bf16[2,2,2,128,128]{4,3,2,1,0:T(8,128)(2,1)S(1)} %get-tuple-element.36), channel_id=1, source_target_pairs={{0,8},{1,9},{2,10},{3,11},{4,12},{5,13},{6,14},{7,15},{8,0},{9,1},... | collective-permute-start | bytes 786440 | tf_op jit(solution)/shard_map/ppermute | solution.py:23
  5.5 13.1 %collective-permute-start = (bf16[2,2,2,128,128]{4,3,2,1,0:T(8,128)(2,1)S(1)}, bf16[2,2,2,128,128]{4,3,2,1,0:T(8,128)(2,1)S(1)}, u32[]{:S(2)}, u32[]{:S(2)}) collective-permute-start(bf16[2,2,2,128,128]{4,3,2,1,0:T(8,128)(2,1)S(1)} %get-tuple-element.37), channel_id=1, source_target_pairs={{0,12},{1,13},{2,14},{3,15},{4,8},{5,9},{6,10},{7,11},{8,4},{9,5},... | collective-permute-start | bytes 786440 | tf_op jit(solution)/shard_map/ppermute | solution.py:23
  6.3 17.3 %collective-permute-start.11 = (bf16[2,2,2,128,128]{4,3,2,1,0:T(8,128)(2,1)S(1)}, bf16[2,2,2,128,128]{4,3,2,1,0:T(8,128)(2,1)S(1)}, u32[]{:S(2)}, u32[]{:S(2)}) collective-permute-start(bf16[2,2,2,128,128]{4,3,2,1,0:T(8,128)(2,1)S(1)} %get-tuple-element.32), channel_id=1, source_target_pairs={{0,64},{16,80},{32,96},{48,112},{64,0},{80,16},{96,32},{112,48},{1... | collective-permute-start | bytes 786440 | tf_op jit(solution)/shard_map/ppermute | solution.py:23
  7.6 16.8 %collective-permute-start.10 = (bf16[2,2,2,128,128]{4,3,2,1,0:T(8,128)(2,1)S(1)}, bf16[2,2,2,128,128]{4,3,2,1,0:T(8,128)(2,1)S(1)}, u32[]{:S(2)}, u32[]{:S(2)}) collective-permute-start(bf16[2,2,2,128,128]{4,3,2,1,0:T(8,128)(2,1)S(1)} %get-tuple-element.33), channel_id=1, source_target_pairs={{0,128},{16,144},{32,160},{48,176},{64,192},{80,208},{96,224},{112... | collective-permute-start | bytes 786440 | tf_op jit(solution)/shard_map/ppermute | solution.py:23
  12.1 13.0 %collective-permute-start.9 = (bf16[2,2,2,128,128]{4,3,2,1,0:T(8,128)(2,1)S(1)}, bf16[2,2,2,128,128]{4,3,2,1,0:T(8,128)(2,1)S(1)}, u32[]{:S(2)}, u32[]{:S(2)}) collective-permute-start(bf16[2,2,2,128,128]{4,3,2,1,0:T(8,128)(2,1)S(1)} %get-tuple-element.30), channel_id=1, source_target_pairs={{0,192},{16,208},{32,224},{48,240},{64,128},{80,144},{96,160},{112... | collective-permute-start | bytes 786440 | tf_op jit(solution)/shard_map/ppermute | solution.py:23
  18.9 8.7 %collective-permute-start.3 = (bf16[4,128,128]{2,1,0:T(8,128)(2,1)S(1)}, bf16[4,128,128]{2,1,0:T(8,128)(2,1)S(1)}, u32[]{:S(2)}, u32[]{:S(2)}) collective-permute-start(bf16[4,128,128]{2,1,0:T(8,128)(2,1)S(1)} %get-tuple-element.40), channel_id=1, source_target_pairs={{0,3},{1,2},{2,1},{3,0},{4,7},{5,6},{6,5},{7,4},{8,11},{9,10},{10,... | collective-permute-start | bytes 393224 | tf_op jit(solution)/shard_map/ppermute | solution.py:23
  23.6 8.9 %collective-permute-start.4 = (bf16[4,128,128]{2,1,0:T(8,128)(2,1)S(1)}, bf16[4,128,128]{2,1,0:T(8,128)(2,1)S(1)}, u32[]{:S(2)}, u32[]{:S(2)}) collective-permute-start(bf16[4,128,128]{2,1,0:T(8,128)(2,1)S(1)} %get-tuple-element.39), channel_id=1, source_target_pairs={{0,2},{1,3},{2,0},{3,1},{4,6},{5,7},{6,4},{7,5},{8,10},{9,11},{10,... | collective-permute-start | bytes 393224 | tf_op jit(solution)/shard_map/ppermute | solution.py:23
  23.6 8.9 %collective-permute-start.5 = (bf16[4,128,128]{2,1,0:T(8,128)(2,1)S(1)}, bf16[4,128,128]{2,1,0:T(8,128)(2,1)S(1)}, u32[]{:S(2)}, u32[]{:S(2)}) collective-permute-start(bf16[4,128,128]{2,1,0:T(8,128)(2,1)S(1)} %get-tuple-element.38), channel_id=1, source_target_pairs={{0,1},{1,0},{2,3},{3,2},{4,5},{5,4},{6,7},{7,6},{8,9},{9,8},{10,11... | collective-permute-start | bytes 393224 | tf_op jit(solution)/shard_map/ppermute | solution.py:23
  25.4 19.0 %collective-permute-start.12 = (bf16[4,2,128,128]{3,2,1,0:T(8,128)(2,1)S(1)}, bf16[4,2,128,128]{3,2,1,0:T(8,128)(2,1)S(1)}, u32[]{:S(2)}, u32[]{:S(2)}) collective-permute-start(bf16[4,2,128,128]{3,2,1,0:T(8,128)(2,1)S(1)} %dynamic-slice_bitcast_fusion), channel_id=1, source_target_pairs={{0,16},{16,0},{32,48},{48,32},{64,80},{80,64},{96,112},{112,96},{1... | collective-permute-start | bytes 786440 | tf_op jit(solution)/shard_map/ppermute | solution.py:23
  32.5 40.4 %copy-start.4 = (s32[3]{0:T(128)S(1)}, s32[3]{0:T(128)}, u32[]{:S(2)}) copy-start(s32[3]{0:T(128)} %constant.93.clone) | copy-start | bytes 40
  32.6 8.3 %collective-permute-start.8 = (bf16[4,128,128]{2,1,0:T(8,128)(2,1)S(1)}, bf16[4,128,128]{2,1,0:T(8,128)(2,1)S(1)}, u32[]{:S(2)}, u32[]{:S(2)}) collective-permute-start(bf16[4,128,128]{2,1,0:T(8,128)(2,1)S(1)} %fusion.9), channel_id=1, source_target_pairs={{0,3},{1,2},{2,1},{3,0},{4,7},{5,6},{6,5},{7,4},{8,11},{9,10},{10,... | collective-permute-start | bytes 393224 | tf_op jit(solution)/shard_map/ppermute | solution.py:23
  35.4 8.9 %collective-permute-start.7 = (bf16[4,128,128]{2,1,0:T(8,128)(2,1)S(1)}, bf16[4,128,128]{2,1,0:T(8,128)(2,1)S(1)}, u32[]{:S(2)}, u32[]{:S(2)}) collective-permute-start(bf16[4,128,128]{2,1,0:T(8,128)(2,1)S(1)} %fusion.9), channel_id=1, source_target_pairs={{0,2},{1,3},{2,0},{3,1},{4,6},{5,7},{6,4},{7,5},{8,10},{9,11},{10,... | collective-permute-start | bytes 393224 | tf_op jit(solution)/shard_map/ppermute | solution.py:23
  35.4 8.9 %collective-permute-start.6 = (bf16[4,128,128]{2,1,0:T(8,128)(2,1)S(1)}, bf16[4,128,128]{2,1,0:T(8,128)(2,1)S(1)}, u32[]{:S(2)}, u32[]{:S(2)}) collective-permute-start(bf16[4,128,128]{2,1,0:T(8,128)(2,1)S(1)} %fusion.9), channel_id=1, source_target_pairs={{0,1},{1,0},{2,3},{3,2},{4,5},{5,4},{6,7},{7,6},{8,9},{9,8},{10,11... | collective-permute-start | bytes 393224 | tf_op jit(solution)/shard_map/ppermute | solution.py:23
  44.5 21.2 %collective-permute-start.14 = (bf16[16,128,128]{2,1,0:T(8,128)(2,1)S(1)}, bf16[16,128,128]{2,1,0:T(8,128)(2,1)S(1)}, u32[]{:S(2)}, u32[]{:S(2)}) collective-permute-start(bf16[16,128,128]{2,1,0:T(8,128)(2,1)S(1)} %pad_maximum_fusion.1), channel_id=1, source_target_pairs={{0,4},{1,5},{2,6},{3,7},{4,0},{5,1},{6,2},{7,3},{8,12},{9,13},{10,... | collective-permute-start | bytes 1572872 | tf_op jit(solution)/shard_map/ppermute | solution.py:23
  48.4 17.3 %collective-permute-start.15 = (bf16[16,128,128]{2,1,0:T(8,128)(2,1)S(1)}, bf16[16,128,128]{2,1,0:T(8,128)(2,1)S(1)}, u32[]{:S(2)}, u32[]{:S(2)}) collective-permute-start(bf16[16,128,128]{2,1,0:T(8,128)(2,1)S(1)} %pad_maximum_fusion.1), channel_id=1, source_target_pairs={{0,12},{1,13},{2,14},{3,15},{4,8},{5,9},{6,10},{7,11},{8,4},{9,5},... | collective-permute-start | bytes 1572872 | tf_op jit(solution)/shard_map/ppermute | solution.py:23
  48.4 17.2 %collective-permute-start.13 = (bf16[4,2,128,128]{3,2,1,0:T(8,128)(2,1)S(1)}, bf16[4,2,128,128]{3,2,1,0:T(8,128)(2,1)S(1)}, u32[]{:S(2)}, u32[]{:S(2)}) collective-permute-start(bf16[4,2,128,128]{3,2,1,0:T(8,128)(2,1)S(1)} %bitcast_select_fusion), channel_id=1, source_target_pairs={{0,32},{16,48},{32,0},{48,16},{64,96},{80,112},{96,64},{112,80},{1... | collective-permute-start | bytes 786440 | tf_op jit(solution)/shard_map/ppermute | solution.py:23
  65.7 7.3 %collective-permute-start.17 = (bf16[8,128,128]{2,1,0:T(8,128)(2,1)S(1)}, bf16[8,128,128]{2,1,0:T(8,128)(2,1)S(1)}, u32[]{:S(2)}, u32[]{:S(2)}) collective-permute-start(bf16[8,128,128]{2,1,0:T(8,128)(2,1)S(1)} %bitcast.90), channel_id=1, source_target_pairs={{0,64},{16,80},{32,96},{48,112},{64,0},{80,16},{96,32},{112,48},{1... | collective-permute-start | bytes 786440 | tf_op jit(solution)/shard_map/ppermute | solution.py:23
  67.4 10.7 %collective-permute-start.18 = (bf16[8,128,128]{2,1,0:T(8,128)(2,1)S(1)}, bf16[8,128,128]{2,1,0:T(8,128)(2,1)S(1)}, u32[]{:S(2)}, u32[]{:S(2)}) collective-permute-start(bf16[8,128,128]{2,1,0:T(8,128)(2,1)S(1)} %bitcast.91), channel_id=1, source_target_pairs={{0,128},{16,144},{32,160},{48,176},{64,192},{80,208},{96,224},{112... | collective-permute-start | bytes 786440 | tf_op jit(solution)/shard_map/ppermute | solution.py:23
  70.3 10.4 %collective-permute-start.19 = (bf16[8,128,128]{2,1,0:T(8,128)(2,1)S(1)}, bf16[8,128,128]{2,1,0:T(8,128)(2,1)S(1)}, u32[]{:S(2)}, u32[]{:S(2)}) collective-permute-start(bf16[8,128,128]{2,1,0:T(8,128)(2,1)S(1)} %bitcast.92), channel_id=1, source_target_pairs={{0,192},{16,208},{32,224},{48,240},{64,128},{80,144},{96,160},{112... | collective-permute-start | bytes 786440 | tf_op jit(solution)/shard_map/ppermute | solution.py:23
  70.6 10.8 %collective-permute-start.16 = (bf16[16,128,128]{2,1,0:T(8,128)(2,1)S(1)}, bf16[16,128,128]{2,1,0:T(8,128)(2,1)S(1)}, u32[]{:S(2)}, u32[]{:S(2)}) collective-permute-start(bf16[16,128,128]{2,1,0:T(8,128)(2,1)S(1)} %pad_maximum_fusion.1), channel_id=1, source_target_pairs={{0,8},{1,9},{2,10},{3,11},{4,12},{5,13},{6,14},{7,15},{8,0},{9,1},... | collective-permute-start | bytes 1572872 | tf_op jit(solution)/shard_map/ppermute | solution.py:23
  80.8 2.7 %collective-permute-start.20 = (bf16[32,128,128]{2,1,0:T(8,128)(2,1)S(1)}, bf16[32,128,128]{2,1,0:T(8,128)(2,1)S(1)}, u32[]{:S(2)}, u32[]{:S(2)}) collective-permute-start(bf16[32,128,128]{2,1,0:T(8,128)(2,1)S(1)} %pad_maximum_fusion), channel_id=1, source_target_pairs={{0,16},{16,0},{32,48},{48,32},{64,80},{80,64},{96,112},{112,96},{1... | collective-permute-start | bytes 3145736 | tf_op jit(solution)/shard_map/ppermute | solution.py:23
  81.5 2.2 %copy-start = (bf16[1,1,32,128,128]{4,3,2,1,0:T(8,128)(2,1)S(1)}, bf16[1,1,32,128,128]{4,3,2,1,0:T(8,128)(2,1)}, u32[]{:S(2)}) copy-start(bf16[1,1,32,128,128]{4,3,2,1,0:T(8,128)(2,1)} %param.6) | copy-start | bytes 3145732
  81.5 2.2 %copy-start.1 = (s32[1,1,32]{2,1,0:T(1,128)S(1)}, s32[1,1,32]{2,1,0:T(1,128)}, u32[]{:S(2)}) copy-start(s32[1,1,32]{2,1,0:T(1,128)} %param.10) | copy-start | bytes 388
  87.4 7.6 %collective-permute-start.22 = (f32[8,128]{1,0:T(8,128)S(1)}, f32[8,128]{1,0:T(8,128)S(1)}, u32[]{:S(2)}, u32[]{:S(2)}) collective-permute-start(f32[8,128]{1,0:T(8,128)S(1)} %get-tuple-element.16), channel_id=1, source_target_pairs={{0,32},{16,48},{32,0},{48,16},{64,96},{80,112},{96,64},{112,80},{1... | collective-permute-start | bytes 12296 | tf_op jit(solution)/shard_map/ppermute | solution.py:23
  92.5 6.9 %collective-permute-start.23 = (f32[8,128]{1,0:T(8,128)S(1)}, f32[8,128]{1,0:T(8,128)S(1)}, u32[]{:S(2)}, u32[]{:S(2)}) collective-permute-start(f32[8,128]{1,0:T(8,128)S(1)} %get-tuple-element.16), channel_id=1, source_target_pairs={{0,48},{16,32},{32,16},{48,0},{64,112},{80,96},{96,80},{112,64},{1... | collective-permute-start | bytes 12296 | tf_op jit(solution)/shard_map/ppermute | solution.py:23
  93.3 6.1 %collective-permute-start.21 = (f32[8,128]{1,0:T(8,128)S(1)}, f32[8,128]{1,0:T(8,128)S(1)}, u32[]{:S(2)}, u32[]{:S(2)}) collective-permute-start(f32[8,128]{1,0:T(8,128)S(1)} %get-tuple-element.16), channel_id=1, source_target_pairs={{0,16},{16,0},{32,48},{48,32},{64,80},{80,64},{96,112},{112,96},{1... | collective-permute-start | bytes 12296 | tf_op jit(solution)/shard_map/ppermute | solution.py:23
  99.5 5.2 %collective-permute-start.25 = (f32[8,128]{1,0:T(8,128)S(1)}, f32[8,128]{1,0:T(8,128)S(1)}, u32[]{:S(2)}, u32[]{:S(2)}) collective-permute-start(f32[8,128]{1,0:T(8,128)S(1)} %add_add_fusion.2), channel_id=1, source_target_pairs={{0,128},{16,144},{32,160},{48,176},{64,192},{80,208},{96,224},{112... | collective-permute-start | bytes 12296 | tf_op jit(solution)/shard_map/ppermute | solution.py:23
  100.3 4.8 %collective-permute-start.26 = (f32[8,128]{1,0:T(8,128)S(1)}, f32[8,128]{1,0:T(8,128)S(1)}, u32[]{:S(2)}, u32[]{:S(2)}) collective-permute-start(f32[8,128]{1,0:T(8,128)S(1)} %add_add_fusion.2), channel_id=1, source_target_pairs={{0,192},{16,208},{32,224},{48,240},{64,128},{80,144},{96,160},{112... | collective-permute-start | bytes 12296 | tf_op jit(solution)/shard_map/ppermute | solution.py:23
  101.9 3.6 %collective-permute-start.24 = (f32[8,128]{1,0:T(8,128)S(1)}, f32[8,128]{1,0:T(8,128)S(1)}, u32[]{:S(2)}, u32[]{:S(2)}) collective-permute-start(f32[8,128]{1,0:T(8,128)S(1)} %add_add_fusion.2), channel_id=1, source_target_pairs={{0,64},{16,80},{32,96},{48,112},{64,0},{80,16},{96,32},{112,48},{1... | collective-permute-start | bytes 12296 | tf_op jit(solution)/shard_map/ppermute | solution.py:23
  105.5 4.5 %collective-permute-start.28 = (f32[8,128]{1,0:T(8,128)S(1)}, f32[8,128]{1,0:T(8,128)S(1)}, u32[]{:S(2)}, u32[]{:S(2)}) collective-permute-start(f32[8,128]{1,0:T(8,128)S(1)} %add_add_fusion.1), channel_id=1, source_target_pairs={{0,2},{1,3},{2,0},{3,1},{4,6},{5,7},{6,4},{7,5},{8,10},{9,11},{10,... | collective-permute-start | bytes 12296 | tf_op jit(solution)/shard_map/ppermute | solution.py:23
  105.5 5.5 %collective-permute-start.29 = (f32[8,128]{1,0:T(8,128)S(1)}, f32[8,128]{1,0:T(8,128)S(1)}, u32[]{:S(2)}, u32[]{:S(2)}) collective-permute-start(f32[8,128]{1,0:T(8,128)S(1)} %add_add_fusion.1), channel_id=1, source_target_pairs={{0,3},{1,2},{2,1},{3,0},{4,7},{5,6},{6,5},{7,4},{8,11},{9,10},{10,... | collective-permute-start | bytes 12296 | tf_op jit(solution)/shard_map/ppermute | solution.py:23
  107.6 3.6 %collective-permute-start.27 = (f32[8,128]{1,0:T(8,128)S(1)}, f32[8,128]{1,0:T(8,128)S(1)}, u32[]{:S(2)}, u32[]{:S(2)}) collective-permute-start(f32[8,128]{1,0:T(8,128)S(1)} %add_add_fusion.1), channel_id=1, source_target_pairs={{0,1},{1,0},{2,3},{3,2},{4,5},{5,4},{6,7},{7,6},{8,9},{9,8},{10,11... | collective-permute-start | bytes 12296 | tf_op jit(solution)/shard_map/ppermute | solution.py:23
  111.2 15.4 %collective-permute-start.31 = (f32[8,128]{1,0:T(8,128)S(1)}, f32[8,128]{1,0:T(8,128)S(1)}, u32[]{:S(2)}, u32[]{:S(2)}) collective-permute-start(f32[8,128]{1,0:T(8,128)S(1)} %add_add_fusion), channel_id=1, source_target_pairs={{0,8},{1,9},{2,10},{3,11},{4,12},{5,13},{6,14},{7,15},{8,0},{9,1},... | collective-permute-start | bytes 12296 | tf_op jit(solution)/shard_map/ppermute | solution.py:23
  113.4 13.3 %collective-permute-start.32 = (f32[8,128]{1,0:T(8,128)S(1)}, f32[8,128]{1,0:T(8,128)S(1)}, u32[]{:S(2)}, u32[]{:S(2)}) collective-permute-start(f32[8,128]{1,0:T(8,128)S(1)} %add_add_fusion), channel_id=1, source_target_pairs={{0,12},{1,13},{2,14},{3,15},{4,8},{5,9},{6,10},{7,11},{8,4},{9,5},... | collective-permute-start | bytes 12296 | tf_op jit(solution)/shard_map/ppermute | solution.py:23
  113.7 13.0 %collective-permute-start.30 = (f32[8,128]{1,0:T(8,128)S(1)}, f32[8,128]{1,0:T(8,128)S(1)}, u32[]{:S(2)}, u32[]{:S(2)}) collective-permute-start(f32[8,128]{1,0:T(8,128)S(1)} %add_add_fusion), channel_id=1, source_target_pairs={{0,4},{1,5},{2,6},{3,7},{4,0},{5,1},{6,2},{7,3},{8,12},{9,13},{10,... | collective-permute-start | bytes 12296 | tf_op jit(solution)/shard_map/ppermute | solution.py:23

commit v3 on v2

--- a/solution.py
+++ b/solution.py
@@ -12,10 +12,10 @@
 NO = 32
 TASKS = 1024
 GROUP = 4
-UNROLL = 8
-NGROUP = 288
+UNROLL = 16
+NGROUP = 304
 ZERO = 64
-FIRST = 8
+FIRST, SECOND = 8, 20
 SCALE = 1.0 / (32 * 4 * 128) ** 0.5
 
 
@@ -63,13 +63,15 @@
     got = swap(pick(by_j, 1 - core), "row", 1)
     half = choose([pick(by_j, core), got], ((panels >> 1) & 1) ^ core)
 
-    line = jnp.concatenate([held] + [swap(held, "col", d) for d in (1, 2, 3)])
-    line, half = lax.optimization_barrier((line, half))
-    columns = [line] + [swap(line, "col", 4 * d) for d in (1, 2, 3)]
+    ahead = [swap(held, "col", 4 * d) for d in (1, 2, 3)]
+    near = jnp.concatenate([swap(held, "col", d) for d in (1, 2, 3)])
+    near, half, *ahead = lax.optimization_barrier((near, half, *ahead))
+    behind = [swap(near, "col", 4 * d) for d in (1, 2, 3)]
 
     half = choose([half, swap(half, "row", 2)], ((panels >> 2) & 1) ^ zh).reshape(WIN * 2, BS, BS)
-    half, columns[1], columns[3] = lax.optimization_barrier((half, columns[1], columns[3]))
+    half, behind[0] = lax.optimization_barrier((half, behind[0]))
     line = jnp.concatenate([half] + [swap(half, "row", 4 * d) for d in (1, 2, 3)])
+    columns = [held, near] + [part for pair in zip(ahead, behind) for part in pair]
     return columns, [line, swap(line, "row", 1)]
 
 
@@ -105,7 +107,7 @@
     gid = jnp.arange(NGROUP, dtype=jnp.int32)[:, None]
     target = jnp.sum((gid >= (starts + groups)[None, :]).astype(jnp.int32), axis=1)
     slot_of = jnp.sum(jnp.where(rank[:, None] == slots[None, :], slots[:, None], 0), axis=0)
-    limits = jnp.array([0, FIRST, NO], jnp.int32)
+    limits = jnp.array([0, FIRST, SECOND, NO], jnp.int32)
     bounds = jnp.sum(jnp.where(rank[None, :] < limits[:, None], groups[None, :], 0), axis=1)
     return lists[:, 0] + ZERO, lists[:, 1], target, bounds, slot_of, diag.astype(jnp.int32)
 
@@ -128,7 +130,7 @@
             acc[jnp.minimum(target_ref[g] - base, count)] += product
         return carry
 
-    lax.fori_loop(0, (last - first + UNROLL - 1) >> 3, some, 0)
+    lax.fori_loop(0, (last - first + UNROLL - 1) >> 4, some, 0)
 
 
 def first_kernel(left_ref, right_ref, target_ref, bounds_ref, slot_ref, branch_ref, diag_ref, lhs, rhs, own, out, sums, acc, old, new):
@@ -158,23 +160,41 @@
     sums[1:2, :] = jnp.sum(jnp.where(eye, new[...], 0.0), axis=0, keepdims=True)
 
 
-def rest_kernel(left_ref, right_ref, target_ref, bounds_ref, slot_ref, branch_ref, diag_ref, lhs, rhs, own, filled, out, acc):
-    accumulate(1, FIRST, NO - FIRST, left_ref, right_ref, target_ref, bounds_ref, lhs, rhs, acc)
-
-    def copy(i, carry):
-        out[slot_ref[i]] = filled[i]
-        return carry
-
-    lax.fori_loop(0, FIRST, copy, 0)
+def second_kernel(left_ref, right_ref, target_ref, bounds_ref, slot_ref, branch_ref, lhs, rhs, own, out, acc):
+    accumulate(1, FIRST, SECOND - FIRST, left_ref, right_ref, target_ref, bounds_ref, lhs, rhs, acc)
 
     def finish(i, carry):
         o = slot_ref[FIRST + i]
         product = acc[i]
         value = jnp.where(branch_ref[o] == 0, product, 2.0 * own[o].astype(jnp.float32) - product)
+        out[i] = value.astype(jnp.bfloat16)
+        return carry
+
+    lax.fori_loop(0, SECOND - FIRST, finish, 0)
+
+
+def third_kernel(left_ref, right_ref, target_ref, bounds_ref, slot_ref, branch_ref, lhs, rhs, own, first, second, out, acc):
+    accumulate(2, SECOND, NO - SECOND, left_ref, right_ref, target_ref, bounds_ref, lhs, rhs, acc)
+
+    def copy_first(i, carry):
+        out[slot_ref[i]] = first[i]
+        return carry
+
+    def copy_second(i, carry):
+        out[slot_ref[FIRST + i]] = second[i]
+        return carry
+
+    lax.fori_loop(0, FIRST, copy_first, 0)
+    lax.fori_loop(0, SECOND - FIRST, copy_second, 0)
+
+    def finish(i, carry):
+        o = slot_ref[SECOND + i]
+        product = acc[i]
+        value = jnp.where(branch_ref[o] == 0, product, 2.0 * own[o].astype(jnp.float32) - product)
         out[o] = value.astype(jnp.bfloat16)
         return carry
 
-    lax.fori_loop(0, NO - FIRST, finish, 0)
+    lax.fori_loop(0, NO - SECOND, finish, 0)
 
 
 def products(kernel, count, out_shape, scratch, scalars, arrays):
@@ -200,16 +220,21 @@
     arrays = (lhs, jnp.concatenate(rows), own)
     scalars = (left, right, target, bounds, slot_of, branch[0, 0], diag)
     shapes = (jax.ShapeDtypeStruct((FIRST, BS, BS), jnp.bfloat16), jax.ShapeDtypeStruct((8, BS), jnp.float32))
-    filled, value = products(first_kernel, FIRST, shapes, (FIRST + 1, 0, 0), scalars, arrays)
+    first, value = products(first_kernel, FIRST, shapes, (FIRST + 1, 0, 0), scalars, arrays)
     for axis, low, high in (("row", 1, 2), ("row", 4, 8), ("col", 1, 2)):
         one, two, three = (swap(value, axis, b) for b in (low, high, low + high))
         value = (value + one) + (two + three)
-    value, filled = lax.optimization_barrier((value, filled))
-    one, two, three = (swap(value, "col", b) for b in (4, 8, 12))
+    scalars = scalars[:6]
+    value, own = lax.optimization_barrier((value, own))
+    arrays = arrays[:2] + (own,)
+    other = swap(value, "col", 4)
+    shapes = jax.ShapeDtypeStruct((SECOND - FIRST, BS, BS), jnp.bfloat16)
+    second = products(second_kernel, SECOND - FIRST, shapes, (SECOND - FIRST + 1,), scalars, arrays)
+    value, second = lax.optimization_barrier((value + other, second))
+    other = swap(value, "col", 8)
     shapes = jax.ShapeDtypeStruct((NO, BS, BS), jnp.bfloat16)
-    out = products(rest_kernel, NO - FIRST, shapes, (NO - FIRST + 1,), scalars, arrays + (filled,))
-    value = (value + one) + (two + three)
-    traces = jnp.sum(value, axis=1)[:2] * SCALE
+    out = products(third_kernel, NO - SECOND, shapes, (NO - SECOND + 1,), scalars, arrays + (first, second))
+    traces = jnp.sum(value + other, axis=1)[:2] * SCALE
     return out[None, None], traces
 
 

time: 128 us -> 125 us (0.977)
  waiting for transfers between devices: 48.8 us -> 40.9 us
  starting transfers between devices: 55.6 us -> 60.5 us
    ppermute x33 -> x35, waiting for transfers between devices: 48.8 us -> 40.9 us  [swap(): return lax.ppermute(value, axis, [(i, i ^ bit) for i in range(16)])]
    ppermute x33 -> x35, starting transfers between devices: 55.6 us -> 60.5 us  [swap(): return lax.ppermute(value, axis, [(i, i ^ bit) for i in range(16)])]
    pallas_call x2 -> x3, Pallas kernels: 14.4 us -> 13.3 us  [products(): pl.pallas_call(kernel, out_shape=out_shape, in_specs=[smem] * len(scalars...]
  transfers between devices with their start and end apart: 33 -> 35, of which waited for: 21 -> 21; matrix products, arithmetic and copies ran while one was open for 4% -> 4% of each run, Pallas kernels for 8% -> 8%
where the time goes in v3:
time: 125 us; the launch traced here: 123 us
  starting transfers between devices  60.5 us (48%)
  waiting for transfers between devices  40.9 us (33%)
  Pallas kernels  13.3 us (11%)
  local copies, waits for them, and re-layouts  3.45 us (3%)
  other arithmetic  2.58 us (2%)
  matrix products  1.44 us (1%)
    ppermute x35, starting transfers between devices, swap(): return lax.ppermute(value, axis, [(i, i ^ bit) for i in range(16)])  60.5 us
    ppermute x35, waiting for transfers between devices, swap(): return lax.ppermute(value, axis, [(i, i ^ bit) for i in range(16)])  40.9 us
    pallas_call x3, Pallas kernels, products(): pl.pallas_call(kernel, out_shape=out_shape, in_specs=[smem] * len(scalars...  13.3 us
  transfers between devices with their start and end apart: 35, of which 21 were waited for; matrix products, arithmetic and copies ran while one was open for 4% of the time, Pallas kernels for 8%

profile of v3, /device:TPU:2, one launch (start us, length us, event | category | flops | bytes accessed | tf_op | source)
XLA Modules:
  0.0 123.3 jit_solution(15773890735520163852)
XLA Ops:
  0.7 1.7 %dynamic-slice_bitcast_fusion.4 = (bf16[2,2,2,128,128]{4,3,2,1,0:T(8,128)(2,1)S(1)}, bf16[1,2,2,2,128,128]{5,4,3,2,1,0:T(8,128)(2,1)S(1)}, bf16[2,2,2,128,128]{4...) fusion(bf16[2,2,4,2,128,128]{5,4,3,2,1,0:T(8,128)(2,1)} %bitcas, ...), kind=kLoop, calls=%fused_computation.19 | loop fusion | bytes 4194336 | tf_op jit(solution)/shard_map/jit(dynamic_index_in_dim)/squeeze | solution.py:27
  2.4 2.4 %collective-permute-start.2 = (bf16[2,2,2,128,128]{4,3,2,1,0:T(8,128)(2,1)S(1)}, bf16[2,2,2,128,128]{4,3,2,1,0:T(8,128)(2,1)}, u32[]{:S(2)}, u32[]{:S(2)}) collective-permute-start(bf16[2,2,2,128,128]{4,3,2,1,0:T(8,128)(2,1)S(1)} %get-tuple-element.45), channel_id=1, source_target_pairs={{0,4},{1,5},{2,6},{3,7},{4,0},{5,1},{6,2},{7,3},{8,12},{9,13},{10,... | collective-permute-start | bytes 786440 | tf_op jit(solution)/shard_map/ppermute | solution.py:23
  4.7 0.7 collective-permute-start.1
  5.4 0.9 collective-permute-start
  6.3 1.2 collective-permute-start.11
  7.5 2.9 %collective-permute-start.10 = (bf16[2,2,2,128,128]{4,3,2,1,0:T(8,128)(2,1)S(1)}, bf16[2,2,2,128,128]{4,3,2,1,0:T(8,128)(2,1)S(1)}, u32[]{:S(2)}, u32[]{:S(2)}) collective-permute-start(bf16[2,2,2,128,128]{4,3,2,1,0:T(8,128)(2,1)S(1)} %get-tuple-element.43), channel_id=1, source_target_pairs={{0,128},{16,144},{32,160},{48,176},{64,192},{80,208},{96,224},{112... | collective-permute-start | bytes 786440 | tf_op jit(solution)/shard_map/ppermute | solution.py:23
  11.5 0.9 fusion.3
  12.5 2.3 %collective-permute-start.9 = (bf16[2,2,2,128,128]{4,3,2,1,0:T(8,128)(2,1)S(1)}, bf16[2,2,2,128,128]{4,3,2,1,0:T(8,128)(2,1)S(1)}, u32[]{:S(2)}, u32[]{:S(2)}) collective-permute-start(bf16[2,2,2,128,128]{4,3,2,1,0:T(8,128)(2,1)S(1)} %get-tuple-element.40), channel_id=1, source_target_pairs={{0,192},{16,208},{32,224},{48,240},{64,128},{80,144},{96,160},{112... | collective-permute-start | bytes 786440 | tf_op jit(solution)/shard_map/ppermute | solution.py:23
  14.8 1.0 fusion.22
  15.8 1.4 %collective-permute-done.1 = bf16[2,2,2,128,128]{4,3,2,1,0:T(8,128)(2,1)S(1)} collective-permute-done((bf16[2,2,2,128,128]{4,3,2,1,0:T(8,128)(2,1)S(1)}, bf16[2,2,2,128,128]{4,3,2,1,0:T(8,128)(2,1)S(1)}, u32[]{:S(2)}, u32[]{:S(2)}) %collective-permute-start.1) | collective-permute-done | bytes 262176 | tf_op jit(solution)/shard_map/ppermute | solution.py:23
  17.2 1.3 %collective-permute-done = bf16[2,2,2,128,128]{4,3,2,1,0:T(8,128)(2,1)S(1)} collective-permute-done((bf16[2,2,2,128,128]{4,3,2,1,0:T(8,128)(2,1)S(1)}, bf16[2,2,2,128,128]{4,3,2,1,0:T(8,128)(2,1)S(1)}, u32[]{:S(2)}, u32[]{:S(2)}) %collective-permute-start) | collective-permute-done | bytes 262176 | tf_op jit(solution)/shard_map/ppermute | solution.py:23
  18.9 4.7 %collective-permute-start.3 = (bf16[4,128,128]{2,1,0:T(8,128)(2,1)S(1)}, bf16[4,128,128]{2,1,0:T(8,128)(2,1)S(1)}, u32[]{:S(2)}, u32[]{:S(2)}) collective-permute-start(bf16[4,128,128]{2,1,0:T(8,128)(2,1)S(1)} %get-tuple-element.50), channel_id=1, source_target_pairs={{0,3},{1,2},{2,1},{3,0},{4,7},{5,6},{6,5},{7,4},{8,11},{9,10},{10,... | collective-permute-start | bytes 393224 | tf_op jit(solution)/shard_map/ppermute | solution.py:23
  23.6 0.7 collective-permute-start.5
  24.3 1.1 collective-permute-done.9
  25.9 1.7 %collective-permute-done.3 = bf16[4,128,128]{2,1,0:T(8,128)(2,1)S(1)} collective-permute-done((bf16[4,128,128]{2,1,0:T(8,128)(2,1)S(1)}, bf16[4,128,128]{2,1,0:T(8,128)(2,1)S(1)}, u32[]{:S(2)}, u32[]{:S(2)}) %collective-permute-start.3) | collective-permute-done | bytes 131104 | tf_op jit(solution)/shard_map/ppermute | solution.py:23
  27.6 4.8 %collective-permute-done.4 = bf16[4,128,128]{2,1,0:T(8,128)(2,1)S(1)} collective-permute-done((bf16[4,128,128]{2,1,0:T(8,128)(2,1)S(1)}, bf16[4,128,128]{2,1,0:T(8,128)(2,1)S(1)}, u32[]{:S(2)}, u32[]{:S(2)}) %collective-permute-start.4) | collective-permute-done | bytes 131104 | tf_op jit(solution)/shard_map/ppermute | solution.py:23
  32.6 2.8 %collective-permute-start.8 = (bf16[4,128,128]{2,1,0:T(8,128)(2,1)S(1)}, bf16[4,128,128]{2,1,0:T(8,128)(2,1)S(1)}, u32[]{:S(2)}, u32[]{:S(2)}) collective-permute-start(bf16[4,128,128]{2,1,0:T(8,128)(2,1)S(1)} %get-tuple-element.35), channel_id=1, source_target_pairs={{0,3},{1,2},{2,1},{3,0},{4,7},{5,6},{6,5},{7,4},{8,11},{9,10},{10,... | collective-permute-start | bytes 393224 | tf_op jit(solution)/shard_map/ppermute | solution.py:23
  35.7 1.6 %collective-permute-start.6 = (bf16[4,128,128]{2,1,0:T(8,128)(2,1)S(1)}, bf16[4,128,128]{2,1,0:T(8,128)(2,1)S(1)}, u32[]{:S(2)}, u32[]{:S(2)}) collective-permute-start(bf16[4,128,128]{2,1,0:T(8,128)(2,1)S(1)} %get-tuple-element.35), channel_id=1, source_target_pairs={{0,1},{1,0},{2,3},{3,2},{4,5},{5,4},{6,7},{7,6},{8,9},{9,8},{10,11... | collective-permute-start | bytes 393224 | tf_op jit(solution)/shard_map/ppermute | solution.py:23
  37.3 3.2 %collective-permute-start.13 = (bf16[4,128,128]{2,1,0:T(8,128)(2,1)S(1)}, bf16[4,128,128]{2,1,0:T(8,128)(2,1)S(1)}, u32[]{:S(2)}, u32[]{:S(2)}) collective-permute-start(bf16[4,128,128]{2,1,0:T(8,128)(2,1)S(1)} %get-tuple-element.35), channel_id=1, source_target_pairs={{0,4},{1,5},{2,6},{3,7},{4,0},{5,1},{6,2},{7,3},{8,12},{9,13},{10,... | collective-permute-start | bytes 393224 | tf_op jit(solution)/shard_map/ppermute | solution.py:23
  40.9 2.5 %collective-permute-start.14 = (bf16[4,128,128]{2,1,0:T(8,128)(2,1)S(1)}, bf16[4,128,128]{2,1,0:T(8,128)(2,1)S(1)}, u32[]{:S(2)}, u32[]{:S(2)}) collective-permute-start(bf16[4,128,128]{2,1,0:T(8,128)(2,1)S(1)} %get-tuple-element.35), channel_id=1, source_target_pairs={{0,8},{1,9},{2,10},{3,11},{4,12},{5,13},{6,14},{7,15},{8,0},{9,1},... | collective-permute-start | bytes 393224 | tf_op jit(solution)/shard_map/ppermute | solution.py:23
  43.5 2.2 %collective-permute-start.15 = (bf16[4,128,128]{2,1,0:T(8,128)(2,1)S(1)}, bf16[4,128,128]{2,1,0:T(8,128)(2,1)S(1)}, u32[]{:S(2)}, u32[]{:S(2)}) collective-permute-start(bf16[4,128,128]{2,1,0:T(8,128)(2,1)S(1)} %get-tuple-element.35), channel_id=1, source_target_pairs={{0,12},{1,13},{2,14},{3,15},{4,8},{5,9},{6,10},{7,11},{8,4},{9,5},... | collective-permute-start | bytes 393224 | tf_op jit(solution)/shard_map/ppermute | solution.py:23
  45.8 1.6 %collective-permute-done.14 = bf16[4,128,128]{2,1,0:T(8,128)(2,1)S(1)} collective-permute-done((bf16[4,128,128]{2,1,0:T(8,128)(2,1)S(1)}, bf16[4,128,128]{2,1,0:T(8,128)(2,1)S(1)}, u32[]{:S(2)}, u32[]{:S(2)}) %collective-permute-start.14) | collective-permute-done | bytes 131104 | tf_op jit(solution)/shard_map/ppermute | solution.py:23
  47.4 1.4 %collective-permute-done.15 = bf16[4,128,128]{2,1,0:T(8,128)(2,1)S(1)} collective-permute-done((bf16[4,128,128]{2,1,0:T(8,128)(2,1)S(1)}, bf16[4,128,128]{2,1,0:T(8,128)(2,1)S(1)}, u32[]{:S(2)}, u32[]{:S(2)}) %collective-permute-start.15) | collective-permute-done | bytes 131104 | tf_op jit(solution)/shard_map/ppermute | solution.py:23
  48.8 5.9 %collective-permute-start.16 = (bf16[4,2,128,128]{3,2,1,0:T(8,128)(2,1)S(1)}, bf16[4,2,128,128]{3,2,1,0:T(8,128)(2,1)S(1)}, u32[]{:S(2)}, u32[]{:S(2)}) collective-permute-start(bf16[4,2,128,128]{3,2,1,0:T(8,128)(2,1)S(1)} %bitcast_select_fusion), channel_id=1, source_target_pairs={{0,32},{16,48},{32,0},{48,16},{64,96},{80,112},{96,64},{112,80},{1... | collective-permute-start | bytes 786440 | tf_op jit(solution)/shard_map/ppermute | solution.py:23
  54.8 3.3 %collective-permute-start.17 = (bf16[12,128,128]{2,1,0:T(8,128)(2,1)S(1)}, bf16[12,128,128]{2,1,0:T(8,128)(2,1)S(1)}, u32[]{:S(2)}, u32[]{:S(2)}) collective-permute-start(bf16[12,128,128]{2,1,0:T(8,128)(2,1)S(1)} %pad_maximum_fusion.1), channel_id=1, source_target_pairs={{0,4},{1,5},{2,6},{3,7},{4,0},{5,1},{6,2},{7,3},{8,12},{9,13},{10,... | collective-permute-start | bytes 1179656 | tf_op jit(solution)/shard_map/ppermute | solution.py:23
  58.6 1.2 collective-permute-start.19
  60.2 7.0 %collective-permute-done.17 = bf16[12,128,128]{2,1,0:T(8,128)(2,1)S(1)} collective-permute-done((bf16[12,128,128]{2,1,0:T(8,128)(2,1)S(1)}, bf16[12,128,128]{2,1,0:T(8,128)(2,1)S(1)}, u32[]{:S(2)}, u32[]{:S(2)}) %collective-permute-start.17) | collective-permute-done | bytes 393248 | tf_op jit(solution)/shard_map/ppermute | solution.py:23
  67.2 1.6 %collective-permute-start.20 = (bf16[8,128,128]{2,1,0:T(8,128)(2,1)S(1)}, bf16[8,128,128]{2,1,0:T(8,128)(2,1)S(1)}, u32[]{:S(2)}, u32[]{:S(2)}) collective-permute-start(bf16[8,128,128]{2,1,0:T(8,128)(2,1)S(1)} %bitcast.93), channel_id=1, source_target_pairs={{0,64},{16,80},{32,96},{48,112},{64,0},{80,16},{96,32},{112,48},{1... | collective-permute-start | bytes 786440 | tf_op jit(solution)/shard_map/ppermute | solution.py:23
  68.8 2.9 %collective-permute-start.21 = (bf16[8,128,128]{2,1,0:T(8,128)(2,1)S(1)}, bf16[8,128,128]{2,1,0:T(8,128)(2,1)S(1)}, u32[]{:S(2)}, u32[]{:S(2)}) collective-permute-start(bf16[8,128,128]{2,1,0:T(8,128)(2,1)S(1)} %bitcast.94), channel_id=1, source_target_pairs={{0,128},{16,144},{32,160},{48,176},{64,192},{80,208},{96,224},{112... | collective-permute-start | bytes 786440 | tf_op jit(solution)/shard_map/ppermute | solution.py:23
  72.1 1.5 %collective-permute-done.20 = bf16[8,128,128]{2,1,0:T(8,128)(2,1)S(1)} collective-permute-done((bf16[8,128,128]{2,1,0:T(8,128)(2,1)S(1)}, bf16[8,128,128]{2,1,0:T(8,128)(2,1)S(1)}, u32[]{:S(2)}, u32[]{:S(2)}) %collective-permute-start.20) | collective-permute-done | bytes 262176 | tf_op jit(solution)/shard_map/ppermute | solution.py:23
  73.6 5.4 %collective-permute-done.21 = bf16[8,128,128]{2,1,0:T(8,128)(2,1)S(1)} collective-permute-done((bf16[8,128,128]{2,1,0:T(8,128)(2,1)S(1)}, bf16[8,128,128]{2,1,0:T(8,128)(2,1)S(1)}, u32[]{:S(2)}, u32[]{:S(2)}) %collective-permute-start.21) | collective-permute-done | bytes 262176 | tf_op jit(solution)/shard_map/ppermute | solution.py:23
  79.0 2.7 %collective-permute-done.22 = bf16[8,128,128]{2,1,0:T(8,128)(2,1)S(1)} collective-permute-done((bf16[8,128,128]{2,1,0:T(8,128)(2,1)S(1)}, bf16[8,128,128]{2,1,0:T(8,128)(2,1)S(1)}, u32[]{:S(2)}, u32[]{:S(2)}) %collective-permute-start.22) | collective-permute-done | bytes 262176 | tf_op jit(solution)/shard_map/ppermute | solution.py:23
  82.3 2.2 %collective-permute-done.23 = bf16[32,128,128]{2,1,0:T(8,128)(2,1)S(1)} collective-permute-done((bf16[32,128,128]{2,1,0:T(8,128)(2,1)S(1)}, bf16[32,128,128]{2,1,0:T(8,128)(2,1)S(1)}, u32[]{:S(2)}, u32[]{:S(2)}) %collective-permute-start.23) | collective-permute-done | bytes 1048608 | tf_op jit(solution)/shard_map/ppermute | solution.py:23
  84.7 3.1 %block_products.3 = (bf16[8,128,128]{2,1,0:T(8,128)(2,1)S(1)}, f32[8,128]{1,0:T(8,128)S(1)}) custom-call(s32[1216]{0:T(1024)S(1)} %get-tuple-element.29.left_ref, s32[1216]{0:T(1024)S(1)} %get-tuple-element.28.right_ref, s32[304]{0:T(512)S(1)} %convert_reduce_fusion.1.target_ref, s32[4]{0:T(128)S(1)} %select_reduce_fusion.1.bounds_ref, ...), custom_call_target="tpu_custom_call" | custom-call | flops 1073741824 | bytes 8388608 | tf_op jit(solution)/shard_map/block_products/pallas_call | solution.py:203
  88.2 5.1 %collective-permute-start.26 = (f32[8,128]{1,0:T(8,128)S(1)}, f32[8,128]{1,0:T(8,128)S(1)}, u32[]{:S(2)}, u32[]{:S(2)}) collective-permute-start(f32[8,128]{1,0:T(8,128)S(1)} %get-tuple-element.22), channel_id=1, source_target_pairs={{0,48},{16,32},{32,16},{48,0},{64,112},{80,96},{96,80},{112,64},{1... | collective-permute-start | bytes 12296 | tf_op jit(solution)/shard_map/ppermute | solution.py:23
  93.3 0.7 collective-permute-start.24
  94.0 1.5 %collective-permute-done.25 = f32[8,128]{1,0:T(8,128)S(1)} collective-permute-done((f32[8,128]{1,0:T(8,128)S(1)}, f32[8,128]{1,0:T(8,128)S(1)}, u32[]{:S(2)}, u32[]{:S(2)}) %collective-permute-start.25) | collective-permute-done | bytes 4128 | tf_op jit(solution)/shard_map/ppermute | solution.py:23
  96.1 2.2 %collective-permute-start.29 = (f32[8,128]{1,0:T(8,128)S(1)}, f32[8,128]{1,0:T(8,128)S(1)}, u32[]{:S(2)}, u32[]{:S(2)}) collective-permute-start(f32[8,128]{1,0:T(8,128)S(1)} %add_add_fusion.2), channel_id=1, source_target_pairs={{0,192},{16,208},{32,224},{48,240},{64,128},{80,144},{96,160},{112... | collective-permute-start | bytes 12296 | tf_op jit(solution)/shard_map/ppermute | solution.py:23
  98.3 0.7 collective-permute-start.27
  99.0 1.6 %collective-permute-done.28 = f32[8,128]{1,0:T(8,128)S(1)} collective-permute-done((f32[8,128]{1,0:T(8,128)S(1)}, f32[8,128]{1,0:T(8,128)S(1)}, u32[]{:S(2)}, u32[]{:S(2)}) %collective-permute-start.28) | collective-permute-done | bytes 4128 | tf_op jit(solution)/shard_map/ppermute | solution.py:23
  100.9 1.0 collective-permute-done.27
  101.9 1.6 %collective-permute-start.31 = (f32[8,128]{1,0:T(8,128)S(1)}, f32[8,128]{1,0:T(8,128)S(1)}, u32[]{:S(2)}, u32[]{:S(2)}) collective-permute-start(f32[8,128]{1,0:T(8,128)S(1)} %add_add_fusion.1), channel_id=1, source_target_pairs={{0,2},{1,3},{2,0},{3,1},{4,6},{5,7},{6,4},{7,5},{8,10},{9,11},{10,... | collective-permute-start | bytes 12296 | tf_op jit(solution)/shard_map/ppermute | solution.py:23
  103.5 1.9 %collective-permute-start.32 = (f32[8,128]{1,0:T(8,128)S(1)}, f32[8,128]{1,0:T(8,128)S(1)}, u32[]{:S(2)}, u32[]{:S(2)}) collective-permute-start(f32[8,128]{1,0:T(8,128)S(1)} %add_add_fusion.1), channel_id=1, source_target_pairs={{0,3},{1,2},{2,1},{3,0},{4,7},{5,6},{6,5},{7,4},{8,11},{9,10},{10,... | collective-permute-start | bytes 12296 | tf_op jit(solution)/shard_map/ppermute | solution.py:23
  105.4 1.0 collective-permute-done.31
  106.5 2.5 %collective-permute-done.32 = f32[8,128]{1,0:T(8,128)S(1)} collective-permute-done((f32[8,128]{1,0:T(8,128)S(1)}, f32[8,128]{1,0:T(8,128)S(1)}, u32[]{:S(2)}, u32[]{:S(2)}) %collective-permute-start.32) | collective-permute-done | bytes 4128 | tf_op jit(solution)/shard_map/ppermute | solution.py:23
  109.0 3.4 %collective-permute-start.33 = (f32[8,128]{1,0:T(8,128)S(1)}, f32[8,128]{1,0:T(8,128)S(1)}, u32[]{:S(2)}, u32[]{:S(2)}) collective-permute-start(f32[8,128]{1,0:T(8,128)S(1)} %add_add_fusion), channel_id=1, source_target_pairs={{0,4},{1,5},{2,6},{3,7},{4,0},{5,1},{6,2},{7,3},{8,12},{9,13},{10,... | collective-permute-start | bytes 12296 | tf_op jit(solution)/shard_map/ppermute | solution.py:23
  112.4 4.5 %block_products.4.second = bf16[12,128,128]{2,1,0:T(8,128)(2,1)S(1)} custom-call(s32[1216]{0:T(1024)S(1)} %get-tuple-element.29.left_ref, s32[1216]{0:T(1024)S(1)} %get-tuple-element.28.right_ref, s32[304]{0:T(512)S(1)} %convert_reduce_fusion.1.target_ref, s32[4]{0:T(128)S(1)} %select_reduce_fusion.1.bounds_ref, s32[32]{0:T(128)S(1)} %select_reduce_fusion.slot_ref, ...), custom_call_target="tpu_custom_call" | custom-call | flops 1610612736 | bytes 8388608 | tf_op jit(solution)/shard_map/block_products/pallas_call | solution.py:203
  117.1 5.6 %block_products.5 = bf16[32,128,128]{2,1,0:T(8,128)(2,1)} custom-call(s32[1216]{0:T(1024)S(1)} %get-tuple-element.29.left_ref, s32[1216]{0:T(1024)S(1)} %get-tuple-element.28.right_ref, s32[304]{0:T(512)S(1)} %convert_reduce_fusion.1.target_ref, s32[4]{0:T(128)S(1)} %select_reduce_fusion.1.bounds_ref, s32[32]{0:T(128)S(1)} %select_reduce_fusion.slot_ref, ...), custom_call_target="tpu_custom_call" | custom-call | flops 1610612736 | bytes 8388608 | tf_op jit(solution)/shard_map/block_products/pallas_call | solution.py:203
  (97 shorter events, 7.0 us)
Async XLA Ops:
  0.6 9.8 %copy-start.5 = (s32[1,1,2,32]{3,2,1,0:T(2,128)S(1)}, s32[1,1,2,32]{3,2,1,0:T(2,128)}, u32[]{:S(2)}) copy-start(s32[1,1,2,32]{3,2,1,0:T(2,128)} %param.7) | copy-start | bytes 772
  0.7 9.8 %copy-start.2 = (s32[1,1,4,3,256]{4,2,3,1,0:T(4,128)S(1)}, s32[1,1,4,3,256]{4,2,3,1,0:T(4,128)}, u32[]{:S(2)}) copy-start(s32[1,1,4,3,256]{4,2,3,1,0:T(4,128)} %param.8) | copy-start | bytes 36868
  0.7 10.7 %copy-start.3 = (s32[4]{0:T(128)S(1)}, s32[4]{0:T(128)}, u32[]{:S(2)}) copy-start(s32[4]{0:T(128)} %param.9) | copy-start | bytes 52
  2.4 10.1 %collective-permute-start.2 = (bf16[2,2,2,128,128]{4,3,2,1,0:T(8,128)(2,1)S(1)}, bf16[2,2,2,128,128]{4,3,2,1,0:T(8,128)(2,1)}, u32[]{:S(2)}, u32[]{:S(2)}) collective-permute-start(bf16[2,2,2,128,128]{4,3,2,1,0:T(8,128)(2,1)S(1)} %get-tuple-element.45), channel_id=1, source_target_pairs={{0,4},{1,5},{2,6},{3,7},{4,0},{5,1},{6,2},{7,3},{8,12},{9,13},{10,... | collective-permute-start | bytes 786440 | tf_op jit(solution)/shard_map/ppermute | solution.py:23
  4.7 12.4 %collective-permute-start.1 = (bf16[2,2,2,128,128]{4,3,2,1,0:T(8,128)(2,1)S(1)}, bf16[2,2,2,128,128]{4,3,2,1,0:T(8,128)(2,1)S(1)}, u32[]{:S(2)}, u32[]{:S(2)}) collective-permute-start(bf16[2,2,2,128,128]{4,3,2,1,0:T(8,128)(2,1)S(1)} %get-tuple-element.46), channel_id=1, source_target_pairs={{0,8},{1,9},{2,10},{3,11},{4,12},{5,13},{6,14},{7,15},{8,0},{9,1},... | collective-permute-start | bytes 786440 | tf_op jit(solution)/shard_map/ppermute | solution.py:23
  5.4 13.1 %collective-permute-start = (bf16[2,2,2,128,128]{4,3,2,1,0:T(8,128)(2,1)S(1)}, bf16[2,2,2,128,128]{4,3,2,1,0:T(8,128)(2,1)S(1)}, u32[]{:S(2)}, u32[]{:S(2)}) collective-permute-start(bf16[2,2,2,128,128]{4,3,2,1,0:T(8,128)(2,1)S(1)} %get-tuple-element.47), channel_id=1, source_target_pairs={{0,12},{1,13},{2,14},{3,15},{4,8},{5,9},{6,10},{7,11},{8,4},{9,5},... | collective-permute-start | bytes 786440 | tf_op jit(solution)/shard_map/ppermute | solution.py:23
  6.3 17.3 %collective-permute-start.11 = (bf16[2,2,2,128,128]{4,3,2,1,0:T(8,128)(2,1)S(1)}, bf16[2,2,2,128,128]{4,3,2,1,0:T(8,128)(2,1)S(1)}, u32[]{:S(2)}, u32[]{:S(2)}) collective-permute-start(bf16[2,2,2,128,128]{4,3,2,1,0:T(8,128)(2,1)S(1)} %get-tuple-element.42), channel_id=1, source_target_pairs={{0,64},{16,80},{32,96},{48,112},{64,0},{80,16},{96,32},{112,48},{1... | collective-permute-start | bytes 786440 | tf_op jit(solution)/shard_map/ppermute | solution.py:23
  7.5 16.8 %collective-permute-start.10 = (bf16[2,2,2,128,128]{4,3,2,1,0:T(8,128)(2,1)S(1)}, bf16[2,2,2,128,128]{4,3,2,1,0:T(8,128)(2,1)S(1)}, u32[]{:S(2)}, u32[]{:S(2)}) collective-permute-start(bf16[2,2,2,128,128]{4,3,2,1,0:T(8,128)(2,1)S(1)} %get-tuple-element.43), channel_id=1, source_target_pairs={{0,128},{16,144},{32,160},{48,176},{64,192},{80,208},{96,224},{112... | collective-permute-start | bytes 786440 | tf_op jit(solution)/shard_map/ppermute | solution.py:23
  12.5 12.9 %collective-permute-start.9 = (bf16[2,2,2,128,128]{4,3,2,1,0:T(8,128)(2,1)S(1)}, bf16[2,2,2,128,128]{4,3,2,1,0:T(8,128)(2,1)S(1)}, u32[]{:S(2)}, u32[]{:S(2)}) collective-permute-start(bf16[2,2,2,128,128]{4,3,2,1,0:T(8,128)(2,1)S(1)} %get-tuple-element.40), channel_id=1, source_target_pairs={{0,192},{16,208},{32,224},{48,240},{64,128},{80,144},{96,160},{112... | collective-permute-start | bytes 786440 | tf_op jit(solution)/shard_map/ppermute | solution.py:23
  18.9 8.7 %collective-permute-start.3 = (bf16[4,128,128]{2,1,0:T(8,128)(2,1)S(1)}, bf16[4,128,128]{2,1,0:T(8,128)(2,1)S(1)}, u32[]{:S(2)}, u32[]{:S(2)}) collective-permute-start(bf16[4,128,128]{2,1,0:T(8,128)(2,1)S(1)} %get-tuple-element.50), channel_id=1, source_target_pairs={{0,3},{1,2},{2,1},{3,0},{4,7},{5,6},{6,5},{7,4},{8,11},{9,10},{10,... | collective-permute-start | bytes 393224 | tf_op jit(solution)/shard_map/ppermute | solution.py:23
  23.6 8.8 %collective-permute-start.4 = (bf16[4,128,128]{2,1,0:T(8,128)(2,1)S(1)}, bf16[4,128,128]{2,1,0:T(8,128)(2,1)S(1)}, u32[]{:S(2)}, u32[]{:S(2)}) collective-permute-start(bf16[4,128,128]{2,1,0:T(8,128)(2,1)S(1)} %get-tuple-element.49), channel_id=1, source_target_pairs={{0,2},{1,3},{2,0},{3,1},{4,6},{5,7},{6,4},{7,5},{8,10},{9,11},{10,... | collective-permute-start | bytes 393224 | tf_op jit(solution)/shard_map/ppermute | solution.py:23
  23.6 11.8 %copy-start.4 = (s32[4]{0:T(128)S(1)}, s32[4]{0:T(128)}, u32[]{:S(2)}) copy-start(s32[4]{0:T(128)} %constant.93.clone) | copy-start | bytes 52
  23.6 8.8 %collective-permute-start.5 = (bf16[4,128,128]{2,1,0:T(8,128)(2,1)S(1)}, bf16[4,128,128]{2,1,0:T(8,128)(2,1)S(1)}, u32[]{:S(2)}, u32[]{:S(2)}) collective-permute-start(bf16[4,128,128]{2,1,0:T(8,128)(2,1)S(1)} %get-tuple-element.48), channel_id=1, source_target_pairs={{0,1},{1,0},{2,3},{3,2},{4,5},{5,4},{6,7},{7,6},{8,9},{9,8},{10,11... | collective-permute-start | bytes 393224 | tf_op jit(solution)/shard_map/ppermute | solution.py:23
  25.8 17.7 %collective-permute-start.12 = (bf16[4,2,128,128]{3,2,1,0:T(8,128)(2,1)S(1)}, bf16[4,2,128,128]{3,2,1,0:T(8,128)(2,1)S(1)}, u32[]{:S(2)}, u32[]{:S(2)}) collective-permute-start(bf16[4,2,128,128]{3,2,1,0:T(8,128)(2,1)S(1)} %dynamic-slice_bitcast_fusion), channel_id=1, source_target_pairs={{0,16},{16,0},{32,48},{48,32},{64,80},{80,64},{96,112},{112,96},{1... | collective-permute-start | bytes 786440 | tf_op jit(solution)/shard_map/ppermute | solution.py:23
  32.6 8.3 %collective-permute-start.8 = (bf16[4,128,128]{2,1,0:T(8,128)(2,1)S(1)}, bf16[4,128,128]{2,1,0:T(8,128)(2,1)S(1)}, u32[]{:S(2)}, u32[]{:S(2)}) collective-permute-start(bf16[4,128,128]{2,1,0:T(8,128)(2,1)S(1)} %get-tuple-element.35), channel_id=1, source_target_pairs={{0,3},{1,2},{2,1},{3,0},{4,7},{5,6},{6,5},{7,4},{8,11},{9,10},{10,... | collective-permute-start | bytes 393224 | tf_op jit(solution)/shard_map/ppermute | solution.py:23
  35.6 10.1 %collective-permute-start.7 = (bf16[4,128,128]{2,1,0:T(8,128)(2,1)S(1)}, bf16[4,128,128]{2,1,0:T(8,128)(2,1)S(1)}, u32[]{:S(2)}, u32[]{:S(2)}) collective-permute-start(bf16[4,128,128]{2,1,0:T(8,128)(2,1)S(1)} %get-tuple-element.35), channel_id=1, source_target_pairs={{0,2},{1,3},{2,0},{3,1},{4,6},{5,7},{6,4},{7,5},{8,10},{9,11},{10,... | collective-permute-start | bytes 393224 | tf_op jit(solution)/shard_map/ppermute | solution.py:23
  35.7 10.0 %collective-permute-start.6 = (bf16[4,128,128]{2,1,0:T(8,128)(2,1)S(1)}, bf16[4,128,128]{2,1,0:T(8,128)(2,1)S(1)}, u32[]{:S(2)}, u32[]{:S(2)}) collective-permute-start(bf16[4,128,128]{2,1,0:T(8,128)(2,1)S(1)} %get-tuple-element.35), channel_id=1, source_target_pairs={{0,1},{1,0},{2,3},{3,2},{4,5},{5,4},{6,7},{7,6},{8,9},{9,8},{10,11... | collective-permute-start | bytes 393224 | tf_op jit(solution)/shard_map/ppermute | solution.py:23
  37.3 8.5 %collective-permute-start.13 = (bf16[4,128,128]{2,1,0:T(8,128)(2,1)S(1)}, bf16[4,128,128]{2,1,0:T(8,128)(2,1)S(1)}, u32[]{:S(2)}, u32[]{:S(2)}) collective-permute-start(bf16[4,128,128]{2,1,0:T(8,128)(2,1)S(1)} %get-tuple-element.35), channel_id=1, source_target_pairs={{0,4},{1,5},{2,6},{3,7},{4,0},{5,1},{6,2},{7,3},{8,12},{9,13},{10,... | collective-permute-start | bytes 393224 | tf_op jit(solution)/shard_map/ppermute | solution.py:23
  40.9 6.5 %collective-permute-start.14 = (bf16[4,128,128]{2,1,0:T(8,128)(2,1)S(1)}, bf16[4,128,128]{2,1,0:T(8,128)(2,1)S(1)}, u32[]{:S(2)}, u32[]{:S(2)}) collective-permute-start(bf16[4,128,128]{2,1,0:T(8,128)(2,1)S(1)} %get-tuple-element.35), channel_id=1, source_target_pairs={{0,8},{1,9},{2,10},{3,11},{4,12},{5,13},{6,14},{7,15},{8,0},{9,1},... | collective-permute-start | bytes 393224 | tf_op jit(solution)/shard_map/ppermute | solution.py:23
  43.5 5.3 %collective-permute-start.15 = (bf16[4,128,128]{2,1,0:T(8,128)(2,1)S(1)}, bf16[4,128,128]{2,1,0:T(8,128)(2,1)S(1)}, u32[]{:S(2)}, u32[]{:S(2)}) collective-permute-start(bf16[4,128,128]{2,1,0:T(8,128)(2,1)S(1)} %get-tuple-element.35), channel_id=1, source_target_pairs={{0,12},{1,13},{2,14},{3,15},{4,8},{5,9},{6,10},{7,11},{8,4},{9,5},... | collective-permute-start | bytes 393224 | tf_op jit(solution)/shard_map/ppermute | solution.py:23
  48.8 11.3 %collective-permute-start.16 = (bf16[4,2,128,128]{3,2,1,0:T(8,128)(2,1)S(1)}, bf16[4,2,128,128]{3,2,1,0:T(8,128)(2,1)S(1)}, u32[]{:S(2)}, u32[]{:S(2)}) collective-permute-start(bf16[4,2,128,128]{3,2,1,0:T(8,128)(2,1)S(1)} %bitcast_select_fusion), channel_id=1, source_target_pairs={{0,32},{16,48},{32,0},{48,16},{64,96},{80,112},{96,64},{112,80},{1... | collective-permute-start | bytes 786440 | tf_op jit(solution)/shard_map/ppermute | solution.py:23
  54.8 12.5 %collective-permute-start.17 = (bf16[12,128,128]{2,1,0:T(8,128)(2,1)S(1)}, bf16[12,128,128]{2,1,0:T(8,128)(2,1)S(1)}, u32[]{:S(2)}, u32[]{:S(2)}) collective-permute-start(bf16[12,128,128]{2,1,0:T(8,128)(2,1)S(1)} %pad_maximum_fusion.1), channel_id=1, source_target_pairs={{0,4},{1,5},{2,6},{3,7},{4,0},{5,1},{6,2},{7,3},{8,12},{9,13},{10,... | collective-permute-start | bytes 1179656 | tf_op jit(solution)/shard_map/ppermute | solution.py:23
  58.2 23.8 %collective-permute-start.18 = (bf16[12,128,128]{2,1,0:T(8,128)(2,1)S(1)}, bf16[12,128,128]{2,1,0:T(8,128)(2,1)S(1)}, u32[]{:S(2)}, u32[]{:S(2)}) collective-permute-start(bf16[12,128,128]{2,1,0:T(8,128)(2,1)S(1)} %pad_maximum_fusion.1), channel_id=1, source_target_pairs={{0,8},{1,9},{2,10},{3,11},{4,12},{5,13},{6,14},{7,15},{8,0},{9,1},... | collective-permute-start | bytes 1179656 | tf_op jit(solution)/shard_map/ppermute | solution.py:23
  58.6 23.5 %collective-permute-start.19 = (bf16[12,128,128]{2,1,0:T(8,128)(2,1)S(1)}, bf16[12,128,128]{2,1,0:T(8,128)(2,1)S(1)}, u32[]{:S(2)}, u32[]{:S(2)}) collective-permute-start(bf16[12,128,128]{2,1,0:T(8,128)(2,1)S(1)} %pad_maximum_fusion.1), channel_id=1, source_target_pairs={{0,12},{1,13},{2,14},{3,15},{4,8},{5,9},{6,10},{7,11},{8,4},{9,5},... | collective-permute-start | bytes 1179656 | tf_op jit(solution)/shard_map/ppermute | solution.py:23
  67.2 6.4 %collective-permute-start.20 = (bf16[8,128,128]{2,1,0:T(8,128)(2,1)S(1)}, bf16[8,128,128]{2,1,0:T(8,128)(2,1)S(1)}, u32[]{:S(2)}, u32[]{:S(2)}) collective-permute-start(bf16[8,128,128]{2,1,0:T(8,128)(2,1)S(1)} %bitcast.93), channel_id=1, source_target_pairs={{0,64},{16,80},{32,96},{48,112},{64,0},{80,16},{96,32},{112,48},{1... | collective-permute-start | bytes 786440 | tf_op jit(solution)/shard_map/ppermute | solution.py:23
  68.8 10.2 %collective-permute-start.21 = (bf16[8,128,128]{2,1,0:T(8,128)(2,1)S(1)}, bf16[8,128,128]{2,1,0:T(8,128)(2,1)S(1)}, u32[]{:S(2)}, u32[]{:S(2)}) collective-permute-start(bf16[8,128,128]{2,1,0:T(8,128)(2,1)S(1)} %bitcast.94), channel_id=1, source_target_pairs={{0,128},{16,144},{32,160},{48,176},{64,192},{80,208},{96,224},{112... | collective-permute-start | bytes 786440 | tf_op jit(solution)/shard_map/ppermute | solution.py:23
  71.7 10.0 %collective-permute-start.22 = (bf16[8,128,128]{2,1,0:T(8,128)(2,1)S(1)}, bf16[8,128,128]{2,1,0:T(8,128)(2,1)S(1)}, u32[]{:S(2)}, u32[]{:S(2)}) collective-permute-start(bf16[8,128,128]{2,1,0:T(8,128)(2,1)S(1)} %bitcast.95), channel_id=1, source_target_pairs={{0,192},{16,208},{32,224},{48,240},{64,128},{80,144},{96,160},{112... | collective-permute-start | bytes 786440 | tf_op jit(solution)/shard_map/ppermute | solution.py:23
  81.8 2.7 %collective-permute-start.23 = (bf16[32,128,128]{2,1,0:T(8,128)(2,1)S(1)}, bf16[32,128,128]{2,1,0:T(8,128)(2,1)S(1)}, u32[]{:S(2)}, u32[]{:S(2)}) collective-permute-start(bf16[32,128,128]{2,1,0:T(8,128)(2,1)S(1)} %pad_maximum_fusion), channel_id=1, source_target_pairs={{0,16},{16,0},{32,48},{48,32},{64,80},{80,64},{96,112},{112,96},{1... | collective-permute-start | bytes 3145736 | tf_op jit(solution)/shard_map/ppermute | solution.py:23
  82.1 2.6 %copy-start = (bf16[1,1,32,128,128]{4,3,2,1,0:T(8,128)(2,1)S(1)}, bf16[1,1,32,128,128]{4,3,2,1,0:T(8,128)(2,1)}, u32[]{:S(2)}) copy-start(bf16[1,1,32,128,128]{4,3,2,1,0:T(8,128)(2,1)} %param.6) | copy-start | bytes 3145732
  82.1 2.6 %copy-start.1 = (s32[1,1,32]{2,1,0:T(1,128)S(1)}, s32[1,1,32]{2,1,0:T(1,128)}, u32[]{:S(2)}) copy-start(s32[1,1,32]{2,1,0:T(1,128)} %param.10) | copy-start | bytes 388
  87.9 7.6 %collective-permute-start.25 = (f32[8,128]{1,0:T(8,128)S(1)}, f32[8,128]{1,0:T(8,128)S(1)}, u32[]{:S(2)}, u32[]{:S(2)}) collective-permute-start(f32[8,128]{1,0:T(8,128)S(1)} %get-tuple-element.22), channel_id=1, source_target_pairs={{0,32},{16,48},{32,0},{48,16},{64,96},{80,112},{96,64},{112,80},{1... | collective-permute-start | bytes 12296 | tf_op jit(solution)/shard_map/ppermute | solution.py:23
  88.2 7.2 %collective-permute-start.26 = (f32[8,128]{1,0:T(8,128)S(1)}, f32[8,128]{1,0:T(8,128)S(1)}, u32[]{:S(2)}, u32[]{:S(2)}) collective-permute-start(f32[8,128]{1,0:T(8,128)S(1)} %get-tuple-element.22), channel_id=1, source_target_pairs={{0,48},{16,32},{32,16},{48,0},{64,112},{80,96},{96,80},{112,64},{1... | collective-permute-start | bytes 12296 | tf_op jit(solution)/shard_map/ppermute | solution.py:23
  93.3 2.1 %collective-permute-start.24 = (f32[8,128]{1,0:T(8,128)S(1)}, f32[8,128]{1,0:T(8,128)S(1)}, u32[]{:S(2)}, u32[]{:S(2)}) collective-permute-start(f32[8,128]{1,0:T(8,128)S(1)} %get-tuple-element.22), channel_id=1, source_target_pairs={{0,16},{16,0},{32,48},{48,32},{64,80},{80,64},{96,112},{112,96},{1... | collective-permute-start | bytes 12296 | tf_op jit(solution)/shard_map/ppermute | solution.py:23
  95.5 5.2 %collective-permute-start.28 = (f32[8,128]{1,0:T(8,128)S(1)}, f32[8,128]{1,0:T(8,128)S(1)}, u32[]{:S(2)}, u32[]{:S(2)}) collective-permute-start(f32[8,128]{1,0:T(8,128)S(1)} %add_add_fusion.2), channel_id=1, source_target_pairs={{0,128},{16,144},{32,160},{48,176},{64,192},{80,208},{96,224},{112... | collective-permute-start | bytes 12296 | tf_op jit(solution)/shard_map/ppermute | solution.py:23
  96.1 4.8 %collective-permute-start.29 = (f32[8,128]{1,0:T(8,128)S(1)}, f32[8,128]{1,0:T(8,128)S(1)}, u32[]{:S(2)}, u32[]{:S(2)}) collective-permute-start(f32[8,128]{1,0:T(8,128)S(1)} %add_add_fusion.2), channel_id=1, source_target_pairs={{0,192},{16,208},{32,224},{48,240},{64,128},{80,144},{96,160},{112... | collective-permute-start | bytes 12296 | tf_op jit(solution)/shard_map/ppermute | solution.py:23
  98.3 3.6 %collective-permute-start.27 = (f32[8,128]{1,0:T(8,128)S(1)}, f32[8,128]{1,0:T(8,128)S(1)}, u32[]{:S(2)}, u32[]{:S(2)}) collective-permute-start(f32[8,128]{1,0:T(8,128)S(1)} %add_add_fusion.2), channel_id=1, source_target_pairs={{0,64},{16,80},{32,96},{48,112},{64,0},{80,16},{96,32},{112,48},{1... | collective-permute-start | bytes 12296 | tf_op jit(solution)/shard_map/ppermute | solution.py:23
  101.9 4.5 %collective-permute-start.31 = (f32[8,128]{1,0:T(8,128)S(1)}, f32[8,128]{1,0:T(8,128)S(1)}, u32[]{:S(2)}, u32[]{:S(2)}) collective-permute-start(f32[8,128]{1,0:T(8,128)S(1)} %add_add_fusion.1), channel_id=1, source_target_pairs={{0,2},{1,3},{2,0},{3,1},{4,6},{5,7},{6,4},{7,5},{8,10},{9,11},{10,... | collective-permute-start | bytes 12296 | tf_op jit(solution)/shard_map/ppermute | solution.py:23
  103.5 5.4 %collective-permute-start.32 = (f32[8,128]{1,0:T(8,128)S(1)}, f32[8,128]{1,0:T(8,128)S(1)}, u32[]{:S(2)}, u32[]{:S(2)}) collective-permute-start(f32[8,128]{1,0:T(8,128)S(1)} %add_add_fusion.1), channel_id=1, source_target_pairs={{0,3},{1,2},{2,1},{3,0},{4,7},{5,6},{6,5},{7,4},{8,11},{9,10},{10,... | collective-permute-start | bytes 12296 | tf_op jit(solution)/shard_map/ppermute | solution.py:23
  105.4 3.6 %collective-permute-start.30 = (f32[8,128]{1,0:T(8,128)S(1)}, f32[8,128]{1,0:T(8,128)S(1)}, u32[]{:S(2)}, u32[]{:S(2)}) collective-permute-start(f32[8,128]{1,0:T(8,128)S(1)} %add_add_fusion.1), channel_id=1, source_target_pairs={{0,1},{1,0},{2,3},{3,2},{4,5},{5,4},{6,7},{7,6},{8,9},{9,8},{10,11... | collective-permute-start | bytes 12296 | tf_op jit(solution)/shard_map/ppermute | solution.py:23
  109.0 7.9 %collective-permute-start.33 = (f32[8,128]{1,0:T(8,128)S(1)}, f32[8,128]{1,0:T(8,128)S(1)}, u32[]{:S(2)}, u32[]{:S(2)}) collective-permute-start(f32[8,128]{1,0:T(8,128)S(1)} %add_add_fusion), channel_id=1, source_target_pairs={{0,4},{1,5},{2,6},{3,7},{4,0},{5,1},{6,2},{7,3},{8,12},{9,13},{10,... | collective-permute-start | bytes 12296 | tf_op jit(solution)/shard_map/ppermute | solution.py:23
  117.0 5.7 %collective-permute-start.34 = (f32[8,128]{1,0:T(8,128)S(1)}, f32[8,128]{1,0:T(8,128)S(1)}, u32[]{:S(2)}, u32[]{:S(2)}) collective-permute-start(f32[8,128]{1,0:T(8,128)S(1)} %add.235), channel_id=1, source_target_pairs={{0,8},{1,9},{2,10},{3,11},{4,12},{5,13},{6,14},{7,15},{8,0},{9,1},... | collective-permute-start | bytes 12296 | tf_op jit(solution)/shard_map/ppermute | solution.py:23

commit v4 on v3

--- a/solution.py
+++ b/solution.py
@@ -221,17 +221,17 @@
     scalars = (left, right, target, bounds, slot_of, branch[0, 0], diag)
     shapes = (jax.ShapeDtypeStruct((FIRST, BS, BS), jnp.bfloat16), jax.ShapeDtypeStruct((8, BS), jnp.float32))
     first, value = products(first_kernel, FIRST, shapes, (FIRST + 1, 0, 0), scalars, arrays)
-    for axis, low, high in (("row", 1, 2), ("row", 4, 8), ("col", 1, 2)):
+    for axis, low, high in (("row", 4, 8), ("col", 1, 2), ("col", 4, 8)):
         one, two, three = (swap(value, axis, b) for b in (low, high, low + high))
         value = (value + one) + (two + three)
     scalars = scalars[:6]
     value, own = lax.optimization_barrier((value, own))
     arrays = arrays[:2] + (own,)
-    other = swap(value, "col", 4)
+    other = swap(value, "row", 1)
     shapes = jax.ShapeDtypeStruct((SECOND - FIRST, BS, BS), jnp.bfloat16)
     second = products(second_kernel, SECOND - FIRST, shapes, (SECOND - FIRST + 1,), scalars, arrays)
     value, second = lax.optimization_barrier((value + other, second))
-    other = swap(value, "col", 8)
+    other = swap(value, "row", 2)
     shapes = jax.ShapeDtypeStruct((NO, BS, BS), jnp.bfloat16)
     out = products(third_kernel, NO - SECOND, shapes, (NO - SECOND + 1,), scalars, arrays + (first, second))
     traces = jnp.sum(value + other, axis=1)[:2] * SCALE

time: 125 us -> 123 us (0.984)
  starting transfers between devices: 60.5 us -> 58.7 us
    ppermute x35, starting transfers between devices: 60.5 us -> 58.7 us  [swap(): return lax.ppermute(value, axis, [(i, i ^ bit) for i in range(16)])]
where the time goes in v4:
time: 123 us; the launch traced here: 121 us
  starting transfers between devices  58.7 us (48%)
  waiting for transfers between devices  40 us (33%)
  Pallas kernels  14 us (11%)
  local copies, waits for them, and re-layouts  3.45 us (3%)
  other arithmetic  2.58 us (2%)
  matrix products  1.44 us (1%)
    ppermute x35, starting transfers between devices, swap(): return lax.ppermute(value, axis, [(i, i ^ bit) for i in range(16)])  58.7 us
    ppermute x35, waiting for transfers between devices, swap(): return lax.ppermute(value, axis, [(i, i ^ bit) for i in range(16)])  40 us
    pallas_call x3, Pallas kernels, products(): pl.pallas_call(kernel, out_shape=out_shape, in_specs=[smem] * len(scalars...  14 us
  transfers between devices with their start and end apart: 35, of which 21 were waited for; matrix products, arithmetic and copies ran while one was open for 4% of the time, Pallas kernels for 8%

profile of v4, /device:TPU:2, one launch (start us, length us, event | category | flops | bytes accessed | tf_op | source)
XLA Modules:
  0.0 121.4 jit_solution(1538870160033193192)
XLA Ops:
  0.7 1.7 %dynamic-slice_bitcast_fusion.4 = (bf16[2,2,2,128,128]{4,3,2,1,0:T(8,128)(2,1)S(1)}, bf16[1,2,2,2,128,128]{5,4,3,2,1,0:T(8,128)(2,1)S(1)}, bf16[2,2,2,128,128]{4...) fusion(bf16[2,2,4,2,128,128]{5,4,3,2,1,0:T(8,128)(2,1)} %bitcas, ...), kind=kLoop, calls=%fused_computation.19 | loop fusion | bytes 4194336 | tf_op jit(solution)/shard_map/jit(dynamic_index_in_dim)/squeeze | solution.py:27
  2.4 2.4 %collective-permute-start.2 = (bf16[2,2,2,128,128]{4,3,2,1,0:T(8,128)(2,1)S(1)}, bf16[2,2,2,128,128]{4,3,2,1,0:T(8,128)(2,1)}, u32[]{:S(2)}, u32[]{:S(2)}) collective-permute-start(bf16[2,2,2,128,128]{4,3,2,1,0:T(8,128)(2,1)S(1)} %get-tuple-element.45), channel_id=1, source_target_pairs={{0,4},{1,5},{2,6},{3,7},{4,0},{5,1},{6,2},{7,3},{8,12},{9,13},{10,... | collective-permute-start | bytes 786440 | tf_op jit(solution)/shard_map/ppermute | solution.py:23
  4.7 0.7 collective-permute-start.1
  5.4 0.9 collective-permute-start
  6.3 1.2 %collective-permute-start.11 = (bf16[2,2,2,128,128]{4,3,2,1,0:T(8,128)(2,1)S(1)}, bf16[2,2,2,128,128]{4,3,2,1,0:T(8,128)(2,1)S(1)}, u32[]{:S(2)}, u32[]{:S(2)}) collective-permute-start(bf16[2,2,2,128,128]{4,3,2,1,0:T(8,128)(2,1)S(1)} %get-tuple-element.42), channel_id=1, source_target_pairs={{0,64},{16,80},{32,96},{48,112},{64,0},{80,16},{96,32},{112,48},{1... | collective-permute-start | bytes 786440 | tf_op jit(solution)/shard_map/ppermute | solution.py:23
  7.5 2.9 %collective-permute-start.10 = (bf16[2,2,2,128,128]{4,3,2,1,0:T(8,128)(2,1)S(1)}, bf16[2,2,2,128,128]{4,3,2,1,0:T(8,128)(2,1)S(1)}, u32[]{:S(2)}, u32[]{:S(2)}) collective-permute-start(bf16[2,2,2,128,128]{4,3,2,1,0:T(8,128)(2,1)S(1)} %get-tuple-element.43), channel_id=1, source_target_pairs={{0,128},{16,144},{32,160},{48,176},{64,192},{80,208},{96,224},{112... | collective-permute-start | bytes 786440 | tf_op jit(solution)/shard_map/ppermute | solution.py:23
  11.5 0.9 fusion.3
  12.5 2.3 %collective-permute-start.9 = (bf16[2,2,2,128,128]{4,3,2,1,0:T(8,128)(2,1)S(1)}, bf16[2,2,2,128,128]{4,3,2,1,0:T(8,128)(2,1)S(1)}, u32[]{:S(2)}, u32[]{:S(2)}) collective-permute-start(bf16[2,2,2,128,128]{4,3,2,1,0:T(8,128)(2,1)S(1)} %get-tuple-element.40), channel_id=1, source_target_pairs={{0,192},{16,208},{32,224},{48,240},{64,128},{80,144},{96,160},{112... | collective-permute-start | bytes 786440 | tf_op jit(solution)/shard_map/ppermute | solution.py:23
  14.8 1.0 fusion.22
  15.8 1.4 %collective-permute-done.1 = bf16[2,2,2,128,128]{4,3,2,1,0:T(8,128)(2,1)S(1)} collective-permute-done((bf16[2,2,2,128,128]{4,3,2,1,0:T(8,128)(2,1)S(1)}, bf16[2,2,2,128,128]{4,3,2,1,0:T(8,128)(2,1)S(1)}, u32[]{:S(2)}, u32[]{:S(2)}) %collective-permute-start.1) | collective-permute-done | bytes 262176 | tf_op jit(solution)/shard_map/ppermute | solution.py:23
  17.2 1.3 %collective-permute-done = bf16[2,2,2,128,128]{4,3,2,1,0:T(8,128)(2,1)S(1)} collective-permute-done((bf16[2,2,2,128,128]{4,3,2,1,0:T(8,128)(2,1)S(1)}, bf16[2,2,2,128,128]{4,3,2,1,0:T(8,128)(2,1)S(1)}, u32[]{:S(2)}, u32[]{:S(2)}) %collective-permute-start) | collective-permute-done | bytes 262176 | tf_op jit(solution)/shard_map/ppermute | solution.py:23
  18.9 4.7 %collective-permute-start.3 = (bf16[4,128,128]{2,1,0:T(8,128)(2,1)S(1)}, bf16[4,128,128]{2,1,0:T(8,128)(2,1)S(1)}, u32[]{:S(2)}, u32[]{:S(2)}) collective-permute-start(bf16[4,128,128]{2,1,0:T(8,128)(2,1)S(1)} %get-tuple-element.50), channel_id=1, source_target_pairs={{0,3},{1,2},{2,1},{3,0},{4,7},{5,6},{6,5},{7,4},{8,11},{9,10},{10,... | collective-permute-start | bytes 393224 | tf_op jit(solution)/shard_map/ppermute | solution.py:23
  23.6 0.7 collective-permute-start.5
  24.3 1.1 collective-permute-done.9
  25.9 1.7 %collective-permute-done.3 = bf16[4,128,128]{2,1,0:T(8,128)(2,1)S(1)} collective-permute-done((bf16[4,128,128]{2,1,0:T(8,128)(2,1)S(1)}, bf16[4,128,128]{2,1,0:T(8,128)(2,1)S(1)}, u32[]{:S(2)}, u32[]{:S(2)}) %collective-permute-start.3) | collective-permute-done | bytes 131104 | tf_op jit(solution)/shard_map/ppermute | solution.py:23
  27.6 4.8 %collective-permute-done.4 = bf16[4,128,128]{2,1,0:T(8,128)(2,1)S(1)} collective-permute-done((bf16[4,128,128]{2,1,0:T(8,128)(2,1)S(1)}, bf16[4,128,128]{2,1,0:T(8,128)(2,1)S(1)}, u32[]{:S(2)}, u32[]{:S(2)}) %collective-permute-start.4) | collective-permute-done | bytes 131104 | tf_op jit(solution)/shard_map/ppermute | solution.py:23
  32.6 2.8 %collective-permute-start.8 = (bf16[4,128,128]{2,1,0:T(8,128)(2,1)S(1)}, bf16[4,128,128]{2,1,0:T(8,128)(2,1)S(1)}, u32[]{:S(2)}, u32[]{:S(2)}) collective-permute-start(bf16[4,128,128]{2,1,0:T(8,128)(2,1)S(1)} %get-tuple-element.35), channel_id=1, source_target_pairs={{0,3},{1,2},{2,1},{3,0},{4,7},{5,6},{6,5},{7,4},{8,11},{9,10},{10,... | collective-permute-start | bytes 393224 | tf_op jit(solution)/shard_map/ppermute | solution.py:23
  35.7 1.6 %collective-permute-start.6 = (bf16[4,128,128]{2,1,0:T(8,128)(2,1)S(1)}, bf16[4,128,128]{2,1,0:T(8,128)(2,1)S(1)}, u32[]{:S(2)}, u32[]{:S(2)}) collective-permute-start(bf16[4,128,128]{2,1,0:T(8,128)(2,1)S(1)} %get-tuple-element.35), channel_id=1, source_target_pairs={{0,1},{1,0},{2,3},{3,2},{4,5},{5,4},{6,7},{7,6},{8,9},{9,8},{10,11... | collective-permute-start | bytes 393224 | tf_op jit(solution)/shard_map/ppermute | solution.py:23
  37.3 3.2 %collective-permute-start.13 = (bf16[4,128,128]{2,1,0:T(8,128)(2,1)S(1)}, bf16[4,128,128]{2,1,0:T(8,128)(2,1)S(1)}, u32[]{:S(2)}, u32[]{:S(2)}) collective-permute-start(bf16[4,128,128]{2,1,0:T(8,128)(2,1)S(1)} %get-tuple-element.35), channel_id=1, source_target_pairs={{0,4},{1,5},{2,6},{3,7},{4,0},{5,1},{6,2},{7,3},{8,12},{9,13},{10,... | collective-permute-start | bytes 393224 | tf_op jit(solution)/shard_map/ppermute | solution.py:23
  40.9 2.5 %collective-permute-start.14 = (bf16[4,128,128]{2,1,0:T(8,128)(2,1)S(1)}, bf16[4,128,128]{2,1,0:T(8,128)(2,1)S(1)}, u32[]{:S(2)}, u32[]{:S(2)}) collective-permute-start(bf16[4,128,128]{2,1,0:T(8,128)(2,1)S(1)} %get-tuple-element.35), channel_id=1, source_target_pairs={{0,8},{1,9},{2,10},{3,11},{4,12},{5,13},{6,14},{7,15},{8,0},{9,1},... | collective-permute-start | bytes 393224 | tf_op jit(solution)/shard_map/ppermute | solution.py:23
  43.5 2.2 %collective-permute-start.15 = (bf16[4,128,128]{2,1,0:T(8,128)(2,1)S(1)}, bf16[4,128,128]{2,1,0:T(8,128)(2,1)S(1)}, u32[]{:S(2)}, u32[]{:S(2)}) collective-permute-start(bf16[4,128,128]{2,1,0:T(8,128)(2,1)S(1)} %get-tuple-element.35), channel_id=1, source_target_pairs={{0,12},{1,13},{2,14},{3,15},{4,8},{5,9},{6,10},{7,11},{8,4},{9,5},... | collective-permute-start | bytes 393224 | tf_op jit(solution)/shard_map/ppermute | solution.py:23
  45.8 1.6 %collective-permute-done.14 = bf16[4,128,128]{2,1,0:T(8,128)(2,1)S(1)} collective-permute-done((bf16[4,128,128]{2,1,0:T(8,128)(2,1)S(1)}, bf16[4,128,128]{2,1,0:T(8,128)(2,1)S(1)}, u32[]{:S(2)}, u32[]{:S(2)}) %collective-permute-start.14) | collective-permute-done | bytes 131104 | tf_op jit(solution)/shard_map/ppermute | solution.py:23
  47.4 1.4 %collective-permute-done.15 = bf16[4,128,128]{2,1,0:T(8,128)(2,1)S(1)} collective-permute-done((bf16[4,128,128]{2,1,0:T(8,128)(2,1)S(1)}, bf16[4,128,128]{2,1,0:T(8,128)(2,1)S(1)}, u32[]{:S(2)}, u32[]{:S(2)}) %collective-permute-start.15) | collective-permute-done | bytes 131104 | tf_op jit(solution)/shard_map/ppermute | solution.py:23
  48.8 5.9 %collective-permute-start.16 = (bf16[4,2,128,128]{3,2,1,0:T(8,128)(2,1)S(1)}, bf16[4,2,128,128]{3,2,1,0:T(8,128)(2,1)S(1)}, u32[]{:S(2)}, u32[]{:S(2)}) collective-permute-start(bf16[4,2,128,128]{3,2,1,0:T(8,128)(2,1)S(1)} %bitcast_select_fusion), channel_id=1, source_target_pairs={{0,32},{16,48},{32,0},{48,16},{64,96},{80,112},{96,64},{112,80},{1... | collective-permute-start | bytes 786440 | tf_op jit(solution)/shard_map/ppermute | solution.py:23
  54.8 3.3 %collective-permute-start.17 = (bf16[12,128,128]{2,1,0:T(8,128)(2,1)S(1)}, bf16[12,128,128]{2,1,0:T(8,128)(2,1)S(1)}, u32[]{:S(2)}, u32[]{:S(2)}) collective-permute-start(bf16[12,128,128]{2,1,0:T(8,128)(2,1)S(1)} %pad_maximum_fusion.1), channel_id=1, source_target_pairs={{0,4},{1,5},{2,6},{3,7},{4,0},{5,1},{6,2},{7,3},{8,12},{9,13},{10,... | collective-permute-start | bytes 1179656 | tf_op jit(solution)/shard_map/ppermute | solution.py:23
  58.6 1.2 collective-permute-start.19
  60.2 7.0 %collective-permute-done.17 = bf16[12,128,128]{2,1,0:T(8,128)(2,1)S(1)} collective-permute-done((bf16[12,128,128]{2,1,0:T(8,128)(2,1)S(1)}, bf16[12,128,128]{2,1,0:T(8,128)(2,1)S(1)}, u32[]{:S(2)}, u32[]{:S(2)}) %collective-permute-start.17) | collective-permute-done | bytes 393248 | tf_op jit(solution)/shard_map/ppermute | solution.py:23
  67.2 1.6 %collective-permute-start.20 = (bf16[8,128,128]{2,1,0:T(8,128)(2,1)S(1)}, bf16[8,128,128]{2,1,0:T(8,128)(2,1)S(1)}, u32[]{:S(2)}, u32[]{:S(2)}) collective-permute-start(bf16[8,128,128]{2,1,0:T(8,128)(2,1)S(1)} %bitcast.93), channel_id=1, source_target_pairs={{0,64},{16,80},{32,96},{48,112},{64,0},{80,16},{96,32},{112,48},{1... | collective-permute-start | bytes 786440 | tf_op jit(solution)/shard_map/ppermute | solution.py:23
  68.8 2.9 %collective-permute-start.21 = (bf16[8,128,128]{2,1,0:T(8,128)(2,1)S(1)}, bf16[8,128,128]{2,1,0:T(8,128)(2,1)S(1)}, u32[]{:S(2)}, u32[]{:S(2)}) collective-permute-start(bf16[8,128,128]{2,1,0:T(8,128)(2,1)S(1)} %bitcast.94), channel_id=1, source_target_pairs={{0,128},{16,144},{32,160},{48,176},{64,192},{80,208},{96,224},{112... | collective-permute-start | bytes 786440 | tf_op jit(solution)/shard_map/ppermute | solution.py:23
  72.1 1.5 %collective-permute-done.20 = bf16[8,128,128]{2,1,0:T(8,128)(2,1)S(1)} collective-permute-done((bf16[8,128,128]{2,1,0:T(8,128)(2,1)S(1)}, bf16[8,128,128]{2,1,0:T(8,128)(2,1)S(1)}, u32[]{:S(2)}, u32[]{:S(2)}) %collective-permute-start.20) | collective-permute-done | bytes 262176 | tf_op jit(solution)/shard_map/ppermute | solution.py:23
  73.6 5.4 %collective-permute-done.21 = bf16[8,128,128]{2,1,0:T(8,128)(2,1)S(1)} collective-permute-done((bf16[8,128,128]{2,1,0:T(8,128)(2,1)S(1)}, bf16[8,128,128]{2,1,0:T(8,128)(2,1)S(1)}, u32[]{:S(2)}, u32[]{:S(2)}) %collective-permute-start.21) | collective-permute-done | bytes 262176 | tf_op jit(solution)/shard_map/ppermute | solution.py:23
  79.0 2.7 %collective-permute-done.22 = bf16[8,128,128]{2,1,0:T(8,128)(2,1)S(1)} collective-permute-done((bf16[8,128,128]{2,1,0:T(8,128)(2,1)S(1)}, bf16[8,128,128]{2,1,0:T(8,128)(2,1)S(1)}, u32[]{:S(2)}, u32[]{:S(2)}) %collective-permute-start.22) | collective-permute-done | bytes 262176 | tf_op jit(solution)/shard_map/ppermute | solution.py:23
  82.3 2.2 %collective-permute-done.23 = bf16[32,128,128]{2,1,0:T(8,128)(2,1)S(1)} collective-permute-done((bf16[32,128,128]{2,1,0:T(8,128)(2,1)S(1)}, bf16[32,128,128]{2,1,0:T(8,128)(2,1)S(1)}, u32[]{:S(2)}, u32[]{:S(2)}) %collective-permute-start.23) | collective-permute-done | bytes 1048608 | tf_op jit(solution)/shard_map/ppermute | solution.py:23
  84.7 3.8 %block_products.3 = (bf16[8,128,128]{2,1,0:T(8,128)(2,1)S(1)}, f32[8,128]{1,0:T(8,128)S(1)}) custom-call(s32[1216]{0:T(1024)S(1)} %get-tuple-element.29.left_ref, s32[1216]{0:T(1024)S(1)} %get-tuple-element.28.right_ref, s32[304]{0:T(512)S(1)} %convert_reduce_fusion.1.target_ref, s32[4]{0:T(128)S(1)} %select_reduce_fusion.1.bounds_ref, ...), custom_call_target="tpu_custom_call" | custom-call | flops 1073741824 | bytes 8388608 | tf_op jit(solution)/shard_map/block_products/pallas_call | solution.py:203
  88.7 2.1 %collective-permute-start.26 = (f32[8,128]{1,0:T(8,128)S(1)}, f32[8,128]{1,0:T(8,128)S(1)}, u32[]{:S(2)}, u32[]{:S(2)}) collective-permute-start(f32[8,128]{1,0:T(8,128)S(1)} %get-tuple-element.22), channel_id=1, source_target_pairs={{0,192},{16,208},{32,224},{48,240},{64,128},{80,144},{96,160},{112... | collective-permute-start | bytes 12296 | tf_op jit(solution)/shard_map/ppermute | solution.py:23
  90.7 1.4 %collective-permute-start.24 = (f32[8,128]{1,0:T(8,128)S(1)}, f32[8,128]{1,0:T(8,128)S(1)}, u32[]{:S(2)}, u32[]{:S(2)}) collective-permute-start(f32[8,128]{1,0:T(8,128)S(1)} %get-tuple-element.22), channel_id=1, source_target_pairs={{0,64},{16,80},{32,96},{48,112},{64,0},{80,16},{96,32},{112,48},{1... | collective-permute-start | bytes 12296 | tf_op jit(solution)/shard_map/ppermute | solution.py:23
  92.1 1.6 %collective-permute-done.25 = f32[8,128]{1,0:T(8,128)S(1)} collective-permute-done((f32[8,128]{1,0:T(8,128)S(1)}, f32[8,128]{1,0:T(8,128)S(1)}, u32[]{:S(2)}, u32[]{:S(2)}) %collective-permute-start.25) | collective-permute-done | bytes 4128 | tf_op jit(solution)/shard_map/ppermute | solution.py:23
  94.3 1.9 %collective-permute-start.29 = (f32[8,128]{1,0:T(8,128)S(1)}, f32[8,128]{1,0:T(8,128)S(1)}, u32[]{:S(2)}, u32[]{:S(2)}) collective-permute-start(f32[8,128]{1,0:T(8,128)S(1)} %add_add_fusion.2), channel_id=1, source_target_pairs={{0,3},{1,2},{2,1},{3,0},{4,7},{5,6},{6,5},{7,4},{8,11},{9,10},{10,... | collective-permute-start | bytes 12296 | tf_op jit(solution)/shard_map/ppermute | solution.py:23
  96.3 1.5 %collective-permute-start.27 = (f32[8,128]{1,0:T(8,128)S(1)}, f32[8,128]{1,0:T(8,128)S(1)}, u32[]{:S(2)}, u32[]{:S(2)}) collective-permute-start(f32[8,128]{1,0:T(8,128)S(1)} %add_add_fusion.2), channel_id=1, source_target_pairs={{0,1},{1,0},{2,3},{3,2},{4,5},{5,4},{6,7},{7,6},{8,9},{9,8},{10,11... | collective-permute-start | bytes 12296 | tf_op jit(solution)/shard_map/ppermute | solution.py:23
  97.8 1.0 collective-permute-done.28
  98.8 1.0 collective-permute-done.29
  99.9 1.1 collective-permute-start.31
  101.0 2.9 %collective-permute-start.32 = (f32[8,128]{1,0:T(8,128)S(1)}, f32[8,128]{1,0:T(8,128)S(1)}, u32[]{:S(2)}, u32[]{:S(2)}) collective-permute-start(f32[8,128]{1,0:T(8,128)S(1)} %add_add_fusion.1), channel_id=1, source_target_pairs={{0,12},{1,13},{2,14},{3,15},{4,8},{5,9},{6,10},{7,11},{8,4},{9,5},... | collective-permute-start | bytes 12296 | tf_op jit(solution)/shard_map/ppermute | solution.py:23
  103.8 0.8 collective-permute-start.30
  105.4 2.0 %collective-permute-done.30 = f32[8,128]{1,0:T(8,128)S(1)} collective-permute-done((f32[8,128]{1,0:T(8,128)S(1)}, f32[8,128]{1,0:T(8,128)S(1)}, u32[]{:S(2)}, u32[]{:S(2)}) %collective-permute-start.30) | collective-permute-done | bytes 4128 | tf_op jit(solution)/shard_map/ppermute | solution.py:23
  107.5 4.5 %block_products.4.second = bf16[12,128,128]{2,1,0:T(8,128)(2,1)S(1)} custom-call(s32[1216]{0:T(1024)S(1)} %get-tuple-element.29.left_ref, s32[1216]{0:T(1024)S(1)} %get-tuple-element.28.right_ref, s32[304]{0:T(512)S(1)} %convert_reduce_fusion.1.target_ref, s32[4]{0:T(128)S(1)} %select_reduce_fusion.1.bounds_ref, s32[32]{0:T(128)S(1)} %select_reduce_fusion.slot_ref, ...), custom_call_target="tpu_custom_call" | custom-call | flops 1610612736 | bytes 8388608 | tf_op jit(solution)/shard_map/block_products/pallas_call | solution.py:203
  112.0 3.1 %collective-permute-start.34 = (f32[8,128]{1,0:T(8,128)S(1)}, f32[8,128]{1,0:T(8,128)S(1)}, u32[]{:S(2)}, u32[]{:S(2)}) collective-permute-start(f32[8,128]{1,0:T(8,128)S(1)} %add.235), channel_id=1, source_target_pairs={{0,32},{16,48},{32,0},{48,16},{64,96},{80,112},{96,64},{112,80},{1... | collective-permute-start | bytes 12296 | tf_op jit(solution)/shard_map/ppermute | solution.py:23
  115.1 5.6 %block_products.5 = bf16[32,128,128]{2,1,0:T(8,128)(2,1)} custom-call(s32[1216]{0:T(1024)S(1)} %get-tuple-element.29.left_ref, s32[1216]{0:T(1024)S(1)} %get-tuple-element.28.right_ref, s32[304]{0:T(512)S(1)} %convert_reduce_fusion.1.target_ref, s32[4]{0:T(128)S(1)} %select_reduce_fusion.1.bounds_ref, s32[32]{0:T(128)S(1)} %select_reduce_fusion.slot_ref, ...), custom_call_target="tpu_custom_call" | custom-call | flops 1610612736 | bytes 8388608 | tf_op jit(solution)/shard_map/block_products/pallas_call | solution.py:203
  (97 shorter events, 7.1 us)
Async XLA Ops:
  0.6 9.8 %copy-start.5 = (s32[1,1,2,32]{3,2,1,0:T(2,128)S(1)}, s32[1,1,2,32]{3,2,1,0:T(2,128)}, u32[]{:S(2)}) copy-start(s32[1,1,2,32]{3,2,1,0:T(2,128)} %param.7) | copy-start | bytes 772
  0.7 9.8 %copy-start.2 = (s32[1,1,4,3,256]{4,2,3,1,0:T(4,128)S(1)}, s32[1,1,4,3,256]{4,2,3,1,0:T(4,128)}, u32[]{:S(2)}) copy-start(s32[1,1,4,3,256]{4,2,3,1,0:T(4,128)} %param.8) | copy-start | bytes 36868
  0.7 10.7 %copy-start.3 = (s32[4]{0:T(128)S(1)}, s32[4]{0:T(128)}, u32[]{:S(2)}) copy-start(s32[4]{0:T(128)} %param.9) | copy-start | bytes 52
  2.4 10.1 %collective-permute-start.2 = (bf16[2,2,2,128,128]{4,3,2,1,0:T(8,128)(2,1)S(1)}, bf16[2,2,2,128,128]{4,3,2,1,0:T(8,128)(2,1)}, u32[]{:S(2)}, u32[]{:S(2)}) collective-permute-start(bf16[2,2,2,128,128]{4,3,2,1,0:T(8,128)(2,1)S(1)} %get-tuple-element.45), channel_id=1, source_target_pairs={{0,4},{1,5},{2,6},{3,7},{4,0},{5,1},{6,2},{7,3},{8,12},{9,13},{10,... | collective-permute-start | bytes 786440 | tf_op jit(solution)/shard_map/ppermute | solution.py:23
  4.7 12.4 %collective-permute-start.1 = (bf16[2,2,2,128,128]{4,3,2,1,0:T(8,128)(2,1)S(1)}, bf16[2,2,2,128,128]{4,3,2,1,0:T(8,128)(2,1)S(1)}, u32[]{:S(2)}, u32[]{:S(2)}) collective-permute-start(bf16[2,2,2,128,128]{4,3,2,1,0:T(8,128)(2,1)S(1)} %get-tuple-element.46), channel_id=1, source_target_pairs={{0,8},{1,9},{2,10},{3,11},{4,12},{5,13},{6,14},{7,15},{8,0},{9,1},... | collective-permute-start | bytes 786440 | tf_op jit(solution)/shard_map/ppermute | solution.py:23
  5.4 13.1 %collective-permute-start = (bf16[2,2,2,128,128]{4,3,2,1,0:T(8,128)(2,1)S(1)}, bf16[2,2,2,128,128]{4,3,2,1,0:T(8,128)(2,1)S(1)}, u32[]{:S(2)}, u32[]{:S(2)}) collective-permute-start(bf16[2,2,2,128,128]{4,3,2,1,0:T(8,128)(2,1)S(1)} %get-tuple-element.47), channel_id=1, source_target_pairs={{0,12},{1,13},{2,14},{3,15},{4,8},{5,9},{6,10},{7,11},{8,4},{9,5},... | collective-permute-start | bytes 786440 | tf_op jit(solution)/shard_map/ppermute | solution.py:23
  6.3 17.3 %collective-permute-start.11 = (bf16[2,2,2,128,128]{4,3,2,1,0:T(8,128)(2,1)S(1)}, bf16[2,2,2,128,128]{4,3,2,1,0:T(8,128)(2,1)S(1)}, u32[]{:S(2)}, u32[]{:S(2)}) collective-permute-start(bf16[2,2,2,128,128]{4,3,2,1,0:T(8,128)(2,1)S(1)} %get-tuple-element.42), channel_id=1, source_target_pairs={{0,64},{16,80},{32,96},{48,112},{64,0},{80,16},{96,32},{112,48},{1... | collective-permute-start | bytes 786440 | tf_op jit(solution)/shard_map/ppermute | solution.py:23
  7.5 16.8 %collective-permute-start.10 = (bf16[2,2,2,128,128]{4,3,2,1,0:T(8,128)(2,1)S(1)}, bf16[2,2,2,128,128]{4,3,2,1,0:T(8,128)(2,1)S(1)}, u32[]{:S(2)}, u32[]{:S(2)}) collective-permute-start(bf16[2,2,2,128,128]{4,3,2,1,0:T(8,128)(2,1)S(1)} %get-tuple-element.43), channel_id=1, source_target_pairs={{0,128},{16,144},{32,160},{48,176},{64,192},{80,208},{96,224},{112... | collective-permute-start | bytes 786440 | tf_op jit(solution)/shard_map/ppermute | solution.py:23
  12.5 12.9 %collective-permute-start.9 = (bf16[2,2,2,128,128]{4,3,2,1,0:T(8,128)(2,1)S(1)}, bf16[2,2,2,128,128]{4,3,2,1,0:T(8,128)(2,1)S(1)}, u32[]{:S(2)}, u32[]{:S(2)}) collective-permute-start(bf16[2,2,2,128,128]{4,3,2,1,0:T(8,128)(2,1)S(1)} %get-tuple-element.40), channel_id=1, source_target_pairs={{0,192},{16,208},{32,224},{48,240},{64,128},{80,144},{96,160},{112... | collective-permute-start | bytes 786440 | tf_op jit(solution)/shard_map/ppermute | solution.py:23
  18.9 8.7 %collective-permute-start.3 = (bf16[4,128,128]{2,1,0:T(8,128)(2,1)S(1)}, bf16[4,128,128]{2,1,0:T(8,128)(2,1)S(1)}, u32[]{:S(2)}, u32[]{:S(2)}) collective-permute-start(bf16[4,128,128]{2,1,0:T(8,128)(2,1)S(1)} %get-tuple-element.50), channel_id=1, source_target_pairs={{0,3},{1,2},{2,1},{3,0},{4,7},{5,6},{6,5},{7,4},{8,11},{9,10},{10,... | collective-permute-start | bytes 393224 | tf_op jit(solution)/shard_map/ppermute | solution.py:23
  23.6 8.8 %collective-permute-start.4 = (bf16[4,128,128]{2,1,0:T(8,128)(2,1)S(1)}, bf16[4,128,128]{2,1,0:T(8,128)(2,1)S(1)}, u32[]{:S(2)}, u32[]{:S(2)}) collective-permute-start(bf16[4,128,128]{2,1,0:T(8,128)(2,1)S(1)} %get-tuple-element.49), channel_id=1, source_target_pairs={{0,2},{1,3},{2,0},{3,1},{4,6},{5,7},{6,4},{7,5},{8,10},{9,11},{10,... | collective-permute-start | bytes 393224 | tf_op jit(solution)/shard_map/ppermute | solution.py:23
  23.6 11.8 %copy-start.4 = (s32[4]{0:T(128)S(1)}, s32[4]{0:T(128)}, u32[]{:S(2)}) copy-start(s32[4]{0:T(128)} %constant.93.clone) | copy-start | bytes 52
  23.6 8.8 %collective-permute-start.5 = (bf16[4,128,128]{2,1,0:T(8,128)(2,1)S(1)}, bf16[4,128,128]{2,1,0:T(8,128)(2,1)S(1)}, u32[]{:S(2)}, u32[]{:S(2)}) collective-permute-start(bf16[4,128,128]{2,1,0:T(8,128)(2,1)S(1)} %get-tuple-element.48), channel_id=1, source_target_pairs={{0,1},{1,0},{2,3},{3,2},{4,5},{5,4},{6,7},{7,6},{8,9},{9,8},{10,11... | collective-permute-start | bytes 393224 | tf_op jit(solution)/shard_map/ppermute | solution.py:23
  25.8 17.7 %collective-permute-start.12 = (bf16[4,2,128,128]{3,2,1,0:T(8,128)(2,1)S(1)}, bf16[4,2,128,128]{3,2,1,0:T(8,128)(2,1)S(1)}, u32[]{:S(2)}, u32[]{:S(2)}) collective-permute-start(bf16[4,2,128,128]{3,2,1,0:T(8,128)(2,1)S(1)} %dynamic-slice_bitcast_fusion), channel_id=1, source_target_pairs={{0,16},{16,0},{32,48},{48,32},{64,80},{80,64},{96,112},{112,96},{1... | collective-permute-start | bytes 786440 | tf_op jit(solution)/shard_map/ppermute | solution.py:23
  32.6 8.3 %collective-permute-start.8 = (bf16[4,128,128]{2,1,0:T(8,128)(2,1)S(1)}, bf16[4,128,128]{2,1,0:T(8,128)(2,1)S(1)}, u32[]{:S(2)}, u32[]{:S(2)}) collective-permute-start(bf16[4,128,128]{2,1,0:T(8,128)(2,1)S(1)} %get-tuple-element.35), channel_id=1, source_target_pairs={{0,3},{1,2},{2,1},{3,0},{4,7},{5,6},{6,5},{7,4},{8,11},{9,10},{10,... | collective-permute-start | bytes 393224 | tf_op jit(solution)/shard_map/ppermute | solution.py:23
  35.6 10.1 %collective-permute-start.7 = (bf16[4,128,128]{2,1,0:T(8,128)(2,1)S(1)}, bf16[4,128,128]{2,1,0:T(8,128)(2,1)S(1)}, u32[]{:S(2)}, u32[]{:S(2)}) collective-permute-start(bf16[4,128,128]{2,1,0:T(8,128)(2,1)S(1)} %get-tuple-element.35), channel_id=1, source_target_pairs={{0,2},{1,3},{2,0},{3,1},{4,6},{5,7},{6,4},{7,5},{8,10},{9,11},{10,... | collective-permute-start | bytes 393224 | tf_op jit(solution)/shard_map/ppermute | solution.py:23
  35.7 10.0 %collective-permute-start.6 = (bf16[4,128,128]{2,1,0:T(8,128)(2,1)S(1)}, bf16[4,128,128]{2,1,0:T(8,128)(2,1)S(1)}, u32[]{:S(2)}, u32[]{:S(2)}) collective-permute-start(bf16[4,128,128]{2,1,0:T(8,128)(2,1)S(1)} %get-tuple-element.35), channel_id=1, source_target_pairs={{0,1},{1,0},{2,3},{3,2},{4,5},{5,4},{6,7},{7,6},{8,9},{9,8},{10,11... | collective-permute-start | bytes 393224 | tf_op jit(solution)/shard_map/ppermute | solution.py:23
  37.3 8.5 %collective-permute-start.13 = (bf16[4,128,128]{2,1,0:T(8,128)(2,1)S(1)}, bf16[4,128,128]{2,1,0:T(8,128)(2,1)S(1)}, u32[]{:S(2)}, u32[]{:S(2)}) collective-permute-start(bf16[4,128,128]{2,1,0:T(8,128)(2,1)S(1)} %get-tuple-element.35), channel_id=1, source_target_pairs={{0,4},{1,5},{2,6},{3,7},{4,0},{5,1},{6,2},{7,3},{8,12},{9,13},{10,... | collective-permute-start | bytes 393224 | tf_op jit(solution)/shard_map/ppermute | solution.py:23
  40.9 6.5 %collective-permute-start.14 = (bf16[4,128,128]{2,1,0:T(8,128)(2,1)S(1)}, bf16[4,128,128]{2,1,0:T(8,128)(2,1)S(1)}, u32[]{:S(2)}, u32[]{:S(2)}) collective-permute-start(bf16[4,128,128]{2,1,0:T(8,128)(2,1)S(1)} %get-tuple-element.35), channel_id=1, source_target_pairs={{0,8},{1,9},{2,10},{3,11},{4,12},{5,13},{6,14},{7,15},{8,0},{9,1},... | collective-permute-start | bytes 393224 | tf_op jit(solution)/shard_map/ppermute | solution.py:23
  43.5 5.3 %collective-permute-start.15 = (bf16[4,128,128]{2,1,0:T(8,128)(2,1)S(1)}, bf16[4,128,128]{2,1,0:T(8,128)(2,1)S(1)}, u32[]{:S(2)}, u32[]{:S(2)}) collective-permute-start(bf16[4,128,128]{2,1,0:T(8,128)(2,1)S(1)} %get-tuple-element.35), channel_id=1, source_target_pairs={{0,12},{1,13},{2,14},{3,15},{4,8},{5,9},{6,10},{7,11},{8,4},{9,5},... | collective-permute-start | bytes 393224 | tf_op jit(solution)/shard_map/ppermute | solution.py:23
  48.8 11.3 %collective-permute-start.16 = (bf16[4,2,128,128]{3,2,1,0:T(8,128)(2,1)S(1)}, bf16[4,2,128,128]{3,2,1,0:T(8,128)(2,1)S(1)}, u32[]{:S(2)}, u32[]{:S(2)}) collective-permute-start(bf16[4,2,128,128]{3,2,1,0:T(8,128)(2,1)S(1)} %bitcast_select_fusion), channel_id=1, source_target_pairs={{0,32},{16,48},{32,0},{48,16},{64,96},{80,112},{96,64},{112,80},{1... | collective-permute-start | bytes 786440 | tf_op jit(solution)/shard_map/ppermute | solution.py:23
  54.8 12.5 %collective-permute-start.17 = (bf16[12,128,128]{2,1,0:T(8,128)(2,1)S(1)}, bf16[12,128,128]{2,1,0:T(8,128)(2,1)S(1)}, u32[]{:S(2)}, u32[]{:S(2)}) collective-permute-start(bf16[12,128,128]{2,1,0:T(8,128)(2,1)S(1)} %pad_maximum_fusion.1), channel_id=1, source_target_pairs={{0,4},{1,5},{2,6},{3,7},{4,0},{5,1},{6,2},{7,3},{8,12},{9,13},{10,... | collective-permute-start | bytes 1179656 | tf_op jit(solution)/shard_map/ppermute | solution.py:23
  58.2 23.8 %collective-permute-start.18 = (bf16[12,128,128]{2,1,0:T(8,128)(2,1)S(1)}, bf16[12,128,128]{2,1,0:T(8,128)(2,1)S(1)}, u32[]{:S(2)}, u32[]{:S(2)}) collective-permute-start(bf16[12,128,128]{2,1,0:T(8,128)(2,1)S(1)} %pad_maximum_fusion.1), channel_id=1, source_target_pairs={{0,8},{1,9},{2,10},{3,11},{4,12},{5,13},{6,14},{7,15},{8,0},{9,1},... | collective-permute-start | bytes 1179656 | tf_op jit(solution)/shard_map/ppermute | solution.py:23
  58.6 23.5 %collective-permute-start.19 = (bf16[12,128,128]{2,1,0:T(8,128)(2,1)S(1)}, bf16[12,128,128]{2,1,0:T(8,128)(2,1)S(1)}, u32[]{:S(2)}, u32[]{:S(2)}) collective-permute-start(bf16[12,128,128]{2,1,0:T(8,128)(2,1)S(1)} %pad_maximum_fusion.1), channel_id=1, source_target_pairs={{0,12},{1,13},{2,14},{3,15},{4,8},{5,9},{6,10},{7,11},{8,4},{9,5},... | collective-permute-start | bytes 1179656 | tf_op jit(solution)/shard_map/ppermute | solution.py:23
  67.2 6.4 %collective-permute-start.20 = (bf16[8,128,128]{2,1,0:T(8,128)(2,1)S(1)}, bf16[8,128,128]{2,1,0:T(8,128)(2,1)S(1)}, u32[]{:S(2)}, u32[]{:S(2)}) collective-permute-start(bf16[8,128,128]{2,1,0:T(8,128)(2,1)S(1)} %bitcast.93), channel_id=1, source_target_pairs={{0,64},{16,80},{32,96},{48,112},{64,0},{80,16},{96,32},{112,48},{1... | collective-permute-start | bytes 786440 | tf_op jit(solution)/shard_map/ppermute | solution.py:23
  68.8 10.2 %collective-permute-start.21 = (bf16[8,128,128]{2,1,0:T(8,128)(2,1)S(1)}, bf16[8,128,128]{2,1,0:T(8,128)(2,1)S(1)}, u32[]{:S(2)}, u32[]{:S(2)}) collective-permute-start(bf16[8,128,128]{2,1,0:T(8,128)(2,1)S(1)} %bitcast.94), channel_id=1, source_target_pairs={{0,128},{16,144},{32,160},{48,176},{64,192},{80,208},{96,224},{112... | collective-permute-start | bytes 786440 | tf_op jit(solution)/shard_map/ppermute | solution.py:23
  71.7 10.0 %collective-permute-start.22 = (bf16[8,128,128]{2,1,0:T(8,128)(2,1)S(1)}, bf16[8,128,128]{2,1,0:T(8,128)(2,1)S(1)}, u32[]{:S(2)}, u32[]{:S(2)}) collective-permute-start(bf16[8,128,128]{2,1,0:T(8,128)(2,1)S(1)} %bitcast.95), channel_id=1, source_target_pairs={{0,192},{16,208},{32,224},{48,240},{64,128},{80,144},{96,160},{112... | collective-permute-start | bytes 786440 | tf_op jit(solution)/shard_map/ppermute | solution.py:23
  81.8 2.7 %collective-permute-start.23 = (bf16[32,128,128]{2,1,0:T(8,128)(2,1)S(1)}, bf16[32,128,128]{2,1,0:T(8,128)(2,1)S(1)}, u32[]{:S(2)}, u32[]{:S(2)}) collective-permute-start(bf16[32,128,128]{2,1,0:T(8,128)(2,1)S(1)} %pad_maximum_fusion), channel_id=1, source_target_pairs={{0,16},{16,0},{32,48},{48,32},{64,80},{80,64},{96,112},{112,96},{1... | collective-permute-start | bytes 3145736 | tf_op jit(solution)/shard_map/ppermute | solution.py:23
  82.1 2.6 %copy-start = (bf16[1,1,32,128,128]{4,3,2,1,0:T(8,128)(2,1)S(1)}, bf16[1,1,32,128,128]{4,3,2,1,0:T(8,128)(2,1)}, u32[]{:S(2)}) copy-start(bf16[1,1,32,128,128]{4,3,2,1,0:T(8,128)(2,1)} %param.6) | copy-start | bytes 3145732
  82.1 2.6 %copy-start.1 = (s32[1,1,32]{2,1,0:T(1,128)S(1)}, s32[1,1,32]{2,1,0:T(1,128)}, u32[]{:S(2)}) copy-start(s32[1,1,32]{2,1,0:T(1,128)} %param.10) | copy-start | bytes 388
  88.6 5.2 %collective-permute-start.25 = (f32[8,128]{1,0:T(8,128)S(1)}, f32[8,128]{1,0:T(8,128)S(1)}, u32[]{:S(2)}, u32[]{:S(2)}) collective-permute-start(f32[8,128]{1,0:T(8,128)S(1)} %get-tuple-element.22), channel_id=1, source_target_pairs={{0,128},{16,144},{32,160},{48,176},{64,192},{80,208},{96,224},{112... | collective-permute-start | bytes 12296 | tf_op jit(solution)/shard_map/ppermute | solution.py:23
  88.7 5.1 %collective-permute-start.26 = (f32[8,128]{1,0:T(8,128)S(1)}, f32[8,128]{1,0:T(8,128)S(1)}, u32[]{:S(2)}, u32[]{:S(2)}) collective-permute-start(f32[8,128]{1,0:T(8,128)S(1)} %get-tuple-element.22), channel_id=1, source_target_pairs={{0,192},{16,208},{32,224},{48,240},{64,128},{80,144},{96,160},{112... | collective-permute-start | bytes 12296 | tf_op jit(solution)/shard_map/ppermute | solution.py:23
  90.7 3.6 %collective-permute-start.24 = (f32[8,128]{1,0:T(8,128)S(1)}, f32[8,128]{1,0:T(8,128)S(1)}, u32[]{:S(2)}, u32[]{:S(2)}) collective-permute-start(f32[8,128]{1,0:T(8,128)S(1)} %get-tuple-element.22), channel_id=1, source_target_pairs={{0,64},{16,80},{32,96},{48,112},{64,0},{80,16},{96,32},{112,48},{1... | collective-permute-start | bytes 12296 | tf_op jit(solution)/shard_map/ppermute | solution.py:23
  94.3 4.5 %collective-permute-start.28 = (f32[8,128]{1,0:T(8,128)S(1)}, f32[8,128]{1,0:T(8,128)S(1)}, u32[]{:S(2)}, u32[]{:S(2)}) collective-permute-start(f32[8,128]{1,0:T(8,128)S(1)} %add_add_fusion.2), channel_id=1, source_target_pairs={{0,2},{1,3},{2,0},{3,1},{4,6},{5,7},{6,4},{7,5},{8,10},{9,11},{10,... | collective-permute-start | bytes 12296 | tf_op jit(solution)/shard_map/ppermute | solution.py:23
  94.3 5.5 %collective-permute-start.29 = (f32[8,128]{1,0:T(8,128)S(1)}, f32[8,128]{1,0:T(8,128)S(1)}, u32[]{:S(2)}, u32[]{:S(2)}) collective-permute-start(f32[8,128]{1,0:T(8,128)S(1)} %add_add_fusion.2), channel_id=1, source_target_pairs={{0,3},{1,2},{2,1},{3,0},{4,7},{5,6},{6,5},{7,4},{8,11},{9,10},{10,... | collective-permute-start | bytes 12296 | tf_op jit(solution)/shard_map/ppermute | solution.py:23
  96.3 3.6 %collective-permute-start.27 = (f32[8,128]{1,0:T(8,128)S(1)}, f32[8,128]{1,0:T(8,128)S(1)}, u32[]{:S(2)}, u32[]{:S(2)}) collective-permute-start(f32[8,128]{1,0:T(8,128)S(1)} %add_add_fusion.2), channel_id=1, source_target_pairs={{0,1},{1,0},{2,3},{3,2},{4,5},{5,4},{6,7},{7,6},{8,9},{9,8},{10,11... | collective-permute-start | bytes 12296 | tf_op jit(solution)/shard_map/ppermute | solution.py:23
  99.9 5.2 %collective-permute-start.31 = (f32[8,128]{1,0:T(8,128)S(1)}, f32[8,128]{1,0:T(8,128)S(1)}, u32[]{:S(2)}, u32[]{:S(2)}) collective-permute-start(f32[8,128]{1,0:T(8,128)S(1)} %add_add_fusion.1), channel_id=1, source_target_pairs={{0,8},{1,9},{2,10},{3,11},{4,12},{5,13},{6,14},{7,15},{8,0},{9,1},... | collective-permute-start | bytes 12296 | tf_op jit(solution)/shard_map/ppermute | solution.py:23
  101.0 4.4 %collective-permute-start.32 = (f32[8,128]{1,0:T(8,128)S(1)}, f32[8,128]{1,0:T(8,128)S(1)}, u32[]{:S(2)}, u32[]{:S(2)}) collective-permute-start(f32[8,128]{1,0:T(8,128)S(1)} %add_add_fusion.1), channel_id=1, source_target_pairs={{0,12},{1,13},{2,14},{3,15},{4,8},{5,9},{6,10},{7,11},{8,4},{9,5},... | collective-permute-start | bytes 12296 | tf_op jit(solution)/shard_map/ppermute | solution.py:23
  103.8 3.6 %collective-permute-start.30 = (f32[8,128]{1,0:T(8,128)S(1)}, f32[8,128]{1,0:T(8,128)S(1)}, u32[]{:S(2)}, u32[]{:S(2)}) collective-permute-start(f32[8,128]{1,0:T(8,128)S(1)} %add_add_fusion.1), channel_id=1, source_target_pairs={{0,4},{1,5},{2,6},{3,7},{4,0},{5,1},{6,2},{7,3},{8,12},{9,13},{10,... | collective-permute-start | bytes 12296 | tf_op jit(solution)/shard_map/ppermute | solution.py:23
  107.5 4.5 %collective-permute-start.33 = (f32[8,128]{1,0:T(8,128)S(1)}, f32[8,128]{1,0:T(8,128)S(1)}, u32[]{:S(2)}, u32[]{:S(2)}) collective-permute-start(f32[8,128]{1,0:T(8,128)S(1)} %add_add_fusion), channel_id=1, source_target_pairs={{0,16},{16,0},{32,48},{48,32},{64,80},{80,64},{96,112},{112,96},{1... | collective-permute-start | bytes 12296 | tf_op jit(solution)/shard_map/ppermute | solution.py:23
  112.0 8.7 %collective-permute-start.34 = (f32[8,128]{1,0:T(8,128)S(1)}, f32[8,128]{1,0:T(8,128)S(1)}, u32[]{:S(2)}, u32[]{:S(2)}) collective-permute-start(f32[8,128]{1,0:T(8,128)S(1)} %add.235), channel_id=1, source_target_pairs={{0,32},{16,48},{32,0},{48,16},{64,96},{80,112},{96,64},{112,80},{1... | collective-permute-start | bytes 12296 | tf_op jit(solution)/shard_map/ppermute | solution.py:23

commit v5 on v4

--- a/solution.py
+++ b/solution.py
@@ -70,9 +70,10 @@
 
     half = choose([half, swap(half, "row", 2)], ((panels >> 2) & 1) ^ zh).reshape(WIN * 2, BS, BS)
     half, behind[0] = lax.optimization_barrier((half, behind[0]))
-    line = jnp.concatenate([half] + [swap(half, "row", 4 * d) for d in (1, 2, 3)])
+    by_y = [half] + [swap(half, "row", 4 * d) for d in (1, 2, 3)]
+    pairs = [jnp.concatenate(by_y[:2]), jnp.concatenate(by_y[2:])]
     columns = [held, near] + [part for pair in zip(ahead, behind) for part in pair]
-    return columns, [line, swap(line, "row", 1)]
+    return columns, pairs + [swap(pair, "row", 1) for pair in pairs]
 
 
 def plan(tasks, coords):

time: 123 us -> 122 us (level); the launches traced: 121 us -> 122 us
  waiting for transfers between devices: 40 us -> 38.5 us
  Pallas kernels: 14 us -> 15.4 us
    ppermute x35 -> x36, waiting for transfers between devices: 40 us -> 38.5 us  [swap(): return lax.ppermute(value, axis, [(i, i ^ bit) for i in range(16)])]
    pallas_call x3, Pallas kernels: 14 us -> 15.4 us  [products(): pl.pallas_call(kernel, out_shape=out_shape, in_specs=[smem] * len(scalars...]
    ppermute x35 -> x36, starting transfers between devices: 58.7 us -> 59.3 us  [swap(): return lax.ppermute(value, axis, [(i, i ^ bit) for i in range(16)])]
  transfers between devices with their start and end apart: 35 -> 36, of which waited for: 21 -> 22; matrix products, arithmetic and copies ran while one was open for 4% -> 4% of each run, Pallas kernels for 8% -> 9%
where the time goes in v5:
time: 122 us
  starting transfers between devices  59.3 us (49%)
  waiting for transfers between devices  38.5 us (32%)
  Pallas kernels  15.4 us (13%)
  local copies, waits for them, and re-layouts  3.48 us (3%)
  other arithmetic  2.51 us (2%)
  matrix products  1.44 us (1%)
  between operations  1.26 us (1%)
    ppermute x36, starting transfers between devices, swap(): return lax.ppermute(value, axis, [(i, i ^ bit) for i in range(16)])  59.3 us
    ppermute x36, waiting for transfers between devices, swap(): return lax.ppermute(value, axis, [(i, i ^ bit) for i in range(16)])  38.5 us
    pallas_call x3, Pallas kernels, products(): pl.pallas_call(kernel, out_shape=out_shape, in_specs=[smem] * len(scalars...  15.4 us
  transfers between devices with their start and end apart: 36, of which 22 were waited for; matrix products, arithmetic and copies ran while one was open for 4% of the time, Pallas kernels for 9%

profile of v5, /device:TPU:2, one launch (start us, length us, event | category | flops | bytes accessed | tf_op | source)
XLA Modules:
  0.0 121.9 jit_solution(6796211096237238901)
XLA Ops:
  0.7 1.7 %dynamic-slice_bitcast_fusion.4 = (bf16[2,2,2,128,128]{4,3,2,1,0:T(8,128)(2,1)S(1)}, bf16[1,2,2,2,128,128]{5,4,3,2,1,0:T(8,128)(2,1)S(1)}, bf16[2,2,2,128,128]{4...) fusion(bf16[2,2,4,2,128,128]{5,4,3,2,1,0:T(8,128)(2,1)} %bitcas, ...), kind=kLoop, calls=%fused_computation.20 | loop fusion | bytes 4194336 | tf_op jit(solution)/shard_map/jit(dynamic_index_in_dim)/squeeze | solution.py:27
  2.4 2.4 %collective-permute-start.2 = (bf16[2,2,2,128,128]{4,3,2,1,0:T(8,128)(2,1)S(1)}, bf16[2,2,2,128,128]{4,3,2,1,0:T(8,128)(2,1)}, u32[]{:S(2)}, u32[]{:S(2)}) collective-permute-start(bf16[2,2,2,128,128]{4,3,2,1,0:T(8,128)(2,1)S(1)} %get-tuple-element.45), channel_id=1, source_target_pairs={{0,4},{1,5},{2,6},{3,7},{4,0},{5,1},{6,2},{7,3},{8,12},{9,13},{10,... | collective-permute-start | bytes 786440 | tf_op jit(solution)/shard_map/ppermute | solution.py:23
  4.8 0.7 collective-permute-start.1
  5.4 0.9 collective-permute-start
  6.3 1.2 %collective-permute-start.11 = (bf16[2,2,2,128,128]{4,3,2,1,0:T(8,128)(2,1)S(1)}, bf16[2,2,2,128,128]{4,3,2,1,0:T(8,128)(2,1)S(1)}, u32[]{:S(2)}, u32[]{:S(2)}) collective-permute-start(bf16[2,2,2,128,128]{4,3,2,1,0:T(8,128)(2,1)S(1)} %get-tuple-element.42), channel_id=1, source_target_pairs={{0,64},{16,80},{32,96},{48,112},{64,0},{80,16},{96,32},{112,48},{1... | collective-permute-start | bytes 786440 | tf_op jit(solution)/shard_map/ppermute | solution.py:23
  7.6 2.9 %collective-permute-start.10 = (bf16[2,2,2,128,128]{4,3,2,1,0:T(8,128)(2,1)S(1)}, bf16[2,2,2,128,128]{4,3,2,1,0:T(8,128)(2,1)S(1)}, u32[]{:S(2)}, u32[]{:S(2)}) collective-permute-start(bf16[2,2,2,128,128]{4,3,2,1,0:T(8,128)(2,1)S(1)} %get-tuple-element.43), channel_id=1, source_target_pairs={{0,128},{16,144},{32,160},{48,176},{64,192},{80,208},{96,224},{112... | collective-permute-start | bytes 786440 | tf_op jit(solution)/shard_map/ppermute | solution.py:23
  11.6 0.9 fusion.3
  12.7 2.1 %collective-permute-start.9 = (bf16[2,2,2,128,128]{4,3,2,1,0:T(8,128)(2,1)S(1)}, bf16[2,2,2,128,128]{4,3,2,1,0:T(8,128)(2,1)S(1)}, u32[]{:S(2)}, u32[]{:S(2)}) collective-permute-start(bf16[2,2,2,128,128]{4,3,2,1,0:T(8,128)(2,1)S(1)} %get-tuple-element.40), channel_id=1, source_target_pairs={{0,192},{16,208},{32,224},{48,240},{64,128},{80,144},{96,160},{112... | collective-permute-start | bytes 786440 | tf_op jit(solution)/shard_map/ppermute | solution.py:23
  14.8 1.0 fusion.22
  15.8 1.4 %collective-permute-done.1 = bf16[2,2,2,128,128]{4,3,2,1,0:T(8,128)(2,1)S(1)} collective-permute-done((bf16[2,2,2,128,128]{4,3,2,1,0:T(8,128)(2,1)S(1)}, bf16[2,2,2,128,128]{4,3,2,1,0:T(8,128)(2,1)S(1)}, u32[]{:S(2)}, u32[]{:S(2)}) %collective-permute-start.1) | collective-permute-done | bytes 262176 | tf_op jit(solution)/shard_map/ppermute | solution.py:23
  17.2 1.3 %collective-permute-done = bf16[2,2,2,128,128]{4,3,2,1,0:T(8,128)(2,1)S(1)} collective-permute-done((bf16[2,2,2,128,128]{4,3,2,1,0:T(8,128)(2,1)S(1)}, bf16[2,2,2,128,128]{4,3,2,1,0:T(8,128)(2,1)S(1)}, u32[]{:S(2)}, u32[]{:S(2)}) %collective-permute-start) | collective-permute-done | bytes 262176 | tf_op jit(solution)/shard_map/ppermute | solution.py:23
  18.9 4.7 %collective-permute-start.3 = (bf16[4,128,128]{2,1,0:T(8,128)(2,1)S(1)}, bf16[4,128,128]{2,1,0:T(8,128)(2,1)S(1)}, u32[]{:S(2)}, u32[]{:S(2)}) collective-permute-start(bf16[4,128,128]{2,1,0:T(8,128)(2,1)S(1)} %get-tuple-element.50), channel_id=1, source_target_pairs={{0,3},{1,2},{2,1},{3,0},{4,7},{5,6},{6,5},{7,4},{8,11},{9,10},{10,... | collective-permute-start | bytes 393224 | tf_op jit(solution)/shard_map/ppermute | solution.py:23
  23.6 0.7 collective-permute-start.5
  24.3 1.2 %collective-permute-done.9 = bf16[2,2,2,128,128]{4,3,2,1,0:T(8,128)(2,1)S(1)} collective-permute-done((bf16[2,2,2,128,128]{4,3,2,1,0:T(8,128)(2,1)S(1)}, bf16[2,2,2,128,128]{4,3,2,1,0:T(8,128)(2,1)S(1)}, u32[]{:S(2)}, u32[]{:S(2)}) %collective-permute-start.9) | collective-permute-done | bytes 262176 | tf_op jit(solution)/shard_map/ppermute | solution.py:23
  26.0 1.6 %collective-permute-done.3 = bf16[4,128,128]{2,1,0:T(8,128)(2,1)S(1)} collective-permute-done((bf16[4,128,128]{2,1,0:T(8,128)(2,1)S(1)}, bf16[4,128,128]{2,1,0:T(8,128)(2,1)S(1)}, u32[]{:S(2)}, u32[]{:S(2)}) %collective-permute-start.3) | collective-permute-done | bytes 131104 | tf_op jit(solution)/shard_map/ppermute | solution.py:23
  27.6 4.8 %collective-permute-done.4 = bf16[4,128,128]{2,1,0:T(8,128)(2,1)S(1)} collective-permute-done((bf16[4,128,128]{2,1,0:T(8,128)(2,1)S(1)}, bf16[4,128,128]{2,1,0:T(8,128)(2,1)S(1)}, u32[]{:S(2)}, u32[]{:S(2)}) %collective-permute-start.4) | collective-permute-done | bytes 131104 | tf_op jit(solution)/shard_map/ppermute | solution.py:23
  32.6 2.8 %collective-permute-start.8 = (bf16[4,128,128]{2,1,0:T(8,128)(2,1)S(1)}, bf16[4,128,128]{2,1,0:T(8,128)(2,1)S(1)}, u32[]{:S(2)}, u32[]{:S(2)}) collective-permute-start(bf16[4,128,128]{2,1,0:T(8,128)(2,1)S(1)} %get-tuple-element.35), channel_id=1, source_target_pairs={{0,3},{1,2},{2,1},{3,0},{4,7},{5,6},{6,5},{7,4},{8,11},{9,10},{10,... | collective-permute-start | bytes 393224 | tf_op jit(solution)/shard_map/ppermute | solution.py:23
  35.7 1.6 %collective-permute-start.6 = (bf16[4,128,128]{2,1,0:T(8,128)(2,1)S(1)}, bf16[4,128,128]{2,1,0:T(8,128)(2,1)S(1)}, u32[]{:S(2)}, u32[]{:S(2)}) collective-permute-start(bf16[4,128,128]{2,1,0:T(8,128)(2,1)S(1)} %get-tuple-element.35), channel_id=1, source_target_pairs={{0,1},{1,0},{2,3},{3,2},{4,5},{5,4},{6,7},{7,6},{8,9},{9,8},{10,11... | collective-permute-start | bytes 393224 | tf_op jit(solution)/shard_map/ppermute | solution.py:23
  37.3 3.3 %collective-permute-start.13 = (bf16[4,128,128]{2,1,0:T(8,128)(2,1)S(1)}, bf16[4,128,128]{2,1,0:T(8,128)(2,1)S(1)}, u32[]{:S(2)}, u32[]{:S(2)}) collective-permute-start(bf16[4,128,128]{2,1,0:T(8,128)(2,1)S(1)} %get-tuple-element.35), channel_id=1, source_target_pairs={{0,4},{1,5},{2,6},{3,7},{4,0},{5,1},{6,2},{7,3},{8,12},{9,13},{10,... | collective-permute-start | bytes 393224 | tf_op jit(solution)/shard_map/ppermute | solution.py:23
  40.9 2.6 %collective-permute-start.14 = (bf16[4,128,128]{2,1,0:T(8,128)(2,1)S(1)}, bf16[4,128,128]{2,1,0:T(8,128)(2,1)S(1)}, u32[]{:S(2)}, u32[]{:S(2)}) collective-permute-start(bf16[4,128,128]{2,1,0:T(8,128)(2,1)S(1)} %get-tuple-element.35), channel_id=1, source_target_pairs={{0,8},{1,9},{2,10},{3,11},{4,12},{5,13},{6,14},{7,15},{8,0},{9,1},... | collective-permute-start | bytes 393224 | tf_op jit(solution)/shard_map/ppermute | solution.py:23
  43.5 2.2 %collective-permute-start.15 = (bf16[4,128,128]{2,1,0:T(8,128)(2,1)S(1)}, bf16[4,128,128]{2,1,0:T(8,128)(2,1)S(1)}, u32[]{:S(2)}, u32[]{:S(2)}) collective-permute-start(bf16[4,128,128]{2,1,0:T(8,128)(2,1)S(1)} %get-tuple-element.35), channel_id=1, source_target_pairs={{0,12},{1,13},{2,14},{3,15},{4,8},{5,9},{6,10},{7,11},{8,4},{9,5},... | collective-permute-start | bytes 393224 | tf_op jit(solution)/shard_map/ppermute | solution.py:23
  45.8 1.6 %collective-permute-done.14 = bf16[4,128,128]{2,1,0:T(8,128)(2,1)S(1)} collective-permute-done((bf16[4,128,128]{2,1,0:T(8,128)(2,1)S(1)}, bf16[4,128,128]{2,1,0:T(8,128)(2,1)S(1)}, u32[]{:S(2)}, u32[]{:S(2)}) %collective-permute-start.14) | collective-permute-done | bytes 131104 | tf_op jit(solution)/shard_map/ppermute | solution.py:23
  47.4 1.4 %collective-permute-done.15 = bf16[4,128,128]{2,1,0:T(8,128)(2,1)S(1)} collective-permute-done((bf16[4,128,128]{2,1,0:T(8,128)(2,1)S(1)}, bf16[4,128,128]{2,1,0:T(8,128)(2,1)S(1)}, u32[]{:S(2)}, u32[]{:S(2)}) %collective-permute-start.15) | collective-permute-done | bytes 131104 | tf_op jit(solution)/shard_map/ppermute | solution.py:23
  48.8 5.9 %collective-permute-start.16 = (bf16[4,2,128,128]{3,2,1,0:T(8,128)(2,1)S(1)}, bf16[4,2,128,128]{3,2,1,0:T(8,128)(2,1)S(1)}, u32[]{:S(2)}, u32[]{:S(2)}) collective-permute-start(bf16[4,2,128,128]{3,2,1,0:T(8,128)(2,1)S(1)} %bitcast_select_fusion), channel_id=1, source_target_pairs={{0,32},{16,48},{32,0},{48,16},{64,96},{80,112},{96,64},{112,80},{1... | collective-permute-start | bytes 786440 | tf_op jit(solution)/shard_map/ppermute | solution.py:23
  54.8 3.3 %collective-permute-start.17 = (bf16[12,128,128]{2,1,0:T(8,128)(2,1)S(1)}, bf16[12,128,128]{2,1,0:T(8,128)(2,1)S(1)}, u32[]{:S(2)}, u32[]{:S(2)}) collective-permute-start(bf16[12,128,128]{2,1,0:T(8,128)(2,1)S(1)} %pad_maximum_fusion.2), channel_id=1, source_target_pairs={{0,4},{1,5},{2,6},{3,7},{4,0},{5,1},{6,2},{7,3},{8,12},{9,13},{10,... | collective-permute-start | bytes 1179656 | tf_op jit(solution)/shard_map/ppermute | solution.py:23
  58.4 1.3 %collective-permute-start.19 = (bf16[12,128,128]{2,1,0:T(8,128)(2,1)S(1)}, bf16[12,128,128]{2,1,0:T(8,128)(2,1)S(1)}, u32[]{:S(2)}, u32[]{:S(2)}) collective-permute-start(bf16[12,128,128]{2,1,0:T(8,128)(2,1)S(1)} %pad_maximum_fusion.2), channel_id=1, source_target_pairs={{0,12},{1,13},{2,14},{3,15},{4,8},{5,9},{6,10},{7,11},{8,4},{9,5},... | collective-permute-start | bytes 1179656 | tf_op jit(solution)/shard_map/ppermute | solution.py:23
  60.2 7.1 %collective-permute-done.17 = bf16[12,128,128]{2,1,0:T(8,128)(2,1)S(1)} collective-permute-done((bf16[12,128,128]{2,1,0:T(8,128)(2,1)S(1)}, bf16[12,128,128]{2,1,0:T(8,128)(2,1)S(1)}, u32[]{:S(2)}, u32[]{:S(2)}) %collective-permute-start.17) | collective-permute-done | bytes 393248 | tf_op jit(solution)/shard_map/ppermute | solution.py:23
  67.3 1.6 %collective-permute-start.20 = (bf16[8,128,128]{2,1,0:T(8,128)(2,1)S(1)}, bf16[8,128,128]{2,1,0:T(8,128)(2,1)S(1)}, u32[]{:S(2)}, u32[]{:S(2)}) collective-permute-start(bf16[8,128,128]{2,1,0:T(8,128)(2,1)S(1)} %bitcast.93), channel_id=1, source_target_pairs={{0,64},{16,80},{32,96},{48,112},{64,0},{80,16},{96,32},{112,48},{1... | collective-permute-start | bytes 786440 | tf_op jit(solution)/shard_map/ppermute | solution.py:23
  68.8 2.9 %collective-permute-start.21 = (bf16[8,128,128]{2,1,0:T(8,128)(2,1)S(1)}, bf16[8,128,128]{2,1,0:T(8,128)(2,1)S(1)}, u32[]{:S(2)}, u32[]{:S(2)}) collective-permute-start(bf16[8,128,128]{2,1,0:T(8,128)(2,1)S(1)} %bitcast.94), channel_id=1, source_target_pairs={{0,128},{16,144},{32,160},{48,176},{64,192},{80,208},{96,224},{112... | collective-permute-start | bytes 786440 | tf_op jit(solution)/shard_map/ppermute | solution.py:23
  72.2 0.8 collective-permute-done.19
  73.8 5.2 %collective-permute-done.21 = bf16[8,128,128]{2,1,0:T(8,128)(2,1)S(1)} collective-permute-done((bf16[8,128,128]{2,1,0:T(8,128)(2,1)S(1)}, bf16[8,128,128]{2,1,0:T(8,128)(2,1)S(1)}, u32[]{:S(2)}, u32[]{:S(2)}) %collective-permute-start.21) | collective-permute-done | bytes 262176 | tf_op jit(solution)/shard_map/ppermute | solution.py:23
  79.0 2.7 %collective-permute-done.22 = bf16[8,128,128]{2,1,0:T(8,128)(2,1)S(1)} collective-permute-done((bf16[8,128,128]{2,1,0:T(8,128)(2,1)S(1)}, bf16[8,128,128]{2,1,0:T(8,128)(2,1)S(1)}, u32[]{:S(2)}, u32[]{:S(2)}) %collective-permute-start.22) | collective-permute-done | bytes 262176 | tf_op jit(solution)/shard_map/ppermute | solution.py:23
  82.1 1.7 %collective-permute-done.24 = bf16[16,128,128]{2,1,0:T(8,128)(2,1)S(1)} collective-permute-done((bf16[16,128,128]{2,1,0:T(8,128)(2,1)S(1)}, bf16[16,128,128]{2,1,0:T(8,128)(2,1)S(1)}, u32[]{:S(2)}, u32[]{:S(2)}) %collective-permute-start.24) | collective-permute-done | bytes 524320 | tf_op jit(solution)/shard_map/ppermute | solution.py:23
  83.9 3.8 %block_products.3 = (bf16[8,128,128]{2,1,0:T(8,128)(2,1)S(1)}, f32[8,128]{1,0:T(8,128)S(1)}) custom-call(s32[1216]{0:T(1024)S(1)} %get-tuple-element.29.left_ref, s32[1216]{0:T(1024)S(1)} %get-tuple-element.28.right_ref, s32[304]{0:T(512)S(1)} %convert_reduce_fusion.1.target_ref, s32[4]{0:T(128)S(1)} %select_reduce_fusion.1.bounds_ref, ...), custom_call_target="tpu_custom_call" | custom-call | flops 1073741824 | bytes 8388608 | tf_op jit(solution)/shard_map/block_products/pallas_call | solution.py:204
  87.8 1.4 %collective-permute-start.27 = (f32[8,128]{1,0:T(8,128)S(1)}, f32[8,128]{1,0:T(8,128)S(1)}, u32[]{:S(2)}, u32[]{:S(2)}) collective-permute-start(f32[8,128]{1,0:T(8,128)S(1)} %get-tuple-element.22), channel_id=1, source_target_pairs={{0,192},{16,208},{32,224},{48,240},{64,128},{80,144},{96,160},{112... | collective-permute-start | bytes 12296 | tf_op jit(solution)/shard_map/ppermute | solution.py:23
  89.1 2.1 %collective-permute-start.25 = (f32[8,128]{1,0:T(8,128)S(1)}, f32[8,128]{1,0:T(8,128)S(1)}, u32[]{:S(2)}, u32[]{:S(2)}) collective-permute-start(f32[8,128]{1,0:T(8,128)S(1)} %get-tuple-element.22), channel_id=1, source_target_pairs={{0,64},{16,80},{32,96},{48,112},{64,0},{80,16},{96,32},{112,48},{1... | collective-permute-start | bytes 12296 | tf_op jit(solution)/shard_map/ppermute | solution.py:23
  91.3 1.6 %collective-permute-done.26 = f32[8,128]{1,0:T(8,128)S(1)} collective-permute-done((f32[8,128]{1,0:T(8,128)S(1)}, f32[8,128]{1,0:T(8,128)S(1)}, u32[]{:S(2)}, u32[]{:S(2)}) %collective-permute-start.26) | collective-permute-done | bytes 4128 | tf_op jit(solution)/shard_map/ppermute | solution.py:23
  93.0 2.0 %collective-permute-start.30 = (f32[8,128]{1,0:T(8,128)S(1)}, f32[8,128]{1,0:T(8,128)S(1)}, u32[]{:S(2)}, u32[]{:S(2)}) collective-permute-start(f32[8,128]{1,0:T(8,128)S(1)} %add_add_fusion.2), channel_id=1, source_target_pairs={{0,3},{1,2},{2,1},{3,0},{4,7},{5,6},{6,5},{7,4},{8,11},{9,10},{10,... | collective-permute-start | bytes 12296 | tf_op jit(solution)/shard_map/ppermute | solution.py:23
  95.0 1.5 %collective-permute-start.28 = (f32[8,128]{1,0:T(8,128)S(1)}, f32[8,128]{1,0:T(8,128)S(1)}, u32[]{:S(2)}, u32[]{:S(2)}) collective-permute-start(f32[8,128]{1,0:T(8,128)S(1)} %add_add_fusion.2), channel_id=1, source_target_pairs={{0,1},{1,0},{2,3},{3,2},{4,5},{5,4},{6,7},{7,6},{8,9},{9,8},{10,11... | collective-permute-start | bytes 12296 | tf_op jit(solution)/shard_map/ppermute | solution.py:23
  96.5 1.0 collective-permute-done.29
  97.5 1.0 collective-permute-done.30
  98.6 1.3 %collective-permute-start.32 = (f32[8,128]{1,0:T(8,128)S(1)}, f32[8,128]{1,0:T(8,128)S(1)}, u32[]{:S(2)}, u32[]{:S(2)}) collective-permute-start(f32[8,128]{1,0:T(8,128)S(1)} %add_add_fusion.1), channel_id=1, source_target_pairs={{0,8},{1,9},{2,10},{3,11},{4,12},{5,13},{6,14},{7,15},{8,0},{9,1},... | collective-permute-start | bytes 12296 | tf_op jit(solution)/shard_map/ppermute | solution.py:23
  99.9 2.4 %collective-permute-start.33 = (f32[8,128]{1,0:T(8,128)S(1)}, f32[8,128]{1,0:T(8,128)S(1)}, u32[]{:S(2)}, u32[]{:S(2)}) collective-permute-start(f32[8,128]{1,0:T(8,128)S(1)} %add_add_fusion.1), channel_id=1, source_target_pairs={{0,12},{1,13},{2,14},{3,15},{4,8},{5,9},{6,10},{7,11},{8,4},{9,5},... | collective-permute-start | bytes 12296 | tf_op jit(solution)/shard_map/ppermute | solution.py:23
  102.3 1.0 collective-permute-start.31
  103.9 2.0 %collective-permute-done.31 = f32[8,128]{1,0:T(8,128)S(1)} collective-permute-done((f32[8,128]{1,0:T(8,128)S(1)}, f32[8,128]{1,0:T(8,128)S(1)}, u32[]{:S(2)}, u32[]{:S(2)}) %collective-permute-start.31) | collective-permute-done | bytes 4128 | tf_op jit(solution)/shard_map/ppermute | solution.py:23
  105.9 5.2 %block_products.4.second = bf16[12,128,128]{2,1,0:T(8,128)(2,1)S(1)} custom-call(s32[1216]{0:T(1024)S(1)} %get-tuple-element.29.left_ref, s32[1216]{0:T(1024)S(1)} %get-tuple-element.28.right_ref, s32[304]{0:T(512)S(1)} %convert_reduce_fusion.1.target_ref, s32[4]{0:T(128)S(1)} %select_reduce_fusion.1.bounds_ref, s32[32]{0:T(128)S(1)} %select_reduce_fusion.slot_ref, ...), custom_call_target="tpu_custom_call" | custom-call | flops 1610612736 | bytes 8388608 | tf_op jit(solution)/shard_map/block_products/pallas_call | solution.py:204
  111.1 3.8 %collective-permute-start.35 = (f32[8,128]{1,0:T(8,128)S(1)}, f32[8,128]{1,0:T(8,128)S(1)}, u32[]{:S(2)}, u32[]{:S(2)}) collective-permute-start(f32[8,128]{1,0:T(8,128)S(1)} %add.235), channel_id=1, source_target_pairs={{0,32},{16,48},{32,0},{48,16},{64,96},{80,112},{96,64},{112,80},{1... | collective-permute-start | bytes 12296 | tf_op jit(solution)/shard_map/ppermute | solution.py:23
  114.9 6.3 %block_products.5 = bf16[32,128,128]{2,1,0:T(8,128)(2,1)} custom-call(s32[1216]{0:T(1024)S(1)} %get-tuple-element.29.left_ref, s32[1216]{0:T(1024)S(1)} %get-tuple-element.28.right_ref, s32[304]{0:T(512)S(1)} %convert_reduce_fusion.1.target_ref, s32[4]{0:T(128)S(1)} %select_reduce_fusion.1.bounds_ref, s32[32]{0:T(128)S(1)} %select_reduce_fusion.slot_ref, ...), custom_call_target="tpu_custom_call" | custom-call | flops 1610612736 | bytes 8388608 | tf_op jit(solution)/shard_map/block_products/pallas_call | solution.py:204
  (101 shorter events, 7.1 us)
Async XLA Ops:
  0.6 9.8 %copy-start.5 = (s32[1,1,2,32]{3,2,1,0:T(2,128)S(1)}, s32[1,1,2,32]{3,2,1,0:T(2,128)}, u32[]{:S(2)}) copy-start(s32[1,1,2,32]{3,2,1,0:T(2,128)} %param.7) | copy-start | bytes 772
  0.7 9.8 %copy-start.2 = (s32[1,1,4,3,256]{4,2,3,1,0:T(4,128)S(1)}, s32[1,1,4,3,256]{4,2,3,1,0:T(4,128)}, u32[]{:S(2)}) copy-start(s32[1,1,4,3,256]{4,2,3,1,0:T(4,128)} %param.8) | copy-start | bytes 36868
  0.7 10.8 %copy-start.3 = (s32[4]{0:T(128)S(1)}, s32[4]{0:T(128)}, u32[]{:S(2)}) copy-start(s32[4]{0:T(128)} %param.9) | copy-start | bytes 52
  2.4 10.1 %copy-start.4 = (s32[4]{0:T(128)S(1)}, s32[4]{0:T(128)}, u32[]{:S(2)}) copy-start(s32[4]{0:T(128)} %constant.93.clone) | copy-start | bytes 52
  2.4 10.3 %collective-permute-start.2 = (bf16[2,2,2,128,128]{4,3,2,1,0:T(8,128)(2,1)S(1)}, bf16[2,2,2,128,128]{4,3,2,1,0:T(8,128)(2,1)}, u32[]{:S(2)}, u32[]{:S(2)}) collective-permute-start(bf16[2,2,2,128,128]{4,3,2,1,0:T(8,128)(2,1)S(1)} %get-tuple-element.45), channel_id=1, source_target_pairs={{0,4},{1,5},{2,6},{3,7},{4,0},{5,1},{6,2},{7,3},{8,12},{9,13},{10,... | collective-permute-start | bytes 786440 | tf_op jit(solution)/shard_map/ppermute | solution.py:23
  4.8 12.4 %collective-permute-start.1 = (bf16[2,2,2,128,128]{4,3,2,1,0:T(8,128)(2,1)S(1)}, bf16[2,2,2,128,128]{4,3,2,1,0:T(8,128)(2,1)S(1)}, u32[]{:S(2)}, u32[]{:S(2)}) collective-permute-start(bf16[2,2,2,128,128]{4,3,2,1,0:T(8,128)(2,1)S(1)} %get-tuple-element.46), channel_id=1, source_target_pairs={{0,8},{1,9},{2,10},{3,11},{4,12},{5,13},{6,14},{7,15},{8,0},{9,1},... | collective-permute-start | bytes 786440 | tf_op jit(solution)/shard_map/ppermute | solution.py:23
  5.4 13.1 %collective-permute-start = (bf16[2,2,2,128,128]{4,3,2,1,0:T(8,128)(2,1)S(1)}, bf16[2,2,2,128,128]{4,3,2,1,0:T(8,128)(2,1)S(1)}, u32[]{:S(2)}, u32[]{:S(2)}) collective-permute-start(bf16[2,2,2,128,128]{4,3,2,1,0:T(8,128)(2,1)S(1)} %get-tuple-element.47), channel_id=1, source_target_pairs={{0,12},{1,13},{2,14},{3,15},{4,8},{5,9},{6,10},{7,11},{8,4},{9,5},... | collective-permute-start | bytes 786440 | tf_op jit(solution)/shard_map/ppermute | solution.py:23
  6.3 17.3 %collective-permute-start.11 = (bf16[2,2,2,128,128]{4,3,2,1,0:T(8,128)(2,1)S(1)}, bf16[2,2,2,128,128]{4,3,2,1,0:T(8,128)(2,1)S(1)}, u32[]{:S(2)}, u32[]{:S(2)}) collective-permute-start(bf16[2,2,2,128,128]{4,3,2,1,0:T(8,128)(2,1)S(1)} %get-tuple-element.42), channel_id=1, source_target_pairs={{0,64},{16,80},{32,96},{48,112},{64,0},{80,16},{96,32},{112,48},{1... | collective-permute-start | bytes 786440 | tf_op jit(solution)/shard_map/ppermute | solution.py:23
  7.6 16.7 %collective-permute-start.10 = (bf16[2,2,2,128,128]{4,3,2,1,0:T(8,128)(2,1)S(1)}, bf16[2,2,2,128,128]{4,3,2,1,0:T(8,128)(2,1)S(1)}, u32[]{:S(2)}, u32[]{:S(2)}) collective-permute-start(bf16[2,2,2,128,128]{4,3,2,1,0:T(8,128)(2,1)S(1)} %get-tuple-element.43), channel_id=1, source_target_pairs={{0,128},{16,144},{32,160},{48,176},{64,192},{80,208},{96,224},{112... | collective-permute-start | bytes 786440 | tf_op jit(solution)/shard_map/ppermute | solution.py:23
  12.7 12.8 %collective-permute-start.9 = (bf16[2,2,2,128,128]{4,3,2,1,0:T(8,128)(2,1)S(1)}, bf16[2,2,2,128,128]{4,3,2,1,0:T(8,128)(2,1)S(1)}, u32[]{:S(2)}, u32[]{:S(2)}) collective-permute-start(bf16[2,2,2,128,128]{4,3,2,1,0:T(8,128)(2,1)S(1)} %get-tuple-element.40), channel_id=1, source_target_pairs={{0,192},{16,208},{32,224},{48,240},{64,128},{80,144},{96,160},{112... | collective-permute-start | bytes 786440 | tf_op jit(solution)/shard_map/ppermute | solution.py:23
  18.9 8.7 %collective-permute-start.3 = (bf16[4,128,128]{2,1,0:T(8,128)(2,1)S(1)}, bf16[4,128,128]{2,1,0:T(8,128)(2,1)S(1)}, u32[]{:S(2)}, u32[]{:S(2)}) collective-permute-start(bf16[4,128,128]{2,1,0:T(8,128)(2,1)S(1)} %get-tuple-element.50), channel_id=1, source_target_pairs={{0,3},{1,2},{2,1},{3,0},{4,7},{5,6},{6,5},{7,4},{8,11},{9,10},{10,... | collective-permute-start | bytes 393224 | tf_op jit(solution)/shard_map/ppermute | solution.py:23
  23.6 8.8 %collective-permute-start.4 = (bf16[4,128,128]{2,1,0:T(8,128)(2,1)S(1)}, bf16[4,128,128]{2,1,0:T(8,128)(2,1)S(1)}, u32[]{:S(2)}, u32[]{:S(2)}) collective-permute-start(bf16[4,128,128]{2,1,0:T(8,128)(2,1)S(1)} %get-tuple-element.49), channel_id=1, source_target_pairs={{0,2},{1,3},{2,0},{3,1},{4,6},{5,7},{6,4},{7,5},{8,10},{9,11},{10,... | collective-permute-start | bytes 393224 | tf_op jit(solution)/shard_map/ppermute | solution.py:23
  23.6 8.8 %collective-permute-start.5 = (bf16[4,128,128]{2,1,0:T(8,128)(2,1)S(1)}, bf16[4,128,128]{2,1,0:T(8,128)(2,1)S(1)}, u32[]{:S(2)}, u32[]{:S(2)}) collective-permute-start(bf16[4,128,128]{2,1,0:T(8,128)(2,1)S(1)} %get-tuple-element.48), channel_id=1, source_target_pairs={{0,1},{1,0},{2,3},{3,2},{4,5},{5,4},{6,7},{7,6},{8,9},{9,8},{10,11... | collective-permute-start | bytes 393224 | tf_op jit(solution)/shard_map/ppermute | solution.py:23
  25.9 17.6 %collective-permute-start.12 = (bf16[4,2,128,128]{3,2,1,0:T(8,128)(2,1)S(1)}, bf16[4,2,128,128]{3,2,1,0:T(8,128)(2,1)S(1)}, u32[]{:S(2)}, u32[]{:S(2)}) collective-permute-start(bf16[4,2,128,128]{3,2,1,0:T(8,128)(2,1)S(1)} %dynamic-slice_bitcast_fusion), channel_id=1, source_target_pairs={{0,16},{16,0},{32,48},{48,32},{64,80},{80,64},{96,112},{112,96},{1... | collective-permute-start | bytes 786440 | tf_op jit(solution)/shard_map/ppermute | solution.py:23
  32.6 8.3 %collective-permute-start.8 = (bf16[4,128,128]{2,1,0:T(8,128)(2,1)S(1)}, bf16[4,128,128]{2,1,0:T(8,128)(2,1)S(1)}, u32[]{:S(2)}, u32[]{:S(2)}) collective-permute-start(bf16[4,128,128]{2,1,0:T(8,128)(2,1)S(1)} %get-tuple-element.35), channel_id=1, source_target_pairs={{0,3},{1,2},{2,1},{3,0},{4,7},{5,6},{6,5},{7,4},{8,11},{9,10},{10,... | collective-permute-start | bytes 393224 | tf_op jit(solution)/shard_map/ppermute | solution.py:23
  35.6 10.2 %collective-permute-start.7 = (bf16[4,128,128]{2,1,0:T(8,128)(2,1)S(1)}, bf16[4,128,128]{2,1,0:T(8,128)(2,1)S(1)}, u32[]{:S(2)}, u32[]{:S(2)}) collective-permute-start(bf16[4,128,128]{2,1,0:T(8,128)(2,1)S(1)} %get-tuple-element.35), channel_id=1, source_target_pairs={{0,2},{1,3},{2,0},{3,1},{4,6},{5,7},{6,4},{7,5},{8,10},{9,11},{10,... | collective-permute-start | bytes 393224 | tf_op jit(solution)/shard_map/ppermute | solution.py:23
  35.7 10.1 %collective-permute-start.6 = (bf16[4,128,128]{2,1,0:T(8,128)(2,1)S(1)}, bf16[4,128,128]{2,1,0:T(8,128)(2,1)S(1)}, u32[]{:S(2)}, u32[]{:S(2)}) collective-permute-start(bf16[4,128,128]{2,1,0:T(8,128)(2,1)S(1)} %get-tuple-element.35), channel_id=1, source_target_pairs={{0,1},{1,0},{2,3},{3,2},{4,5},{5,4},{6,7},{7,6},{8,9},{9,8},{10,11... | collective-permute-start | bytes 393224 | tf_op jit(solution)/shard_map/ppermute | solution.py:23
  37.3 8.5 %collective-permute-start.13 = (bf16[4,128,128]{2,1,0:T(8,128)(2,1)S(1)}, bf16[4,128,128]{2,1,0:T(8,128)(2,1)S(1)}, u32[]{:S(2)}, u32[]{:S(2)}) collective-permute-start(bf16[4,128,128]{2,1,0:T(8,128)(2,1)S(1)} %get-tuple-element.35), channel_id=1, source_target_pairs={{0,4},{1,5},{2,6},{3,7},{4,0},{5,1},{6,2},{7,3},{8,12},{9,13},{10,... | collective-permute-start | bytes 393224 | tf_op jit(solution)/shard_map/ppermute | solution.py:23
  40.9 6.5 %collective-permute-start.14 = (bf16[4,128,128]{2,1,0:T(8,128)(2,1)S(1)}, bf16[4,128,128]{2,1,0:T(8,128)(2,1)S(1)}, u32[]{:S(2)}, u32[]{:S(2)}) collective-permute-start(bf16[4,128,128]{2,1,0:T(8,128)(2,1)S(1)} %get-tuple-element.35), channel_id=1, source_target_pairs={{0,8},{1,9},{2,10},{3,11},{4,12},{5,13},{6,14},{7,15},{8,0},{9,1},... | collective-permute-start | bytes 393224 | tf_op jit(solution)/shard_map/ppermute | solution.py:23
  43.5 5.3 %collective-permute-start.15 = (bf16[4,128,128]{2,1,0:T(8,128)(2,1)S(1)}, bf16[4,128,128]{2,1,0:T(8,128)(2,1)S(1)}, u32[]{:S(2)}, u32[]{:S(2)}) collective-permute-start(bf16[4,128,128]{2,1,0:T(8,128)(2,1)S(1)} %get-tuple-element.35), channel_id=1, source_target_pairs={{0,12},{1,13},{2,14},{3,15},{4,8},{5,9},{6,10},{7,11},{8,4},{9,5},... | collective-permute-start | bytes 393224 | tf_op jit(solution)/shard_map/ppermute | solution.py:23
  48.8 11.3 %collective-permute-start.16 = (bf16[4,2,128,128]{3,2,1,0:T(8,128)(2,1)S(1)}, bf16[4,2,128,128]{3,2,1,0:T(8,128)(2,1)S(1)}, u32[]{:S(2)}, u32[]{:S(2)}) collective-permute-start(bf16[4,2,128,128]{3,2,1,0:T(8,128)(2,1)S(1)} %bitcast_select_fusion), channel_id=1, source_target_pairs={{0,32},{16,48},{32,0},{48,16},{64,96},{80,112},{96,64},{112,80},{1... | collective-permute-start | bytes 786440 | tf_op jit(solution)/shard_map/ppermute | solution.py:23
  54.8 12.5 %collective-permute-start.17 = (bf16[12,128,128]{2,1,0:T(8,128)(2,1)S(1)}, bf16[12,128,128]{2,1,0:T(8,128)(2,1)S(1)}, u32[]{:S(2)}, u32[]{:S(2)}) collective-permute-start(bf16[12,128,128]{2,1,0:T(8,128)(2,1)S(1)} %pad_maximum_fusion.2), channel_id=1, source_target_pairs={{0,4},{1,5},{2,6},{3,7},{4,0},{5,1},{6,2},{7,3},{8,12},{9,13},{10,... | collective-permute-start | bytes 1179656 | tf_op jit(solution)/shard_map/ppermute | solution.py:23
  58.1 14.0 %collective-permute-start.18 = (bf16[12,128,128]{2,1,0:T(8,128)(2,1)S(1)}, bf16[12,128,128]{2,1,0:T(8,128)(2,1)S(1)}, u32[]{:S(2)}, u32[]{:S(2)}) collective-permute-start(bf16[12,128,128]{2,1,0:T(8,128)(2,1)S(1)} %pad_maximum_fusion.2), channel_id=1, source_target_pairs={{0,8},{1,9},{2,10},{3,11},{4,12},{5,13},{6,14},{7,15},{8,0},{9,1},... | collective-permute-start | bytes 1179656 | tf_op jit(solution)/shard_map/ppermute | solution.py:23
  58.4 14.6 %collective-permute-start.19 = (bf16[12,128,128]{2,1,0:T(8,128)(2,1)S(1)}, bf16[12,128,128]{2,1,0:T(8,128)(2,1)S(1)}, u32[]{:S(2)}, u32[]{:S(2)}) collective-permute-start(bf16[12,128,128]{2,1,0:T(8,128)(2,1)S(1)} %pad_maximum_fusion.2), channel_id=1, source_target_pairs={{0,12},{1,13},{2,14},{3,15},{4,8},{5,9},{6,10},{7,11},{8,4},{9,5},... | collective-permute-start | bytes 1179656 | tf_op jit(solution)/shard_map/ppermute | solution.py:23
  67.3 6.4 %collective-permute-start.20 = (bf16[8,128,128]{2,1,0:T(8,128)(2,1)S(1)}, bf16[8,128,128]{2,1,0:T(8,128)(2,1)S(1)}, u32[]{:S(2)}, u32[]{:S(2)}) collective-permute-start(bf16[8,128,128]{2,1,0:T(8,128)(2,1)S(1)} %bitcast.93), channel_id=1, source_target_pairs={{0,64},{16,80},{32,96},{48,112},{64,0},{80,16},{96,32},{112,48},{1... | collective-permute-start | bytes 786440 | tf_op jit(solution)/shard_map/ppermute | solution.py:23
  68.8 10.2 %collective-permute-start.21 = (bf16[8,128,128]{2,1,0:T(8,128)(2,1)S(1)}, bf16[8,128,128]{2,1,0:T(8,128)(2,1)S(1)}, u32[]{:S(2)}, u32[]{:S(2)}) collective-permute-start(bf16[8,128,128]{2,1,0:T(8,128)(2,1)S(1)} %bitcast.94), channel_id=1, source_target_pairs={{0,128},{16,144},{32,160},{48,176},{64,192},{80,208},{96,224},{112... | collective-permute-start | bytes 786440 | tf_op jit(solution)/shard_map/ppermute | solution.py:23
  71.7 10.0 %collective-permute-start.22 = (bf16[8,128,128]{2,1,0:T(8,128)(2,1)S(1)}, bf16[8,128,128]{2,1,0:T(8,128)(2,1)S(1)}, u32[]{:S(2)}, u32[]{:S(2)}) collective-permute-start(bf16[8,128,128]{2,1,0:T(8,128)(2,1)S(1)} %bitcast.95), channel_id=1, source_target_pairs={{0,192},{16,208},{32,224},{48,240},{64,128},{80,144},{96,160},{112... | collective-permute-start | bytes 786440 | tf_op jit(solution)/shard_map/ppermute | solution.py:23
  73.7 10.1 %copy-start = (bf16[1,1,32,128,128]{4,3,2,1,0:T(8,128)(2,1)S(1)}, bf16[1,1,32,128,128]{4,3,2,1,0:T(8,128)(2,1)}, u32[]{:S(2)}) copy-start(bf16[1,1,32,128,128]{4,3,2,1,0:T(8,128)(2,1)} %param.6) | copy-start | bytes 3145732
  73.7 10.1 %copy-start.1 = (s32[1,1,32]{2,1,0:T(1,128)S(1)}, s32[1,1,32]{2,1,0:T(1,128)}, u32[]{:S(2)}) copy-start(s32[1,1,32]{2,1,0:T(1,128)} %param.10) | copy-start | bytes 388
  73.7 8.3 %collective-permute-start.23 = (bf16[16,128,128]{2,1,0:T(8,128)(2,1)S(1)}, bf16[16,128,128]{2,1,0:T(8,128)(2,1)S(1)}, u32[]{:S(2)}, u32[]{:S(2)}) collective-permute-start(bf16[16,128,128]{2,1,0:T(8,128)(2,1)S(1)} %pad_maximum_fusion), channel_id=1, source_target_pairs={{0,16},{16,0},{32,48},{48,32},{64,80},{80,64},{96,112},{112,96},{1... | collective-permute-start | bytes 1572872 | tf_op jit(solution)/shard_map/ppermute | solution.py:23
  81.8 2.0 %collective-permute-start.24 = (bf16[16,128,128]{2,1,0:T(8,128)(2,1)S(1)}, bf16[16,128,128]{2,1,0:T(8,128)(2,1)S(1)}, u32[]{:S(2)}, u32[]{:S(2)}) collective-permute-start(bf16[16,128,128]{2,1,0:T(8,128)(2,1)S(1)} %pad_maximum_fusion.1), channel_id=1, source_target_pairs={{0,16},{16,0},{32,48},{48,32},{64,80},{80,64},{96,112},{112,96},{1... | collective-permute-start | bytes 1572872 | tf_op jit(solution)/shard_map/ppermute | solution.py:23
  87.7 5.2 %collective-permute-start.26 = (f32[8,128]{1,0:T(8,128)S(1)}, f32[8,128]{1,0:T(8,128)S(1)}, u32[]{:S(2)}, u32[]{:S(2)}) collective-permute-start(f32[8,128]{1,0:T(8,128)S(1)} %get-tuple-element.22), channel_id=1, source_target_pairs={{0,128},{16,144},{32,160},{48,176},{64,192},{80,208},{96,224},{112... | collective-permute-start | bytes 12296 | tf_op jit(solution)/shard_map/ppermute | solution.py:23
  87.8 5.1 %collective-permute-start.27 = (f32[8,128]{1,0:T(8,128)S(1)}, f32[8,128]{1,0:T(8,128)S(1)}, u32[]{:S(2)}, u32[]{:S(2)}) collective-permute-start(f32[8,128]{1,0:T(8,128)S(1)} %get-tuple-element.22), channel_id=1, source_target_pairs={{0,192},{16,208},{32,224},{48,240},{64,128},{80,144},{96,160},{112... | collective-permute-start | bytes 12296 | tf_op jit(solution)/shard_map/ppermute | solution.py:23
  89.1 3.7 %collective-permute-start.25 = (f32[8,128]{1,0:T(8,128)S(1)}, f32[8,128]{1,0:T(8,128)S(1)}, u32[]{:S(2)}, u32[]{:S(2)}) collective-permute-start(f32[8,128]{1,0:T(8,128)S(1)} %get-tuple-element.22), channel_id=1, source_target_pairs={{0,64},{16,80},{32,96},{48,112},{64,0},{80,16},{96,32},{112,48},{1... | collective-permute-start | bytes 12296 | tf_op jit(solution)/shard_map/ppermute | solution.py:23
  92.9 4.6 %collective-permute-start.29 = (f32[8,128]{1,0:T(8,128)S(1)}, f32[8,128]{1,0:T(8,128)S(1)}, u32[]{:S(2)}, u32[]{:S(2)}) collective-permute-start(f32[8,128]{1,0:T(8,128)S(1)} %add_add_fusion.2), channel_id=1, source_target_pairs={{0,2},{1,3},{2,0},{3,1},{4,6},{5,7},{6,4},{7,5},{8,10},{9,11},{10,... | collective-permute-start | bytes 12296 | tf_op jit(solution)/shard_map/ppermute | solution.py:23
  93.0 5.5 %collective-permute-start.30 = (f32[8,128]{1,0:T(8,128)S(1)}, f32[8,128]{1,0:T(8,128)S(1)}, u32[]{:S(2)}, u32[]{:S(2)}) collective-permute-start(f32[8,128]{1,0:T(8,128)S(1)} %add_add_fusion.2), channel_id=1, source_target_pairs={{0,3},{1,2},{2,1},{3,0},{4,7},{5,6},{6,5},{7,4},{8,11},{9,10},{10,... | collective-permute-start | bytes 12296 | tf_op jit(solution)/shard_map/ppermute | solution.py:23
  95.0 3.6 %collective-permute-start.28 = (f32[8,128]{1,0:T(8,128)S(1)}, f32[8,128]{1,0:T(8,128)S(1)}, u32[]{:S(2)}, u32[]{:S(2)}) collective-permute-start(f32[8,128]{1,0:T(8,128)S(1)} %add_add_fusion.2), channel_id=1, source_target_pairs={{0,1},{1,0},{2,3},{3,2},{4,5},{5,4},{6,7},{7,6},{8,9},{9,8},{10,11... | collective-permute-start | bytes 12296 | tf_op jit(solution)/shard_map/ppermute | solution.py:23
  98.6 5.1 %collective-permute-start.32 = (f32[8,128]{1,0:T(8,128)S(1)}, f32[8,128]{1,0:T(8,128)S(1)}, u32[]{:S(2)}, u32[]{:S(2)}) collective-permute-start(f32[8,128]{1,0:T(8,128)S(1)} %add_add_fusion.1), channel_id=1, source_target_pairs={{0,8},{1,9},{2,10},{3,11},{4,12},{5,13},{6,14},{7,15},{8,0},{9,1},... | collective-permute-start | bytes 12296 | tf_op jit(solution)/shard_map/ppermute | solution.py:23
  99.9 4.0 %collective-permute-start.33 = (f32[8,128]{1,0:T(8,128)S(1)}, f32[8,128]{1,0:T(8,128)S(1)}, u32[]{:S(2)}, u32[]{:S(2)}) collective-permute-start(f32[8,128]{1,0:T(8,128)S(1)} %add_add_fusion.1), channel_id=1, source_target_pairs={{0,12},{1,13},{2,14},{3,15},{4,8},{5,9},{6,10},{7,11},{8,4},{9,5},... | collective-permute-start | bytes 12296 | tf_op jit(solution)/shard_map/ppermute | solution.py:23
  102.3 3.6 %collective-permute-start.31 = (f32[8,128]{1,0:T(8,128)S(1)}, f32[8,128]{1,0:T(8,128)S(1)}, u32[]{:S(2)}, u32[]{:S(2)}) collective-permute-start(f32[8,128]{1,0:T(8,128)S(1)} %add_add_fusion.1), channel_id=1, source_target_pairs={{0,4},{1,5},{2,6},{3,7},{4,0},{5,1},{6,2},{7,3},{8,12},{9,13},{10,... | collective-permute-start | bytes 12296 | tf_op jit(solution)/shard_map/ppermute | solution.py:23
  105.9 5.2 %collective-permute-start.34 = (f32[8,128]{1,0:T(8,128)S(1)}, f32[8,128]{1,0:T(8,128)S(1)}, u32[]{:S(2)}, u32[]{:S(2)}) collective-permute-start(f32[8,128]{1,0:T(8,128)S(1)} %add_add_fusion), channel_id=1, source_target_pairs={{0,16},{16,0},{32,48},{48,32},{64,80},{80,64},{96,112},{112,96},{1... | collective-permute-start | bytes 12296 | tf_op jit(solution)/shard_map/ppermute | solution.py:23
  111.1 10.1 %collective-permute-start.35 = (f32[8,128]{1,0:T(8,128)S(1)}, f32[8,128]{1,0:T(8,128)S(1)}, u32[]{:S(2)}, u32[]{:S(2)}) collective-permute-start(f32[8,128]{1,0:T(8,128)S(1)} %add.235), channel_id=1, source_target_pairs={{0,32},{16,48},{32,0},{48,16},{64,96},{80,112},{96,64},{112,80},{1... | collective-permute-start | bytes 12296 | tf_op jit(solution)/shard_map/ppermute | solution.py:23
